TPU v7x, 32 devices: a whole 2x2x4 slice. The times are simulated.
32 devices in a mesh: dp: 8 (over y, x, core), fsdp: 4 (over z).
Axes of the slice: x: 2, y: 2, z: 4, core: 2. Of those that a mesh axis runs over, the one named last changes fastest.
Arguments:
- tokens: float32 [32768, 1024], P(('dp', 'fsdp')), may hold values from -6 to 6
- w_query: float32 [1024, 1024], P(('dp', 'fsdp')), may hold values from -0.1875 to 0.1875
- w_key: float32 [1024, 1024], P(('dp', 'fsdp')), may hold values from -0.1875 to 0.1875
- w_value: float32 [1024, 1024], P(('dp', 'fsdp')), may hold values from -0.1875 to 0.1875
- w_output: float32 [1024, 1024], P(('dp', 'fsdp')), may hold values from -1.5 to 1.5
- gain_one: float32 [1024], P(('dp', 'fsdp')), may hold values from 0.1 to 1.9
- shift_one: float32 [1024], P(('dp', 'fsdp')), may hold values from -1.5 to 1.5
- gain_two: float32 [1024], P(('dp', 'fsdp')), may hold values from 0.1 to 1.9
- shift_two: float32 [1024], P(('dp', 'fsdp')), may hold values from -1.5 to 1.5
- expert_in: float32 [1024, 2, 4096], P(('dp', 'fsdp')), may hold values from -0.1875 to 0.1875
- expert_out: float32 [4096, 2, 1024], P(('dp', 'fsdp')), may hold values from -0.09375 to 0.09375
- lengths: int32 [32, 8], P(('dp', 'fsdp')), may hold values from 1 to 768, 1024 in all within a row
- expert_ids: int32 [32768, 1], P(('dp', 'fsdp')), may hold values from 0 to 1; in each aligned block of 1024 rows (0 to 1023, 1024 to 2047, ...) at most 640 rows name the same one
- padding: int32 [32768], P(('dp', 'fsdp')), may hold values 0 or 1
- cotangent: float32 [32768, 1024], P(('dp', 'fsdp')), may hold values from -6 to 6
Outputs:
- output: float32 [32768, 1024], P(('dp', 'fsdp'))
- grad_tokens: float32 [32768, 1024], P(('dp', 'fsdp'))
- grad_query: float32 [1024, 1024], P(('dp', 'fsdp'))
- grad_key: float32 [1024, 1024], P(('dp', 'fsdp'))
- grad_value: float32 [1024, 1024], P(('dp', 'fsdp'))
- grad_output: float32 [1024, 1024], P(('dp', 'fsdp'))
- grad_gain_one: float32 [1024], P(('dp', 'fsdp'))
- grad_shift_one: float32 [1024], P(('dp', 'fsdp'))
- grad_gain_two: float32 [1024], P(('dp', 'fsdp'))
- grad_shift_two: float32 [1024], P(('dp', 'fsdp'))
- grad_expert_in: float32 [1024, 2, 4096], P(('dp', 'fsdp'))
- grad_expert_out: float32 [4096, 2, 1024], P(('dp', 'fsdp'))
Inputs may be any that keep to these rules, and one draw needn't show every extreme that they name: `expert_ids`: in each device's rows every expert is named at most 640 times, a bound that some block reaches. Each device's 8 lengths sum to 1024, and the longest is exactly 768.
All inputs are finite; a program needn't handle non-finite values. No bound on the sum of `padding` on one device may be relied on, other than what follows from the above.
Results may differ from a plain program's by a relative error of at most 0.01.
The roundings to bfloat16 on the way count: a program that leaves them out, or rounds other values in their place, can miss the bound.
Values may be sent and summed in bfloat16 or wider, within the bound.
No kernel may reach another device: no remote copies, remote signals or barrier semaphores. Data moves between devices by JAX's collectives and lax.ppermute only.
A program may use at most 512 MiB of HBM per device.

v0:
```python
import math

import jax
import jax.numpy as jnp
from jax import lax
from jax.sharding import PartitionSpec as P

HEADS = 16
HEAD_DIM = 64
CAP = 640


norm_eps = 1e-05
neg_large = -1e30


def normalize(values, gain, shift):
    center = values - jnp.mean(values, axis=1, keepdims=True)
    inverse = lax.rsqrt(jnp.mean(center * center, axis=1, keepdims=True) + norm_eps)
    scaled = center * inverse
    return (scaled * gain + shift, scaled, inverse)


def normalize_back(grad_rows, scaled, inverse, gain):
    inner = grad_rows * gain
    back_rows = inverse * (
        inner
        - jnp.mean(inner, axis=1, keepdims=True)
        - scaled * jnp.mean(inner * scaled, axis=1, keepdims=True)
    )
    return (back_rows, jnp.sum(grad_rows * scaled, axis=0), jnp.sum(grad_rows, axis=0))


def expert_slots(chosen, experts, capacity):
    row_count = chosen.shape[0]
    row_order = jnp.arange(row_count, dtype=jnp.int32)
    tables = []
    for expert in range(experts):
        member = chosen == expert
        slot_place = jnp.cumsum(member.astype(jnp.int32)) - 1
        target = jnp.where(member, slot_place, capacity)
        tables.append(
            jnp.full((capacity,), row_count, jnp.int32).at[target].set(row_order, mode="drop")
        )
    return jnp.stack(tables)


def with_zero_row(values):
    return jnp.concatenate([values, jnp.zeros((1, values.shape[1]), values.dtype)], axis=0)


def visible_block(segment, spots, padding, block_start, block_size):
    query_seg = segment[block_start : block_start + block_size]
    query_spot = spots[block_start : block_start + block_size]
    same_seq = query_seg[:, None] == segment[None, :]
    causal = spots[None, :] <= query_spot[:, None]
    usable = (padding[None, :] == 1) | (spots[None, :] == query_spot[:, None])
    return same_seq & causal & usable


def masked_scores(query_block, key_heads, visible, score_scale):
    scores = (
        jnp.einsum("qhd,khd->hqk", query_block, key_heads, preferred_element_type=jnp.float32)
        * score_scale
    )
    return jnp.where(visible[None], scores, neg_large)


def local(
    tokens,
    w_query,
    w_key,
    w_value,
    w_output,
    gain_one,
    shift_one,
    gain_two,
    shift_two,
    expert_in,
    expert_out,
    lengths,
    expert_ids,
    padding,
    cotangent,
):
    row_count = tokens.shape[0]
    width_all = tokens.shape[1]
    experts = expert_in.shape[1]
    score_scale = 1.0 / math.sqrt(HEAD_DIM)
    block_size = min(512, row_count)
    attention_set = (
        lax.all_gather(w_query.astype(jnp.bfloat16), ("dp", "fsdp"), axis=0, tiled=True),
        lax.all_gather(w_key.astype(jnp.bfloat16), ("dp", "fsdp"), axis=0, tiled=True),
        lax.all_gather(w_value.astype(jnp.bfloat16), ("dp", "fsdp"), axis=0, tiled=True),
        lax.all_gather(w_output.astype(jnp.bfloat16), ("dp", "fsdp"), axis=0, tiled=True),
        lax.all_gather(gain_one.astype(jnp.bfloat16), ("dp", "fsdp"), axis=0, tiled=True),
        lax.all_gather(shift_one.astype(jnp.bfloat16), ("dp", "fsdp"), axis=0, tiled=True),
        lax.all_gather(gain_two.astype(jnp.bfloat16), ("dp", "fsdp"), axis=0, tiled=True),
        lax.all_gather(shift_two.astype(jnp.bfloat16), ("dp", "fsdp"), axis=0, tiled=True),
    )
    expert_set = (
        lax.all_gather(expert_in.astype(jnp.bfloat16), ("dp", "fsdp"), axis=0, tiled=True),
        lax.all_gather(expert_out.astype(jnp.bfloat16), ("dp", "fsdp"), axis=0, tiled=True),
    )
    w_q, w_k, w_v, w_o, gain_b1, shift_b1, gain_b2, shift_b2 = attention_set
    in_full, out_full = expert_set
    seq_ends = jnp.cumsum(lengths[0])
    spots = jnp.arange(row_count, dtype=jnp.int32)
    segment = jnp.sum((spots[:, None] >= seq_ends[None, :]).astype(jnp.int32), axis=1)
    normed, scaled_one, inverse_one = normalize(
        tokens, gain_b1.astype(jnp.float32), shift_b1.astype(jnp.float32)
    )
    normed_low = normed.astype(jnp.bfloat16)
    queries = jnp.dot(normed_low, w_q, preferred_element_type=jnp.float32).astype(jnp.bfloat16)
    key_rows = jnp.dot(normed_low, w_k, preferred_element_type=jnp.float32).astype(jnp.bfloat16)
    value_rows = jnp.dot(normed_low, w_v, preferred_element_type=jnp.float32).astype(jnp.bfloat16)
    query_heads = queries.reshape(row_count, HEADS, HEAD_DIM)
    key_heads = key_rows.reshape(row_count, HEADS, HEAD_DIM)
    value_heads = value_rows.reshape(row_count, HEADS, HEAD_DIM)
    mixed_parts = []
    logsum_parts = []
    for block_start in range(0, row_count, block_size):
        visible = visible_block(segment, spots, padding, block_start, block_size)
        scores = masked_scores(
            query_heads[block_start : block_start + block_size], key_heads, visible, score_scale
        )
        peak = jnp.max(scores, axis=2, keepdims=True)
        shifted_exp = jnp.exp(scores - peak)
        row_total = jnp.sum(shifted_exp, axis=2, keepdims=True)
        attn_weights = (shifted_exp / row_total).astype(jnp.bfloat16)
        mixed_block = jnp.einsum(
            "hqk,khd->qhd", attn_weights, value_heads, preferred_element_type=jnp.float32
        )
        mixed_parts.append(mixed_block.reshape(block_size, width_all))
        logsum_parts.append(peak + jnp.log(row_total))
    mixed = jnp.concatenate(mixed_parts, axis=0).astype(jnp.bfloat16)
    middle = tokens + jnp.dot(mixed, w_o, preferred_element_type=jnp.float32)
    normed_two, scaled_two, inverse_two = normalize(
        middle, gain_b2.astype(jnp.float32), shift_b2.astype(jnp.float32)
    )
    normed_two_low = normed_two.astype(jnp.bfloat16)
    tables = expert_slots(expert_ids[:, 0], experts, CAP)
    inputs_all = with_zero_row(normed_two_low)[tables]
    expert_sum = jnp.zeros((row_count, width_all), jnp.float32)
    for expert in range(experts):
        hidden = jnp.dot(
            inputs_all[expert], in_full[:, expert, :], preferred_element_type=jnp.float32
        )
        activated = jax.nn.gelu(hidden).astype(jnp.bfloat16)
        expert_sum = expert_sum.at[tables[expert]].add(
            jnp.dot(activated, out_full[:, expert, :], preferred_element_type=jnp.float32),
            mode="drop",
        )
    output = middle + expert_sum
    attention_back = (
        lax.all_gather(w_query.astype(jnp.bfloat16), ("dp", "fsdp"), axis=0, tiled=True),
        lax.all_gather(w_key.astype(jnp.bfloat16), ("dp", "fsdp"), axis=0, tiled=True),
        lax.all_gather(w_value.astype(jnp.bfloat16), ("dp", "fsdp"), axis=0, tiled=True),
        lax.all_gather(w_output.astype(jnp.bfloat16), ("dp", "fsdp"), axis=0, tiled=True),
        lax.all_gather(gain_one.astype(jnp.bfloat16), ("dp", "fsdp"), axis=0, tiled=True),
        lax.all_gather(shift_one.astype(jnp.bfloat16), ("dp", "fsdp"), axis=0, tiled=True),
        lax.all_gather(gain_two.astype(jnp.bfloat16), ("dp", "fsdp"), axis=0, tiled=True),
        lax.all_gather(shift_two.astype(jnp.bfloat16), ("dp", "fsdp"), axis=0, tiled=True),
    )
    expert_back = (
        lax.all_gather(expert_in.astype(jnp.bfloat16), ("dp", "fsdp"), axis=0, tiled=True),
        lax.all_gather(expert_out.astype(jnp.bfloat16), ("dp", "fsdp"), axis=0, tiled=True),
    )
    wq_back, wk_back, wv_back, wo_back, gain_c1, shift_c1, gain_c2, shift_c2 = attention_back
    in_back, out_back = expert_back
    grad_low = cotangent.astype(jnp.bfloat16)
    grad_rows = with_zero_row(grad_low)[tables]
    grad_normed_two = jnp.zeros((row_count, width_all), jnp.float32)
    act_list = []
    hidden_grad_list = []
    for expert in range(experts):
        in_slice = in_back[:, expert, :]
        hidden = jnp.dot(inputs_all[expert], in_slice, preferred_element_type=jnp.float32)
        activated, gelu_pull = jax.vjp(jax.nn.gelu, hidden)
        grad_act = jnp.einsum(
            "cd,hd->ch",
            grad_rows[expert],
            out_back[:, expert, :],
            preferred_element_type=jnp.float32,
        )
        grad_hidden = gelu_pull(grad_act)[0].astype(jnp.bfloat16)
        act_list.append(activated.astype(jnp.bfloat16))
        hidden_grad_list.append(grad_hidden)
        grad_inputs = jnp.einsum(
            "ch,dh->cd", grad_hidden, in_slice, preferred_element_type=jnp.float32
        )
        grad_normed_two = grad_normed_two.at[tables[expert]].add(grad_inputs, mode="drop")
    acts_all = jnp.stack(act_list)
    hidden_grads = jnp.stack(hidden_grad_list)
    columns = inputs_all
    grad_expert_in = lax.psum_scatter(
        jnp.einsum("ecd,ech->deh", columns, hidden_grads, preferred_element_type=jnp.float32),
        ("dp", "fsdp"),
        scatter_dimension=0,
        tiled=True,
    )
    columns = acts_all
    grad_expert_out = lax.psum_scatter(
        jnp.einsum("ech,ecd->hed", columns, grad_rows, preferred_element_type=jnp.float32),
        ("dp", "fsdp"),
        scatter_dimension=0,
        tiled=True,
    )
    back_two, grad_gain_two, grad_shift_two = normalize_back(
        grad_normed_two, scaled_two, inverse_two, gain_c2.astype(jnp.float32)
    )
    grad_middle = cotangent + back_two
    grad_branch = grad_middle.astype(jnp.bfloat16)
    grad_w_output = jnp.einsum("tm,td->md", mixed, grad_branch, preferred_element_type=jnp.float32)
    grad_mixed = jnp.einsum(
        "td,md->tm", grad_branch, wo_back, preferred_element_type=jnp.float32
    ).astype(jnp.bfloat16)
    grad_mixed_heads = grad_mixed.reshape(row_count, HEADS, HEAD_DIM)
    grad_keys = jnp.zeros((row_count, HEADS, HEAD_DIM), jnp.float32)
    grad_values = jnp.zeros((row_count, HEADS, HEAD_DIM), jnp.float32)
    grad_query_parts = []
    for block_index, block_start in enumerate(range(0, row_count, block_size)):
        visible = visible_block(segment, spots, padding, block_start, block_size)
        query_block = query_heads[block_start : block_start + block_size]
        scores = masked_scores(query_block, key_heads, visible, score_scale)
        soft = jnp.exp(scores - logsum_parts[block_index])
        grad_block = grad_mixed_heads[block_start : block_start + block_size]
        grad_values = grad_values + jnp.einsum(
            "hqk,qhd->khd",
            soft.astype(jnp.bfloat16),
            grad_block,
            preferred_element_type=jnp.float32,
        )
        grad_soft = jnp.einsum(
            "qhd,khd->hqk", grad_block, value_heads, preferred_element_type=jnp.float32
        )
        row_inner = jnp.sum(soft * grad_soft, axis=2, keepdims=True)
        grad_scores = (soft * (grad_soft - row_inner)).astype(jnp.bfloat16)
        grad_query_parts.append(
            jnp.einsum("hqk,khd->qhd", grad_scores, key_heads, preferred_element_type=jnp.float32)
            * score_scale
        )
        grad_keys = (
            grad_keys
            + jnp.einsum(
                "hqk,qhd->khd", grad_scores, query_block, preferred_element_type=jnp.float32
            )
            * score_scale
        )
    grad_q_low = (
        jnp.concatenate(grad_query_parts, axis=0).reshape(row_count, width_all).astype(jnp.bfloat16)
    )
    grad_k_low = grad_keys.reshape(row_count, width_all).astype(jnp.bfloat16)
    grad_v_low = grad_values.reshape(row_count, width_all).astype(jnp.bfloat16)
    grad_w_query = jnp.einsum(
        "td,te->de", normed_low, grad_q_low, preferred_element_type=jnp.float32
    )
    grad_w_key = jnp.einsum("td,te->de", normed_low, grad_k_low, preferred_element_type=jnp.float32)
    grad_w_value = jnp.einsum(
        "td,te->de", normed_low, grad_v_low, preferred_element_type=jnp.float32
    )
    grad_normed = jnp.einsum("te,de->td", grad_q_low, wq_back, preferred_element_type=jnp.float32)
    grad_normed = grad_normed + jnp.einsum(
        "te,de->td", grad_k_low, wk_back, preferred_element_type=jnp.float32
    )
    grad_normed = grad_normed + jnp.einsum(
        "te,de->td", grad_v_low, wv_back, preferred_element_type=jnp.float32
    )
    back_one, grad_gain_one, grad_shift_one = normalize_back(
        grad_normed, scaled_one, inverse_one, gain_c1.astype(jnp.float32)
    )
    grad_tokens = grad_middle + back_one
    owned = (
        lax.psum_scatter(grad_w_query, ("dp", "fsdp"), scatter_dimension=0, tiled=True),
        lax.psum_scatter(grad_w_key, ("dp", "fsdp"), scatter_dimension=0, tiled=True),
        lax.psum_scatter(grad_w_value, ("dp", "fsdp"), scatter_dimension=0, tiled=True),
        lax.psum_scatter(grad_w_output, ("dp", "fsdp"), scatter_dimension=0, tiled=True),
        lax.psum_scatter(grad_gain_one, ("dp", "fsdp"), scatter_dimension=0, tiled=True),
        lax.psum_scatter(grad_shift_one, ("dp", "fsdp"), scatter_dimension=0, tiled=True),
        lax.psum_scatter(grad_gain_two, ("dp", "fsdp"), scatter_dimension=0, tiled=True),
        lax.psum_scatter(grad_shift_two, ("dp", "fsdp"), scatter_dimension=0, tiled=True),
    )
    return (
        output,
        grad_tokens,
        owned[0],
        owned[1],
        owned[2],
        owned[3],
        owned[4],
        owned[5],
        owned[6],
        owned[7],
        grad_expert_in,
        grad_expert_out,
    )


def solution(mesh):
    in_specs = (
        P(("dp", "fsdp"), None),
        P(("dp", "fsdp"), None),
        P(("dp", "fsdp"), None),
        P(("dp", "fsdp"), None),
        P(("dp", "fsdp"), None),
        P(("dp", "fsdp")),
        P(("dp", "fsdp")),
        P(("dp", "fsdp")),
        P(("dp", "fsdp")),
        P(("dp", "fsdp"), None, None),
        P(("dp", "fsdp"), None, None),
        P(("dp", "fsdp"), None),
        P(("dp", "fsdp"), None),
        P(("dp", "fsdp")),
        P(("dp", "fsdp"), None),
    )
    out_specs = (
        P(("dp", "fsdp"), None),
        P(("dp", "fsdp"), None),
        P(("dp", "fsdp"), None),
        P(("dp", "fsdp"), None),
        P(("dp", "fsdp"), None),
        P(("dp", "fsdp"), None),
        P(("dp", "fsdp")),
        P(("dp", "fsdp")),
        P(("dp", "fsdp")),
        P(("dp", "fsdp")),
        P(("dp", "fsdp"), None, None),
        P(("dp", "fsdp"), None, None),
    )
    return jax.shard_map(local, mesh=mesh, in_specs=in_specs, out_specs=out_specs, check_vma=False)
```

profile of v0, /device:TPU:0, one launch (start us, length us, event | category | flops | bytes accessed | tf_op | source)
XLA Modules:
  0.0 2400.9 jit_solution(1803777890388257590)
XLA Ops:
  19.8 42.6 %all-reduce.12 = (bf16[1024]{0:T(1024)(128)(2,1)S(1)}, bf16[1024]{0:T(1024)(128)(2,1)S(1)}, bf16[1024]{0:T(1024)(128)(2,1)S(1)}, bf16[1024]{0:T(1024)(128)(2,1)S(1)}) all-reduce(bf16[1024]{0:T(1024)(128)(2,1)S(1)} %dynamic-update-slice.1, bf16[1024]{0:T(1024)(128)(2,1)S(1)} %dynamic-update-slice, ...), channel_id=1, replica_groups=mesh['dp'=8,'fsdp'=4] {'dp','fsdp'}, use_global_device_ids=true, to_apply=%add.3 | all-reduce | flops 4096 | bytes 16384
  65.0 4.3 scatter_custom_fusion.1
  69.4 4.5 scatter_custom_fusion
  73.9 3.8 convert_element_type.176
  82.1 5.1 gather_fusion.1
  94.0 4.0 convolution_convert_fusion.2
  99.1 30.9 %all-gather.11.cloned.1.call-done = bf16[1024,1024]{1,0:T(8,128)(2,1)} async-done(((bf16[32,1024]{1,0:T(8,128)(2,1)}), bf16[1024,1024]{1,0:T(8,128)(2,1)}) %all-gather.11.cloned.1.call-update) | async-done | bytes 2097168 | tf_op jit(solution)/shard_map/all_gather | solution.py:93
  130.0 4.6 convolution_convert_fusion.1
  134.6 54.3 %all-gather.7.cloned.1.call-done = bf16[1024,1024]{1,0:T(8,128)(2,1)} async-done(((bf16[32,1024]{1,0:T(8,128)(2,1)}), bf16[1024,1024]{1,0:T(8,128)(2,1)}) %all-gather.7.cloned.1.call-update) | async-done | bytes 2097168 | tf_op jit(solution)/shard_map/all_gather | solution.py:94
  188.9 4.7 convolution_convert_fusion.3
  193.6 14.1 fusion.75
  207.7 13.8 fusion.76
  221.5 15.1 fusion.1
  236.6 5.5 copy-done
  242.1 7.6 fusion
  249.7 13.4 fusion.50
  263.2 13.7 fusion.51
  277.0 6.1 fusion.77
  285.3 5.1 gather_fusion
  290.4 73.7 %all-gather.15.cloned.1.call-done = bf16[1024,2,4096]{2,0,1:T(8,128)(2,1)} async-done(((bf16[32,2,4096]{2,0,1:T(8,128)(2,1)}), bf16[1024,2,4096]{2,0,1:T(8,128)(2,1)}) %all-gather.15.cloned.1.call-update) | async-done | bytes 16777232 | tf_op jit(solution)/shard_map/all_gather | solution.py:102
  364.1 12.2 fusion.37
  377.4 8.1 fusion.33
  385.5 94.5 %all-gather.17.cloned.1.call-done = bf16[4096,2,1024]{2,0,1:T(8,128)(2,1)} async-done(((bf16[128,2,1024]{2,0,1:T(8,128)(2,1)}), bf16[4096,2,1024]{2,0,1:T(8,128)(2,1)}) %all-gather.17.cloned.1.call-update) | async-done | bytes 16777232 | tf_op jit(solution)/shard_map/all_gather | solution.py:103
  480.0 16.9 fusion.25
  496.9 15.2 fusion.18
  512.1 22.7 convolution_bitcast_fusion
  534.8 49.3 %copy.46 = f32[1024,2,4096]{2,1,0:T(2,128)} copy(f32[1024,2,4096]{0,2,1:T(8,128)} %convolution_bitcast_fusion) | data formatting | bytes 67108864 | tf_op jit(solution)/shard_map/ecd,ech->deh/transpose | solution.py:197
  584.2 14.1 fusion.70
  598.3 22.9 convolution_bitcast_fusion.1
  621.9 10.3 fusion.32
  632.3 11.5 scatter_custom_fusion.4
  643.8 10.1 fusion.36
  653.9 13.5 scatter_fusion.2
  667.4 6.0 multiply_reduce_fusion.2
  674.5 3.2 multiply_add_fusion.1
  679.8 4.4 fusion.54
  686.0 4.6 convolution_convert_fusion
  690.8 16.4 fusion.4
  707.1 17.7 add_convert_fusion
  724.9 6.8 fusion.83
  731.7 24.6 %multiply_reduce_fusion.1 = (f32[16,512]{1,0:T(8,128)S(1)}, f32[16,512,1024]{2,1,0:T(8,128)}) fusion(f32[16,512,1024]{2,1,0:T(8,128)} %get-tuple-element.91, f32[16,512]{1,0:T(8,128)S(1)} %log_add_fusion.1, bf16[512,16,64]{0,2,1:T(8,128)(2,1)} %bitcast.124, bf16[1024,16,64]{0,2,1:T(8,128)(2,1)S(1)} %bitcast.118), kind=kOutput, calls=%fused_computation.12 | convolution fusion | flops 1098899456 | bytes 70320128 | tf_op jit(solution)/shard_map/qhd,khd->hqk/dot_general | solution.py:234
  756.4 28.6 %multiply_convert_fusion.1 = bf16[16,512,1024]{2,1,0:T(8,128)(2,1)} fusion(f32[16,512,1024]{2,1,0:T(8,128)} %get-tuple-element.97, f32[16,512,1024]{2,1,0:T(8,128)} %get-tuple-element.91, f32[16,512]{1,0:T(8,128)S(1)} %get-tuple-element.96, f32[16,512]{1,0:T(8,128)S(1)} %log_add_fusion.1), kind=kLoop, calls=%fused_computation.11 | loop fusion | flops 33554432 | bytes 83951616 | tf_op jit(solution)/shard_map/convert_element_type | solution.py:238
  785.0 12.4 fusion.52
  797.4 23.6 multiply_reduce_fusion
  821.0 29.1 %multiply_convert_fusion = bf16[16,512,1024]{2,1,0:T(8,128)(2,1)} fusion(f32[16,512,1024]{2,1,0:T(8,128)} %get-tuple-element.95, f32[16,512,1024]{2,1,0:T(8,128)} %get-tuple-element.89, f32[16,512]{1,0:T(8,128)S(1)} %get-tuple-element.94, f32[16,512]{1,0:T(8,128)S(1)} %log_add_fusion), kind=kLoop, calls=%fused_computation.8 | loop fusion | flops 33554432 | bytes 83951616 | tf_op jit(solution)/shard_map/convert_element_type | solution.py:238
  850.2 12.1 fusion.53
  865.2 4.5 fusion.81
  871.0 8.8 fusion.79
  879.8 9.2 multiply_convert_fusion.4
  889.0 4.4 fusion.82
  893.4 14.8 fusion.35
  908.2 14.5 scatter_fusion
  922.7 4.8 fusion.78
  931.2 5.7 multiply_reduce_fusion.3
  936.9 41.3 %all-reduce.11 = (f32[1024]{0:T(1024)S(1)}, f32[1024]{0:T(1024)S(1)}, f32[1024]{0:T(1024)S(1)}, f32[1024]{0:T(1024)S(1)}) all-reduce(f32[1024]{0:T(1024)S(1)} %get-tuple-element.62, f32[1024]{0:T(1024)S(1)} %get-tuple-element.67, f32[1024]{0:T(1024)S(1)} %copy-done.59, ...), channel_id=6, replica_groups=mesh['dp'=8,'fsdp'=4] {'dp','fsdp'}, use_global_device_ids=true, to_apply=%region_31.32.clone | all-reduce | flops 4096 | bytes 32768
  980.6 12.9 fusion.39
  993.5 13.5 scatter_fusion.1
  1007.0 7.6 multiply_add_fusion
  1014.6 67.8 %all-reduce.15.cloned.1.call-done = f32[1024,2,4096]{2,1,0:T(2,128)} async-done(((f32[1024,2,4096]{2,1,0:T(2,128)}), f32[1024,2,4096]{2,1,0:T(2,128)}) %all-reduce.15.cloned.1.call-update) | async-done | bytes 33554448
  1084.7 711.6 %reduce-scatter.14.cloned.1.call-done = f32[128,2,1024]{0,2,1:T(8,128)} async-done(((f32[4096,2,1024]{0,2,1:T(8,128)}), f32[128,2,1024]{0,2,1:T(8,128)}) %reduce-scatter.14.cloned.1.call-update) | async-done | bytes 1048592 | tf_op jit(solution)/shard_map/reduce_scatter | solution.py:203
  1798.5 148.3 %reduce-scatter.12.cloned.1.call-done = f32[32,1024]{1,0:T(8,128)} async-done(((f32[1024,1024]{1,0:T(8,128)}), f32[32,1024]{1,0:T(8,128)}) %reduce-scatter.12.cloned.1.call-update) | async-done | bytes 131088 | tf_op jit(solution)/shard_map/reduce_scatter | solution.py:277
  1946.8 148.6 %reduce-scatter.10.cloned.1.call-done = f32[32,1024]{1,0:T(8,128)} async-done(((f32[1024,1024]{1,0:T(8,128)}), f32[32,1024]{1,0:T(8,128)}) %reduce-scatter.10.cloned.1.call-update) | async-done | bytes 131088 | tf_op jit(solution)/shard_map/reduce_scatter | solution.py:276
  2095.5 149.4 %reduce-scatter.6.cloned.1.call-done = f32[32,1024]{1,0:T(8,128)} async-done(((f32[1024,1024]{1,0:T(8,128)}), f32[32,1024]{1,0:T(8,128)}) %reduce-scatter.6.cloned.1.call-update) | async-done | bytes 131088 | tf_op jit(solution)/shard_map/reduce_scatter | solution.py:274
  2244.8 149.0 %reduce-scatter.8.cloned.1.call-done = f32[32,1024]{1,0:T(8,128)} async-done(((f32[1024,1024]{1,0:T(8,128)}), f32[32,1024]{1,0:T(8,128)}) %reduce-scatter.8.cloned.1.call-update) | async-done | bytes 131088 | tf_op jit(solution)/shard_map/reduce_scatter | solution.py:275
  (256 shorter events, 50.9 us)
Async XLA Ops:
  7.2 11.7 copy-start.67
  7.2 11.7 copy-start.68
  7.2 11.7 copy-start.69
  7.2 11.7 copy-start.70
  7.2 56.4 %copy-start.71 = (s32[1,8]{1,0:T(1,128)S(1)}, s32[1,8]{1,0:T(1,128)}, u32[]{:S(2)}) copy-start(s32[1,8]{1,0:T(1,128)} %param.26) | copy-start | bytes 100
  7.2 56.6 %copy-start.61 = (s32[1024,1]{0,1:T(1,128)S(1)}, s32[1024,1]{0,1:T(1,128)}, u32[]{:S(2)}) copy-start(s32[1024,1]{0,1:T(1,128)} %param.27) | copy-start | bytes 12292
  7.2 86.7 %all-gather.9.cloned.1.call-start = ((), (), s32[]{:S(2)}) async-start(), calls=%async_computation.6 | async-start | bytes 2162688 | tf_op jit(solution)/shard_map/all_gather | solution.py:92
  8.9 121.1 %all-gather.11.cloned.1.call-start = ((), (), s32[]{:S(2)}) async-start(), calls=%async_computation.7 | async-start | bytes 2162688 | tf_op jit(solution)/shard_map/all_gather | solution.py:93
  10.5 178.4 %all-gather.7.cloned.1.call-start = ((), (), s32[]{:S(2)}) async-start(), calls=%async_computation.5 | async-start | bytes 2162688 | tf_op jit(solution)/shard_map/all_gather | solution.py:94
  12.1 264.9 %all-gather.13.cloned.1.call-start = ((), (), s32[]{:S(2)}) async-start(), calls=%async_computation.8 | async-start | bytes 2162688 | tf_op jit(solution)/shard_map/all_gather | solution.py:95
  13.7 350.4 %all-gather.15.cloned.1.call-start = ((), (), s32[]{:S(2)}) async-start(), calls=%async_computation.9 | async-start | bytes 17301504 | tf_op jit(solution)/shard_map/all_gather | solution.py:102
  16.4 463.6 %all-gather.17.cloned.1.call-start = ((), (), s32[]{:S(2)}) async-start(), calls=%async_computation.10 | async-start | bytes 17301504 | tf_op jit(solution)/shard_map/all_gather | solution.py:103
  18.8 1063.6 %all-reduce.15.cloned.1.call-start = ((), (), s32[]{:S(2)}) async-start(), calls=%async_computation.16 | async-start | bytes 67108864
  62.4 27.8 %copy-start.40 = (f32[1024]{0:T(1024)}, f32[1024]{0:T(1024)S(1)}, u32[]{:S(2)}) copy-start(f32[1024]{0:T(1024)S(1)} %convert_element_type.149) | copy-start | bytes 12292
  63.6 16.6 copy-start.62
  69.3 8.4 copy-start.52
  73.9 3.9 copy-start.54
  82.0 5.1 copy-start.48
  82.1 5.2 copy-start.63
  87.3 4.1 copy-start.36
  90.2 3.7 copy-start.42
  91.4 6.6 copy-start.24
  99.1 94.4 %copy-start.8 = (bf16[512,1024]{0,1:T(8,128)(2,1)}, bf16[512,1024]{0,1:T(8,128)(2,1)S(1)}, u32[]{:S(2)}) copy-start(bf16[512,1024]{0,1:T(8,128)(2,1)S(1)} %get-tuple-element.79) | copy-start | bytes 3145732
  134.6 73.0 %copy-start.6 = (bf16[1024,1024]{0,1:T(8,128)(2,1)}, bf16[1024,1024]{0,1:T(8,128)(2,1)S(1)}, u32[]{:S(2)}) copy-start(bf16[1024,1024]{0,1:T(8,128)(2,1)S(1)} %convolution_convert_fusion.1) | copy-start | bytes 6291460
  188.9 4.7 copy-start.19
  193.5 69.6 %copy-start.10 = (bf16[1024,1024]{0,1:T(8,128)(2,1)}, bf16[1024,1024]{0,1:T(8,128)(2,1)S(1)}, u32[]{:S(2)}) copy-start(bf16[1024,1024]{0,1:T(8,128)(2,1)S(1)} %convolution_convert_fusion.3) | copy-start | bytes 6291460
  193.6 14.1 copy-start.12
  193.6 14.1 copy-start.18
  207.6 42.1 %copy-start.28 = (f32[16,512]{1,0:T(8,128)}, f32[16,512]{1,0:T(8,128)S(1)}, u32[]{:S(2)}) copy-start(f32[16,512]{1,0:T(8,128)S(1)} %get-tuple-element.88) | copy-start | bytes 98308
  221.5 41.7 %copy-start.30 = (f32[16,512]{1,0:T(8,128)}, f32[16,512]{1,0:T(8,128)S(1)}, u32[]{:S(2)}) copy-start(f32[16,512]{1,0:T(8,128)S(1)} %get-tuple-element.90) | copy-start | bytes 98308
  221.5 20.6 copy-start
  236.6 13.1 copy-start.34
  249.7 13.5 copy-start.32
  263.2 13.8 copy-start.72
  277.0 6.1 copy-start.74
  364.1 12.2 copy-start.22
  364.1 13.2 copy-start.64
  377.4 102.6 %copy-start.21 = (bf16[1280,1024]{1,0:T(8,128)(2,1)S(1)}, bf16[1280,1024]{1,0:T(8,128)(2,1)}, u32[]{:S(2)}) copy-start(bf16[1280,1024]{1,0:T(8,128)(2,1)} %gather_fusion.1) | copy-start | bytes 7864324
  480.0 16.9 copy-start.16
  584.1 1212.2 %reduce-scatter.14.cloned.1.call-start = ((), (), s32[]{:S(2)}) async-start(), calls=%async_computation.15 | async-start | bytes 34603008 | tf_op jit(solution)/shard_map/reduce_scatter | solution.py:203
  621.3 1325.6 %reduce-scatter.12.cloned.1.call-start = ((), (), s32[]{:S(2)}) async-start(), calls=%async_computation.14 | async-start | bytes 4325376 | tf_op jit(solution)/shard_map/reduce_scatter | solution.py:277
  621.9 10.4 copy-start.56
  621.9 31.9 %copy-start.50 = (s32[640]{0:T(1024)}, s32[640]{0:T(1024)S(1)}, u32[]{:S(2)}) copy-start(s32[640]{0:T(1024)S(1)} %compare_select_fusion.3) | copy-start | bytes 7684
  653.9 13.5 copy-start.39
  653.9 13.5 copy-start.45
  653.9 13.5 copy-start.47
  667.4 6.0 copy-start.2
  667.4 7.2 copy-start.3
  674.5 5.3 copy-start.73
  674.5 5.3 copy-start.75
  684.2 1411.2 %reduce-scatter.10.cloned.1.call-start = ((), (), s32[]{:S(2)}) async-start(), calls=%async_computation.13 | async-start | bytes 4325376 | tf_op jit(solution)/shard_map/reduce_scatter | solution.py:276
  690.8 16.4 copy-start.15
  724.9 6.8 copy-start.11
  756.3 1488.5 %reduce-scatter.6.cloned.1.call-start = ((), (), s32[]{:S(2)}) async-start(), calls=%async_computation.11 | async-start | bytes 4325376 | tf_op jit(solution)/shard_map/reduce_scatter | solution.py:274
  756.4 28.6 %copy-start.7 = (bf16[1024,1024]{0,1:T(8,128)(2,1)S(1)}, bf16[1024,1024]{0,1:T(8,128)(2,1)}, u32[]{:S(2)}) copy-start(bf16[1024,1024]{0,1:T(8,128)(2,1)} %copy-done.6) | copy-start | bytes 6291460
  850.1 12.1 copy-start.20
  869.7 10.1 copy-start.9
  869.7 1524.1 %reduce-scatter.8.cloned.1.call-start = ((), (), s32[]{:S(2)}) async-start(), calls=%async_computation.12 | async-start | bytes 4325376 | tf_op jit(solution)/shard_map/reduce_scatter | solution.py:275
  879.8 9.2 copy-start.26
  893.4 14.8 copy-start.57
  922.7 4.8 copy-start.65
  931.2 5.7 copy-start.59
  931.2 5.7 copy-start.60
  980.6 12.9 copy-start.51
  (25 other events, 46.5 us)
Sparse Core Ops, SparseCore 0:
  11.6 59.6 all-gather.8
  74.7 55.2 all-gather.10
  133.5 55.3 all-gather.6
  192.2 55.3 all-gather.12
  250.5 113.6 all-gather.14
  367.0 112.9 all-gather.16
  584.3 498.0 all-reduce.14
  1084.7 711.4 reduce-scatter.13
  1799.2 147.5 reduce-scatter.11
  1949.6 145.7 reduce-scatter.9
  2098.4 146.3 reduce-scatter.5
  2247.6 146.1 reduce-scatter.7
where the time goes:
time: 2410 us; the launch traced here: 2400 us
  waiting for transfers between devices  1630 us (68%)
  matrix products  383 us (16%)
  other arithmetic  188 us (8%)
  local copies, waits for them, and re-layouts  101 us (4%)
  blocking collectives  84 us (3%)
    reduce_scatter x1, waiting for transfers between devices, local(): lax.psum_scatter(jnp.einsum('ech,ecd->hed', columns, grad_rows, preferred...  712 us
    reduce_scatter x1, waiting for transfers between devices, local(): lax.psum_scatter(grad_w_query, ('dp', 'fsdp'), scatter_dimension=0, tiled...  149 us
    reduce_scatter x1, waiting for transfers between devices, local(): lax.psum_scatter(grad_w_key, ('dp', 'fsdp'), scatter_dimension=0, tiled=T...  149 us
    reduce_scatter x1, waiting for transfers between devices, local(): lax.psum_scatter(grad_w_value, ('dp', 'fsdp'), scatter_dimension=0, tiled...  149 us
    reduce_scatter x1, waiting for transfers between devices, local(): lax.psum_scatter(grad_w_output, ('dp', 'fsdp'), scatter_dimension=0, tile...  148 us
    all_gather x1, waiting for transfers between devices, local(): lax.all_gather(expert_out.astype(jnp.bfloat16), ('dp', 'fsdp'), axis=0, t...  94.5 us
    unnamed x2, blocking collectives  84 us
    all_gather x1, waiting for transfers between devices, local(): lax.all_gather(expert_in.astype(jnp.bfloat16), ('dp', 'fsdp'), axis=0, ti...  73.7 us
  transfers between devices with their start and end apart: 12, of which 10 were waited for; matrix products, arithmetic and copies ran while one was open for 23% of the time, Pallas kernels for 0%

commit v1 on v0

v1 whole, which is shorter than its diff:
```python
import functools
import math

import jax
import jax.numpy as jnp
from jax import lax
from jax.experimental import pallas as pl
from jax.experimental.pallas import tpu as pltpu
from jax.sharding import Mesh
from jax.sharding import PartitionSpec as P

HEADS = 16
HEAD_DIM = 64
CAP = 640
CHUNKS = 2
PARTS = 2
MIB = 1 << 20

norm_eps = 1e-05
neg_large = -1e30
gelu_c = math.sqrt(2.0 / math.pi)
gelu_k = 0.044715
f32 = jnp.float32
bf16 = jnp.bfloat16


def nt_dot(a, b):
    return lax.dot_general(a, b, (((1,), (1,)), ((), ())), preferred_element_type=f32)


def tn_dot(a, b):
    return lax.dot_general(a, b, (((0,), (0,)), ((), ())), preferred_element_type=f32)


def nn_dot(a, b):
    return jnp.dot(a, b, preferred_element_type=f32)


def params(mib, steps=1):
    return pltpu.CompilerParams(
        vmem_limit_bytes=mib * MIB, dimension_semantics=("arbitrary",) * steps
    )


def cost(us):
    return pl.CostEstimate(flops=int(us * 1.15e9), bytes_accessed=MIB, transcendentals=0)


def whole(shape, buffers=None):
    zeros = (0,) * len(shape)
    if buffers is None:
        return pl.BlockSpec(shape, lambda *_: zeros)
    return pl.BlockSpec(shape, lambda *_: zeros, pipeline_mode=pl.Buffered(buffers))


def run_kernel(kernel, *, in_specs, inputs, deps=(), prefetch=None, grid=(), out_specs, scratch_shapes=(), **rest):
    start = len(inputs) + (prefetch is not None)
    deps = list(deps)

    def body(*refs):
        kernel(*refs[:start], *refs[start + len(deps) :])

    in_specs = list(in_specs) + [pl.BlockSpec(memory_space=pl.ANY)] * len(deps)
    spec = pltpu.PrefetchScalarGridSpec(
        num_scalar_prefetch=int(prefetch is not None),
        grid=grid,
        in_specs=in_specs,
        out_specs=out_specs,
        scratch_shapes=list(scratch_shapes),
    )
    first_args = [] if prefetch is None else [prefetch]
    return pl.pallas_call(body, grid_spec=spec, **rest)(*first_args, *inputs, *deps)


def swap(value, axis):
    return lax.ppermute(value, axis, [(0, 1), (1, 0)])


class Links:
    def __init__(self, bits, fs):
        self.bits = bits
        self.fs = fs
        self.axes = tuple(f"b{k}" for k in range(bits)) + ("core",)

    def axis(self, step, core):
        return (step + core) % self.bits

    def flip(self, step, core):
        return 1 << (self.bits - 1 - self.axis(step, core))

    def mask(self, index, core):
        return sum(self.flip(t, core) for t in range(self.bits) if index >> t & 1)

    def swap(self, value, step):
        pairs = []
        for source in range(2 << self.bits):
            core = source & 1
            pairs.append((source, source ^ (self.flip(step, core) << 1)))
        return lax.ppermute(value, self.axes, pairs)

    def gather_line(self, shard):
        spread = jnp.broadcast_to(shard[None], (self.fs,) + shard.shape)
        return lax.all_to_all(spread, "fsdp", 0, 0)

    def gather_chips(self, block):
        pieces = [block]
        for t in range(self.bits):
            pieces = pieces + [self.swap(p, t) for p in pieces]
        return pieces

    def reduce_chips(self, keep, send):
        for t in reversed(range(self.bits)):
            got = self.swap(send, t)
            if t > 0:
                half = keep.shape[0] // 2
                send = add_low(keep[half:], got[half:])
                keep = add_low(keep[:half], got[:half])
            else:
                keep = add_low(keep[0], got[0])
        return keep

    def reduce_line_direct(self, value, zed):
        total = pick(value, zed, 0).astype(f32)
        for t in range(1, self.fs):
            pairs = [(z, (z + t) % self.fs) for z in range(self.fs)]
            part = lax.ppermute(pick(value, (zed + t) % self.fs, 0), "fsdp", pairs)
            total = total + part.astype(f32)
        return total

    def reduce_line(self, value):
        got = lax.all_to_all(value, "fsdp", 0, 0)
        return jnp.sum(got.astype(f32), axis=0)


def add_low(a, b):
    return (a.astype(f32) + b.astype(f32)).astype(bf16)


def norm_rows(values):
    center = values - jnp.mean(values, axis=1, keepdims=True)
    inverse = lax.rsqrt(jnp.mean(center * center, axis=1, keepdims=True) + norm_eps)
    return center * inverse, inverse


def norm_back(grad_rows, scaled, inverse, gain):
    inner = grad_rows * gain
    return inverse * (
        inner
        - jnp.mean(inner, axis=1, keepdims=True)
        - scaled * jnp.mean(inner * scaled, axis=1, keepdims=True)
    )


def load_rows(ids, pieces, rows, store):
    for i, piece in enumerate(pieces):
        store(pl.multiple_of(ids[len(pieces) // 2 + i] * rows, rows), piece)


def first_kernel(ids, tok, *refs, count, rows, width):
    pieces = refs[:count]
    h_ref, qkv_ref, w_ref, g_ref, norms = refs[count:]

    @pl.when(pl.program_id(0) == 0)
    def _():
        def store(at, piece):
            w_ref[pl.ds(at, rows), :] = piece[:, : 3 * width]
            norms[pl.ds(at, rows), :] = piece[:, 3 * width :].astype(f32)

        load_rows(ids, pieces, rows, store)
        g_ref[...] = jnp.transpose(norms[...])[:8]

    scaled, _ = norm_rows(tok[...])
    h = (scaled * g_ref[0:1, :] + g_ref[1:2, :]).astype(bf16)
    h_ref[...] = h
    for i in range(3):
        out = nn_dot(h, w_ref[:, i * width : (i + 1) * width]).astype(bf16)
        if i == 0:
            out = out * jnp.asarray(1.0 / math.sqrt(HEAD_DIM), bf16)
        qkv_ref[i] = out


def first(ids, tokens, pieces, deps):
    n, d = tokens.shape
    rows, cols = pieces[0].shape
    tile = 256
    return run_kernel(
        functools.partial(first_kernel, count=len(pieces), rows=rows, width=d),
        prefetch=ids,
        inputs=[tokens, *pieces],
        deps=deps,
        grid=(n // tile,),
        in_specs=[pl.BlockSpec((tile, d), lambda i, s: (i, 0))]
        + [whole((rows, cols), 1) for _ in pieces],
        out_specs=[
            pl.BlockSpec((tile, d), lambda i, s: (i, 0)),
            pl.BlockSpec((3, tile, d), lambda i, s: (0, i, 0)),
            whole((d, 3 * d)),
            whole((8, d)),
        ],
        scratch_shapes=[pltpu.VMEM((d, 128), f32)],
        out_shape=[
            jax.ShapeDtypeStruct((n, d), bf16),
            jax.ShapeDtypeStruct((3, n, d), bf16),
            jax.ShapeDtypeStruct((d, 3 * d), bf16),
            jax.ShapeDtypeStruct((8, d), f32),
        ],
        compiler_params=params(56),
        cost_estimate=cost(16),
        name="qkv",
    )


def make_bias(bias, kseg, qseg, n):
    key_at = lax.broadcasted_iota(jnp.int32, (256, n), 0)
    query_at = lax.broadcasted_iota(jnp.int32, (256, n), 1)
    for b in range(n // 256):
        rows = key_at + b * 256
        same = kseg[b * 256 : (b + 1) * 256, 0:1] == qseg[0:1, :]
        seen = (same & (rows <= query_at)) | (rows == query_at)
        bias[b * 256 : (b + 1) * 256, :] = jnp.where(seen, 0.0, neg_large)


def head_mask(block, head):
    lane = lax.broadcasted_iota(jnp.int32, block.shape, 1)
    return jnp.where((lane < HEAD_DIM) == (head == 0), block, jnp.zeros_like(block))


def attend_kernel(kseg, qseg, qkv, o_ref, lse_ref, bias, *, n):
    @pl.when(pl.program_id(0) == 0)
    def _():
        make_bias(bias, kseg, qseg, n)

    k = qkv[1]
    v_t = jnp.transpose(qkv[2])
    for i in range(n // 256):
        keys = (i + 1) * 256
        cols = slice(i * 256, keys)
        q = qkv[0, cols, :]
        parts = []
        for head in range(2):
            s = nt_dot(k[:keys], head_mask(q, head)) + bias[:keys, cols]
            peak = jnp.max(s, axis=0, keepdims=True)
            e = jnp.exp(s - peak)
            total = jnp.sum(e, axis=0, keepdims=True)
            p = (e * (1.0 / total)).astype(bf16)
            parts.append(nn_dot(v_t[head * HEAD_DIM : (head + 1) * HEAD_DIM, :keys], p))
            lse_ref[0, head : head + 1, cols] = peak + jnp.log(total)
        o_ref[cols, :] = jnp.transpose(jnp.concatenate(parts, axis=0)).astype(bf16)


def attend(kseg, qseg, qkv, part, parts, deps):
    _, n, d = qkv.shape
    pairs = d // 128 // parts
    d = d // parts
    return run_kernel(
        functools.partial(attend_kernel, n=n),
        inputs=[kseg, qseg, qkv],
        deps=deps,
        grid=(pairs,),
        in_specs=[
            whole(kseg.shape),
            whole(qseg.shape),
            pl.BlockSpec((3, n, 128), lambda p: (0, 0, p + part * pairs)),
        ],
        out_specs=[
            pl.BlockSpec((n, 128), lambda p: (0, p)),
            pl.BlockSpec((1, 8, n), lambda p: (p, 0, 0)),
        ],
        out_shape=[
            jax.ShapeDtypeStruct((n, d), bf16),
            jax.ShapeDtypeStruct((pairs, 8, n), f32),
        ],
        scratch_shapes=[pltpu.VMEM((n, n), f32)],
        compiler_params=params(48),
        cost_estimate=cost(21),
        name="attend",
    )


def attend_back_kernel(kseg, qseg, qkv, do_ref, lse_ref, out, bias, dk_acc, dv_acc, *, n):
    @pl.when(pl.program_id(0) == 0)
    def _():
        make_bias(bias, kseg, qseg, n)

    k = qkv[1]
    v = qkv[2]
    k_t = jnp.transpose(k)
    blocks = n // 256
    for i in reversed(range(blocks)):
        keys = (i + 1) * 256
        cols = slice(i * 256, keys)
        parts = []
        for head in range(2):
            q = head_mask(qkv[0, cols, :], head)
            go = head_mask(do_ref[cols, :], head)
            s = nt_dot(k[:keys], q) + bias[:keys, cols]
            p = jnp.exp(s - lse_ref[0, head : head + 1, cols])
            dp = nt_dot(v[:keys], go)
            inner = jnp.sum(p * dp, axis=0, keepdims=True)
            ds = (p * (dp - inner)).astype(bf16)
            dv = nn_dot(p.astype(bf16), go)
            dk = nn_dot(ds, q)
            if i == blocks - 1 and head == 0:
                dv_acc[...] = dv
                dk_acc[...] = dk
            else:
                dv_acc[:keys, :] += dv
                dk_acc[:keys, :] += dk
            parts.append(nn_dot(k_t[head * HEAD_DIM : (head + 1) * HEAD_DIM, :keys], ds))
        dq = jnp.concatenate(parts, axis=0) * (1.0 / math.sqrt(HEAD_DIM))
        out[0, cols, :] = jnp.transpose(dq).astype(bf16)
    out[1] = dk_acc[...].astype(bf16)
    out[2] = dv_acc[...].astype(bf16)


def attend_back(kseg, qseg, qkv, grad_mixed, lse, part, parts, deps):
    _, n, d = qkv.shape
    pairs = d // 128 // parts
    d = d // parts
    return run_kernel(
        functools.partial(attend_back_kernel, n=n),
        inputs=[kseg, qseg, qkv, grad_mixed, lse],
        deps=deps,
        grid=(pairs,),
        in_specs=[
            whole(kseg.shape),
            whole(qseg.shape),
            pl.BlockSpec((3, n, 128), lambda p: (0, 0, p + part * pairs)),
            pl.BlockSpec((n, 128), lambda p: (0, p + part * pairs)),
            pl.BlockSpec((1, 8, n), lambda p: (p, 0, 0)),
        ],
        out_specs=pl.BlockSpec((3, n, 128), lambda p: (0, 0, p)),
        out_shape=jax.ShapeDtypeStruct((3, n, d), bf16),
        scratch_shapes=[
            pltpu.VMEM((n, n), f32),
            pltpu.VMEM((n, 128), f32),
            pltpu.VMEM((n, 128), f32),
        ],
        compiler_params=params(56),
        cost_estimate=cost(11),
        name="attend_back",
    )


def slot_hot(slot_row, start, count):
    n = slot_row.shape[1]
    at = lax.broadcasted_iota(jnp.int32, (count, n), 0) + start
    return jnp.where(at == slot_row, 1.0, 0.0).astype(bf16)


def pack_kernel(slot_row, values, own, other):
    low = values[...].astype(bf16)
    own[...] = nn_dot(slot_hot(slot_row[0:1, :], 0, CAP), low).astype(bf16)
    other[...] = nn_dot(slot_hot(slot_row[0:1, :], CAP, CAP), low).astype(bf16)


def pack(slot_row, values):
    n, d = values.shape
    return pl.pallas_call(
        pack_kernel,
        in_specs=[whole(slot_row.shape), whole((n, d))],
        out_specs=[whole((CAP, d))] * 2,
        out_shape=[jax.ShapeDtypeStruct((CAP, d), bf16)] * 2,
        compiler_params=pltpu.CompilerParams(vmem_limit_bytes=48 * MIB),
        cost_estimate=cost(5),
        name="pack",
    )(slot_row, values)


def second_kernel(ids, slot_row, tok, gains, *refs, count, rows, steps, tile, parts):
    mixed, refs = refs[:parts], refs[parts:]
    pieces = refs[:count]
    x_ref, w_ref, own, other, h_all = refs[count:]
    step = pl.program_id(0)

    @pl.when(step == 0)
    def _():
        def store(at, piece):
            w_ref[pl.ds(at, rows), :] = piece[...]

        load_rows(ids, pieces, rows, store)

    x = tok[...]
    wide = mixed[0].shape[1]
    for i, o_ref in enumerate(mixed):
        x = x + nn_dot(o_ref[...], w_ref[i * wide : (i + 1) * wide, :])
    x_ref[...] = x
    scaled, _ = norm_rows(x)
    h = (scaled * gains[2:3, :] + gains[3:4, :]).astype(bf16)
    h_all[pl.ds(pl.multiple_of(step * tile, tile), tile), :] = h

    @pl.when(step == steps - 1)
    def _():
        own[...] = nn_dot(slot_hot(slot_row[0:1, :], 0, CAP), h_all[...]).astype(bf16)
        other[...] = nn_dot(slot_hot(slot_row[0:1, :], CAP, CAP), h_all[...]).astype(bf16)


def second(ids, slot_row, mixed, tokens, gains, pieces, deps):
    n, d = tokens.shape
    rows, _ = pieces[0].shape
    tile = 256
    return run_kernel(
        functools.partial(
            second_kernel, count=len(pieces), rows=rows, steps=n // tile, tile=tile, parts=len(mixed)
        ),
        prefetch=ids,
        inputs=[slot_row, tokens, gains, *mixed, *pieces],
        deps=deps,
        **dict(
            grid=(n // tile,),
            in_specs=[
                whole(slot_row.shape),
                pl.BlockSpec((tile, d), lambda i, s: (i, 0)),
                whole(gains.shape),
            ]
            + [pl.BlockSpec((tile, o.shape[1]), lambda i, s: (i, 0)) for o in mixed]
            + [whole((rows, d), 1) for _ in pieces],
            out_specs=[
                pl.BlockSpec((tile, d), lambda i, s: (i, 0)),
                whole((d, d)),
                whole((CAP, d)),
                whole((CAP, d)),
            ],
            scratch_shapes=[pltpu.VMEM((n, d), bf16)],
        ),
        out_shape=[
            jax.ShapeDtypeStruct((n, d), f32),
            jax.ShapeDtypeStruct((d, d), bf16),
            jax.ShapeDtypeStruct((CAP, d), bf16),
            jax.ShapeDtypeStruct((CAP, d), bf16),
        ],
        compiler_params=params(56),
        cost_estimate=cost(13),
        name="mix_out",
    )


def expert_kernel(ids, *refs, count, rows, tile, first_chunk, block):
    half = count // 2
    xs, ys = refs[0:2], refs[2:4]
    pos = 4
    prior = None
    if not first_chunk:
        prior = refs[pos : pos + 4]
        pos += 4
    pieces = refs[pos : pos + count]
    pos += count
    y_out, h_out = refs[pos : pos + 2], refs[pos + 2 : pos + 4]
    keep, send = refs[pos + 4 : pos + 6]
    x_s, dy_s, win_s, wout_s, y_acc, h_acc, a_s, du_s, sems = refs[pos + 6 :]
    step = pl.program_id(0)
    d = x_s.shape[1]
    slabs = win_s.shape[1] // d
    total = 2 * CAP

    @pl.when(step == 0)
    def _():
        copies = []

        def fetch(source, target):
            copy = pltpu.make_async_copy(source, target, sems.at[len(copies)])
            copy.start()
            copies.append(copy)

        for side in range(2):
            fetch(xs[side], x_s.at[pl.ds(side * CAP, CAP)])
        for i in range(count):
            at = pl.multiple_of(ids[i] * rows, rows)
            for h in range(slabs):
                fetch(
                    pieces[i].at[pl.ds(h * rows, rows)],
                    win_s.at[pl.ds(at, rows), pl.ds(h * d, d)],
                )
        for side in range(2):
            fetch(ys[side], dy_s.at[pl.ds(side * CAP, CAP)])
        for i in range(count):
            at = pl.multiple_of(ids[i] * tile, tile)
            fetch(pieces[i].at[pl.ds(slabs * rows, tile)], wout_s.at[pl.ds(at, tile)])
        if first_chunk:
            y_acc[...] = jnp.zeros_like(y_acc)
            h_acc[...] = jnp.zeros_like(h_acc)
        else:
            for side in range(2):
                span = slice(side * CAP, (side + 1) * CAP)
                y_acc[span, :] = prior[side][...].astype(f32)
                h_acc[span, :] = prior[2 + side][...].astype(f32)
        for copy in copies:
            copy.wait()

    at = pl.multiple_of(ids[step] * tile, tile)

    def one_block(b, carry):
        span = pl.ds(pl.multiple_of(b * block, block), block)
        u = nn_dot(x_s[span, :], win_s[:, pl.ds(at, tile)])
        da = nt_dot(dy_s[span, :], wout_s[pl.ds(at, tile), :])
        square = u * u
        t = jnp.tanh(gelu_c * (u * (1.0 + gelu_k * square)))
        up = 0.5 * (1.0 + t)
        slope = up + (0.5 * gelu_c) * u * (1.0 - t * t) * (1.0 + 3.0 * gelu_k * square)
        a = (u * up).astype(bf16)
        du = (da * slope).astype(bf16)
        a_s[span, :] = a
        du_s[span, :] = du
        y_acc[span, :] += nn_dot(a, wout_s[pl.ds(at, tile), :])
        h_acc[span, :] += nt_dot(du, win_s[:, pl.ds(at, tile)])
        return carry

    lax.fori_loop(0, total // block, one_block, 0)
    grad = tn_dot(a_s[...], dy_s[...]).astype(bf16)

    @pl.when(step < half)
    def _():
        keep[step, slabs * rows :, :] = grad

    @pl.when(step >= half)
    def _():
        send[step - half, slabs * rows :, :] = grad

    slab = at // d
    row = pl.multiple_of(slab * rows, rows)
    col = pl.multiple_of(at - slab * d, tile)

    def one_piece(i, carry):
        for out, index in ((keep, i), (send, i + half)):
            src = pl.multiple_of(ids[index] * rows, rows)
            out[i, pl.ds(row, rows), pl.ds(col, tile)] = tn_dot(
                x_s[:, pl.ds(src, rows)], du_s[...]
            ).astype(bf16)
        return carry

    lax.fori_loop(0, half, one_piece, 0)

    @pl.when(step == count - 1)
    def _():
        for side in range(2):
            span = slice(side * CAP, (side + 1) * CAP)
            y_out[side][...] = y_acc[span, :].astype(bf16)
            h_out[side][...] = h_acc[span, :].astype(bf16)


def expert(ids, xs, ys, prior, pieces, rows, tile, deps):
    count = len(pieces)
    half = count // 2
    d = xs[0].shape[1]
    hc = count * tile
    total = 2 * CAP
    first_chunk = prior is None
    far = pl.BlockSpec(memory_space=pl.ANY)
    both = (half,) + pieces[0].shape
    return run_kernel(
        functools.partial(
            expert_kernel, count=count, rows=rows, tile=tile, first_chunk=first_chunk, block=320
        ),
        prefetch=ids,
        inputs=list(xs) + list(ys) + list(prior or ()) + list(pieces),
        deps=deps,
        grid=(count,),
        in_specs=[far] * 4
        + ([] if first_chunk else [whole((CAP, d), 1)] * 4)
        + [far] * count,
        out_specs=[whole((CAP, d), 1)] * 4 + [whole(both, 1)] * 2,
        scratch_shapes=[
            pltpu.VMEM((total, d), bf16),
            pltpu.VMEM((total, d), bf16),
            pltpu.VMEM((d, hc), bf16),
            pltpu.VMEM((hc, d), bf16),
            pltpu.VMEM((total, d), f32),
            pltpu.VMEM((total, d), f32),
            pltpu.VMEM((total, tile), bf16),
            pltpu.VMEM((total, tile), bf16),
            pltpu.SemaphoreType.DMA((4 + (hc // d + 1) * count,)),
        ],
        out_shape=[jax.ShapeDtypeStruct((CAP, d), bf16)] * 4
        + [jax.ShapeDtypeStruct(both, bf16)] * 2,
        compiler_params=params(60),
        cost_estimate=cost(27),
        name="experts",
    )


def third_kernel(slot_col, gains, x_ref, cot, w_ref, *refs):
    y_own, y_other, h_own, h_other = refs[:4]
    out_ref, mid_ref, dz_ref, do_ref, g_ref = refs[4:]
    tile = x_ref.shape[0]
    at = lax.broadcasted_iota(jnp.int32, (tile, CAP), 1)
    own = jnp.where(slot_col[:, 0:1] == at, 1.0, 0.0).astype(bf16)
    other = jnp.where(slot_col[:, 0:1] == at + CAP, 1.0, 0.0).astype(bf16)
    x = x_ref[...]
    out_ref[...] = x + nn_dot(own, y_own[...]) + nn_dot(other, y_other[...])
    dh = nn_dot(own, h_own[...]) + nn_dot(other, h_other[...])
    scaled, inverse = norm_rows(x)
    mid = cot[...] + norm_back(dh, scaled, inverse, gains[2:3, :])
    mid_ref[...] = mid
    dz = mid.astype(bf16)
    dz_ref[...] = dz
    do_ref[...] = nt_dot(dz, w_ref[...]).astype(bf16)

    @pl.when(pl.program_id(0) == 0)
    def _():
        g_ref[...] = jnp.zeros_like(g_ref)

    g_ref[0:1, :] += jnp.sum(dh * scaled, axis=0, keepdims=True)
    g_ref[1:2, :] += jnp.sum(dh, axis=0, keepdims=True)


def third(slot_col, gains, middle, cot, w_out, returned, deps):
    n, d = middle.shape
    tile = 256
    row = pl.BlockSpec((tile, d), lambda i: (i, 0))
    return run_kernel(
        third_kernel,
        inputs=[slot_col, gains, middle, cot, w_out, *returned],
        deps=deps,
        grid=(n // tile,),
        in_specs=[
            pl.BlockSpec((tile, slot_col.shape[1]), lambda i: (i, 0)),
            whole(gains.shape),
            row,
            row,
            whole((d, d), 1),
        ]
        + [whole((CAP, d), 1)] * 4,
        out_specs=[row, row, row, row, whole((8, d))],
        out_shape=[
            jax.ShapeDtypeStruct((n, d), f32),
            jax.ShapeDtypeStruct((n, d), f32),
            jax.ShapeDtypeStruct((n, d), bf16),
            jax.ShapeDtypeStruct((n, d), bf16),
            jax.ShapeDtypeStruct((8, d), f32),
        ],
        compiler_params=params(56),
        cost_estimate=cost(8),
        name="combine",
    )


def weights_kernel(ids, right, *refs, count, rows, lefts):
    keep, send, left_t, res = refs[lefts:]

    @pl.when(pl.program_id(0) == 0)
    def _():
        wide = refs[0].shape[1]
        for i in range(lefts):
            left_t[i * wide : (i + 1) * wide, :] = jnp.transpose(refs[i][...])

    res[...] = nn_dot(left_t[...], right[0])
    for i in range(count):
        for out, r in ((keep, count + i), (send, 2 * count + i)):
            src = pl.multiple_of(ids[r] * rows, rows)
            out[i] = res[pl.ds(src, rows), :].astype(bf16)


def weights(ids, lefts, right, count, deps=(), tile=512):
    n = right.shape[1]
    d = sum(left.shape[1] for left in lefts)
    parts, _, wide = right.shape
    per = wide // tile
    rows = d // (2 * count)
    out = pl.BlockSpec((count, rows, tile), lambda j, s: (0, 0, j))
    return run_kernel(
        functools.partial(weights_kernel, count=count, rows=rows, lefts=len(lefts)),
        prefetch=ids,
        inputs=[right, *lefts],
        deps=deps,
        grid=(parts * per,),
        in_specs=[pl.BlockSpec((1, n, tile), lambda j, s: (j // per, 0, j % per))]
        + [whole(left.shape, 1) for left in lefts],
        out_specs=[out, out],
        scratch_shapes=[pltpu.VMEM((d, n), bf16), pltpu.VMEM((d, tile), f32)],
        out_shape=[jax.ShapeDtypeStruct((count, rows, parts * wide), bf16)] * 2,
        compiler_params=params(48),
        cost_estimate=cost(4),
        name="weight_grads",
    )


def last_kernel(gains, tok, mid, w_ref, *refs):
    grads, (out_ref, g_ref) = refs[:-2], refs[-2:]
    d = tok.shape[1]
    wide = grads[0].shape[2]
    dh = None
    for j, grad in enumerate(grads):
        for i in range(3):
            at = i * d + j * wide
            term = nt_dot(grad[i], w_ref[:, at : at + wide])
            dh = term if dh is None else dh + term
    scaled, inverse = norm_rows(tok[...])
    out_ref[...] = mid[...] + norm_back(dh, scaled, inverse, gains[0:1, :])

    @pl.when(pl.program_id(0) == 0)
    def _():
        g_ref[...] = jnp.zeros_like(g_ref)

    g_ref[0:1, :] += jnp.sum(dh * scaled, axis=0, keepdims=True)
    g_ref[1:2, :] += jnp.sum(dh, axis=0, keepdims=True)


def last(gains, tokens, middle_grad, dqkv, w_qkv, deps):
    n, d = tokens.shape
    tile = 256
    row = pl.BlockSpec((tile, d), lambda i: (i, 0))
    return run_kernel(
        last_kernel,
        inputs=[gains, tokens, middle_grad, w_qkv, *dqkv],
        deps=deps,
        grid=(n // tile,),
        in_specs=[
            whole(gains.shape),
            row,
            row,
            whole((d, 3 * d), 1),
        ]
        + [pl.BlockSpec((3, tile, g.shape[2]), lambda i: (0, i, 0)) for g in dqkv],
        out_specs=[row, whole((8, d))],
        out_shape=[jax.ShapeDtypeStruct((n, d), f32), jax.ShapeDtypeStruct((8, d), f32)],
        compiler_params=params(48),
        cost_estimate=cost(8),
        name="token_grads",
    )


def pick(value, index, axis):
    return lax.dynamic_index_in_dim(value, index, axis, keepdims=False)


def after(value, other):
    mark = other.reshape(-1)[0] * jnp.zeros((), other.dtype)
    return value + mark.astype(value.dtype)


def in_order(core, mine, theirs):
    return jnp.where(core == 0, jnp.stack([mine, theirs]), jnp.stack([theirs, mine]))


def local(
    tokens,
    w_query,
    w_key,
    w_value,
    w_output,
    gain_one,
    shift_one,
    gain_two,
    shift_two,
    expert_in,
    expert_out,
    lengths,
    expert_ids,
    padding,
    cotangent,
    *,
    bits,
    fs,
):
    n, d = tokens.shape
    share, _, hidden = expert_in.shape
    owned = expert_out.shape[0]
    chips = 1 << bits
    devices = 2 * chips * fs
    per = owned // CHUNKS
    hc = hidden // CHUNKS
    links = Links(bits, fs)
    core = lax.axis_index("core")
    zed = lax.axis_index("fsdp")
    chip = jnp.int32(0)
    for k in range(bits):
        chip = chip * 2 + lax.axis_index(f"b{k}")
    orders = jnp.array([[links.mask(i, c) for i in range(chips)] for c in range(2)], jnp.int32)
    near, far = chip ^ pick(orders, core, 0), chip ^ pick(orders, 1 - core, 0)
    ids = jnp.concatenate([near, near * 2 + core, far * 2 + 1 - core]).astype(jnp.int32)

    norms = jnp.stack([gain_one, shift_one, gain_two, shift_two], axis=1)
    norms = jnp.pad(norms, ((0, 0), (0, 124)))
    shard = jnp.concatenate([w_query, w_key, w_value, norms, w_output], axis=1).astype(bf16)
    line = links.gather_line(shard).reshape(fs * share, -1)

    def gather_attention(block):
        own = links.gather_chips(block)
        return own + [swap(piece, "core") for piece in own]

    qkv_pieces = gather_attention(line[:, : 3 * d + 128])
    out_pieces = gather_attention(line[:, 3 * d + 128 :])

    slabs = hc // d
    in_rows, out_rows = 2 * fs * share, 2 * fs * per
    in_low = expert_in.astype(bf16).transpose(1, 0, 2).reshape(2, share, devices, CHUNKS, per)
    in_low = in_low.transpose(0, 3, 1, 2, 4).reshape(2, CHUNKS, share, slabs, d)
    in_low = in_low.transpose(0, 1, 3, 2, 4).reshape(2, CHUNKS, slabs * share, d)
    out_low = expert_out.astype(bf16).transpose(1, 0, 2).reshape(2, CHUNKS, per, d)
    low = jnp.concatenate([in_low, out_low], axis=2)
    pair = in_order(core, pick(low, core, 0), swap(pick(low, 1 - core, 0), "core"))
    chunks, lines = [], []
    before = line
    for j in range(CHUNKS):
        got = links.gather_line(after(pair[:, j], before))
        in_part = got[:, :, : slabs * share].reshape(fs, 2, slabs, share, d)
        in_part = in_part.transpose(2, 1, 0, 3, 4).reshape(slabs * in_rows, d)
        out_part = got[:, :, slabs * share :].transpose(1, 0, 2, 3).reshape(out_rows, d)
        lines.append(jnp.concatenate([in_part, out_part], axis=0))
        chunks.append(links.gather_chips(lines[-1]))
        before = chunks[-1][1]

    spots = jnp.arange(n, dtype=jnp.int32)
    eight = jnp.arange(lengths.shape[1])
    ends = jnp.sum(jnp.where(eight[:, None] <= eight[None, :], lengths[0][:, None], 0), axis=0)
    segment = jnp.sum((spots[:, None] >= ends[None, :]).astype(jnp.int32), axis=1)
    key_segment = jnp.where(padding == 1, segment, -1)
    kseg = jnp.broadcast_to(key_segment[:, None], (n, 128))
    qseg = jnp.broadcast_to(segment[None, :], (8, n))
    chosen = expert_ids[:, 0]
    names = jnp.arange(2, dtype=jnp.int32)
    hot = (chosen[:, None] == names[None, :]).astype(bf16)
    before = (spots[:, None] > spots[None, :]).astype(bf16)
    place = nn_dot(before, hot).astype(jnp.int32)
    place = jnp.where(chosen == 0, place[:, 0], place[:, 1])
    slot = jnp.where(chosen == core, place, CAP + place)
    slot_row = jnp.broadcast_to(slot[None, :], (8, n))
    slot_col = jnp.broadcast_to(slot[:, None], (n, 128))

    dy_own, dy_other = pack(slot_row, cotangent)
    dys = (dy_own, swap(dy_other, "core"))
    h1, qkv, w_qkv, gains = first(ids, tokens, qkv_pieces, [lines[0]])
    mixed, lse = [], []
    needs = [[chunks[0][1], *out_pieces[chips:]], []]
    for i in range(PARTS):
        made = attend(kseg, qseg, qkv, i, PARTS, needs[i] + lse[-1:])
        mixed.append(made[0])
        lse.append(made[1])
    middle, w_out, x_own, x_other = second(ids, slot_row, mixed, tokens, gains, out_pieces, [lines[1]])
    xs = (x_own, swap(x_other, "core"))

    def chip_rows(keep, send):
        t = bits - 1
        got = links.swap(send, t)
        while t > 0:
            half = keep.shape[0] // 2
            send, keep = add_low(keep[half:], got[half:]), add_low(keep[:half], got[:half])
            yield send
            t -= 1
            got = links.swap(send, t)
        total = add_low(keep[0], got[0])
        in_part = total[: slabs * in_rows].reshape(slabs, 2, fs, share, d)
        in_part = in_part.transpose(2, 1, 0, 3, 4).reshape(fs, 2, slabs * share, d)
        out_part = total[slabs * in_rows :].reshape(2, fs, per, d).transpose(1, 0, 2, 3)
        total = jnp.concatenate([in_part, out_part], axis=2)
        yield total
        yield links.reduce_line(total)

    made = expert(ids, xs, dys, None, chunks[0], in_rows, out_rows, [chunks[1][1]])
    stages = [list(chip_rows(made[4], made[5]))]
    made = expert(ids, xs, dys, made[:4], chunks[1], in_rows, out_rows, [])
    stages.append(list(chip_rows(made[4], made[5])))
    y_own, y_far, h_own, h_far = made[:4]
    returned = (y_own, swap(y_far, "core"), h_own, swap(h_far, "core"))

    output, grad_middle, dz, grad_mixed, sums_two = third(
        slot_col, gains, middle, cotangent, w_out, returned, [stages[0][0]]
    )

    def attention_rows(keep, send):
        keep = add_low(keep, swap(send, "core"))
        half = chips // 2
        yield keep
        got = links.reduce_chips(keep[:half], keep[half:])
        yield got.reshape(fs, share, -1)

    wide = d // PARTS
    made = weights(ids, mixed, dz[None], chips)
    out_stages = list(attention_rows(*made))
    grads, qkv_stages = [], []
    needs = [[stages[0][-2]], [stages[1][0]]]
    for i in range(PARTS):
        grads.append(
            attend_back(kseg, qseg, qkv, grad_mixed, lse[i], i, PARTS, needs[i] + [made[1]])
        )
        made = weights(ids, [h1], grads[i], chips, [[out_stages[0]], [stages[0][-1], stages[1][-2]]][i])
        qkv_stages.append(list(attention_rows(*made)))
    grad_tokens, sums_one = last(
        gains, tokens, grad_middle, grads, w_qkv, [made[1], qkv_stages[0][-1], out_stages[-1]]
    )
    ready = [g[-1] for g in qkv_stages] + [out_stages[-1]]
    ready = links.reduce_line_direct(jnp.concatenate(ready, axis=2), zed)
    grad_qkv = [
        jnp.concatenate(
            [ready[:, (3 * j + i) * wide : (3 * j + i + 1) * wide] for j in range(PARTS)], axis=1
        )
        for i in range(3)
    ]
    grad_output = ready[:, 3 * d :]

    def settle(rows):
        return in_order(core, pick(rows, core, 0), swap(pick(rows, 1 - core, 0), "core"))

    totals = [settle(s[-1]) for s in stages]
    grad_expert_in = jnp.stack(
        [g[:, : slabs * share].reshape(2, slabs, share, d) for g in totals], axis=0
    )
    grad_expert_in = grad_expert_in.transpose(3, 1, 0, 2, 4).reshape(share, 2, CHUNKS, devices, per)
    grad_expert_in = grad_expert_in.transpose(0, 1, 3, 2, 4).reshape(share, 2, hidden)
    grad_expert_out = jnp.stack([g[:, slabs * share :] for g in totals], axis=1)
    grad_expert_out = grad_expert_out.reshape(2, owned, d).transpose(1, 0, 2)

    sums = jnp.concatenate([sums_one[:2], sums_two[:2]]).reshape(4, devices, share).transpose(1, 0, 2)
    sums = jnp.sum(lax.all_to_all(sums, links.axes + ("fsdp",), 0, 0), axis=0)

    return (
        output,
        grad_tokens,
        grad_qkv[0],
        grad_qkv[1],
        grad_qkv[2],
        grad_output,
        sums[0],
        sums[1],
        sums[2],
        sums[3],
        grad_expert_in,
        grad_expert_out,
    )


def solution(mesh):
    dp, fs = mesh.shape["dp"], mesh.shape["fsdp"]
    bits = (dp // 2).bit_length() - 1
    names = tuple(f"b{k}" for k in range(bits)) + ("core", "fsdp")
    fine = Mesh(mesh.devices.reshape((2,) * (bits + 1) + (fs,)), names)
    rows = lambda rank: P(names, *([None] * (rank - 1)))
    in_specs = tuple(rows(r) for r in (2, 2, 2, 2, 2, 1, 1, 1, 1, 3, 3, 2, 2, 1, 2))
    out_specs = tuple(rows(r) for r in (2, 2, 2, 2, 2, 2, 1, 1, 1, 1, 3, 3))
    return jax.shard_map(
        functools.partial(local, bits=bits, fs=fs),
        mesh=fine,
        in_specs=in_specs,
        out_specs=out_specs,
        check_vma=False,
    )
```

time: 2410 us -> 606 us (0.25)
  waiting for transfers between devices: 1630 us -> 160 us
  matrix products: 383 us -> 0.6 us
  Pallas kernels: 0 us -> 282 us
  other arithmetic: 188 us -> 43.8 us
  blocking collectives: 84 us -> 10.6 us
  local copies, waits for them, and re-layouts: 101 us -> 40.5 us
  starting transfers between devices: 0.9 us -> 58.6 us
    reduce_scatter x5 -> x0, waiting for transfers between devices: 1310 us -> none  [the longest x1 712 us: local(): lax.psum_scatter(jnp.einsum('ech,ecd->hed', columns, grad_rows, preferred...]
    dot_general x34 -> x1, matrix products: 383 us -> 0.6 us  [nn_dot(): return jnp.dot(a, b, preferred_element_type=f32)]
    pallas_call x0 -> x14, Pallas kernels: none -> 282 us  [the longest x13 277 us: run_kernel(): pl.pallas_call(body, grid_spec=spec, **rest)(*first_args, *inputs, *deps)]
    all_gather x6 -> x0, waiting for transfers between devices: 253 us -> none  [the longest x1 94.5 us: local(): lax.all_gather(expert_out.astype(jnp.bfloat16), ('dp', 'fsdp'), axis=0, t...]
    ppermute x0 -> x43, waiting for transfers between devices: none -> 86.8 us  [the longest x22 75.3 us: swap(): return lax.ppermute(value, self.axes, pairs)]
    unnamed x2 -> x0, blocking collectives: 84 us -> none
    all_to_all x0 -> x5, waiting for transfers between devices: none -> 72.8 us  [the longest x2 44.6 us: reduce_line(): got = lax.all_to_all(value, 'fsdp', 0, 0)]
    unnamed x13 -> x0, waiting for transfers between devices: 68 us -> none
  transfers between devices with their start and end apart: 12 -> 48, of which waited for: 10 -> 18; matrix products, arithmetic and copies ran while one was open for 23% -> 10% of each run, Pallas kernels for 0% -> 43%
where the time goes in v1:
time: 606 us; the launch traced here: 598 us
  Pallas kernels  282 us (47%)
  waiting for transfers between devices  160 us (26%)
  starting transfers between devices  58.6 us (10%)
  other arithmetic  43.8 us (7%)
  local copies, waits for them, and re-layouts  40.5 us (7%)
  blocking collectives  10.6 us (2%)
    pallas_call x13, Pallas kernels, run_kernel(): pl.pallas_call(body, grid_spec=spec, **rest)(*first_args, *inputs, *deps)  277 us
    ppermute x22, waiting for transfers between devices, swap(): return lax.ppermute(value, self.axes, pairs)  75.3 us
    all_to_all x2, waiting for transfers between devices, reduce_line(): got = lax.all_to_all(value, 'fsdp', 0, 0)  44.6 us
    all_to_all x3, waiting for transfers between devices, gather_line(): return lax.all_to_all(spread, 'fsdp', 0, 0)  28.2 us
    ppermute x22, starting transfers between devices, swap(): return lax.ppermute(value, self.axes, pairs)  26.2 us
    convert_element_type x13, other arithmetic, add_low(): return (a.astype(f32) + b.astype(f32)).astype(bf16)  20.4 us
    unnamed x84, local copies, waits for them, and re-layouts  17 us
    all_to_all x3, starting transfers between devices, gather_line(): return lax.all_to_all(spread, 'fsdp', 0, 0)  16 us
  transfers between devices with their start and end apart: 48, of which 18 were waited for; matrix products, arithmetic and copies ran while one was open for 10% of the time, Pallas kernels for 43%

profile of v1, /device:TPU:0, one launch (start us, length us, event | category | flops | bytes accessed | tf_op | source)
XLA Modules:
  0.0 598.5 jit_solution(13625179484218504589)
XLA Ops:
  6.9 6.3 %all-to-all-start = ((bf16[4,32,4224]{2,1,0:T(8,128)(2,1)}), bf16[4,32,4224]{2,1,0:T(8,128)(2,1)S(1)}, u32[]{:S(2)}, u32[]{:S(2)}) async-start(bf16[4,32,4224]{2,1,0:T(8,128)(2,1)} %broadcast_in_dim.38), calls=%async_computation | async-start | bytes 2162688 | tf_op jit(solution)/shard_map/all_to_all | solution.py:103
  15.2 1.6 convert_bitcast_fusion
  17.9 2.1 collective-permute-done.7
  20.2 19.5 %all-to-all-done = bf16[4,32,4224]{2,1,0:T(8,128)(2,1)S(1)} async-done(((bf16[4,32,4224]{2,1,0:T(8,128)(2,1)}), bf16[4,32,4224]{2,1,0:T(8,128)(2,1)S(1)}, u32[]{:S(2)}, u32[]{:S(2)}) %all-to-all-start) | async-done | bytes 1081376 | tf_op jit(solution)/shard_map/all_to_all | solution.py:103
  42.1 1.6 broadcast_in_dim.39
  43.7 5.1 all-to-all-start.1
  49.8 1.5 collective-permute-start
  54.1 16.7 %collective-permute-done.refs_3_ = bf16[128,3200]{1,0:T(8,128)(2,1)} collective-permute-done((bf16[128,3200]{1,0:T(8,128)(2,1)}, bf16[128,3200]{1,0:T(8,128)(2,1)}, u32[]{:S(2)}, u32[]{:S(2)}) %collective-permute-start) | collective-permute-done | bytes 819232 | tf_op jit(solution)/shard_map/ppermute | solution.py:99
  70.7 1.9 collective-permute-start.2
  72.7 5.1 pack.1
  79.6 1.5 collective-permute-start.10
  81.4 6.2 %collective-permute-done.10.refs_7_ = bf16[128,1024]{1,0:T(8,128)(2,1)S(1)} collective-permute-done((bf16[128,1024]{1,0:T(8,128)(2,1)}, bf16[128,1024]{1,0:T(8,128)(2,1)S(1)}, u32[]{:S(2)}, u32[]{:S(2)}) %collective-permute-start.10) | collective-permute-done | bytes 262176 | tf_op jit(solution)/shard_map/ppermute | solution.py:99
  89.5 7.1 %all-to-all-done.1 = bf16[4,2,128,1024]{3,2,1,0:T(8,128)(2,1)} async-done(((bf16[4,2,128,1024]{3,2,1,0:T(8,128)(2,1)}), bf16[4,2,128,1024]{3,2,1,0:T(8,128)(2,1)}, u32[]{:S(2)}, u32[]{:S(2)}) %all-to-all-start.1) | async-done | bytes 2097184 | tf_op jit(solution)/shard_map/all_to_all | solution.py:103
  96.6 1.7 fusion.21
  98.8 1.6 collective-permute-start.8
  102.2 16.4 %qkv.1 = (bf16[1024,1024]{1,0:T(8,128)(2,1)}, bf16[3,1024,1024]{2,1,0:T(8,128)(2,1)}, bf16[1024,3072]{1,0:T(8,128)(2,1)}, f32[8,1024]{1,0:T(8,128)}) custom-call(s32[12]{0:T(128)} %pad_add_fusion.refs_0_, f32[1024,1024]{1,0:T(8,128)} %refs_1_.3, bf16[128,3200]{1,0:T(8,128)(2,1)} %slice.239.refs_2_, bf16[128,3200]{1,0:T(8,128)(2,1)} %collective-permute-done.refs_3_, ...), custom_call_target="tpu_custom_call" | custom-call | flops 18400000000 | bytes 1048576 | tf_op jit(solution)/shard_map/qkv/pallas_call | solution.py:72
  118.5 6.4 %collective-permute-done.8.refs_3_.refs_6_ = bf16[1024,1024]{1,0:T(8,128)(2,1)S(1)} collective-permute-done((bf16[1024,1024]{1,0:T(8,128)(2,1)S(1)}, bf16[1024,1024]{1,0:T(8,128)(2,1)S(1)}, u32[]{:S(2)}, u32[]{:S(2)}) %collective-permute-start.8) | collective-permute-done | bytes 2097184 | tf_op jit(solution)/shard_map/ppermute | solution.py:99
  126.9 1.6 broadcast_in_dim.83
  128.5 4.6 all-to-all-start.2
  133.1 1.6 collective-permute-start.18
  135.5 21.3 %attend.2 = (bf16[1024,512]{1,0:T(8,128)(2,1)S(1)}, f32[4,8,1024]{2,1,0:T(8,128)S(1)}) custom-call(s32[1024,128]{1,0:T(8,128)S(1)} %broadcast_in_dim.45.refs_0_, s32[8,1024]{1,0:T(8,128)S(1)} %broadcast_in_dim.82.refs_1_, bf16[3,1024,1024]{2,1,0:T(8,128)(2,1)} %get-tuple-element.52.refs_2_, bf16[1024,1024]{1,0:T(8,128)(2,1)S(1)} %collective-permute-done.8.refs_3_.refs_6_, ...), custom_call_target="tpu_custom_call" | custom-call | flops 24149999616 | bytes 1048576 | tf_op jit(solution)/shard_map/attend/pallas_call | solution.py:72
  157.8 21.2 %attend.3 = (bf16[1024,512]{1,0:T(8,128)(2,1)S(1)}, f32[4,8,1024]{2,1,0:T(8,128)S(1)}) custom-call(s32[1024,128]{1,0:T(8,128)S(1)} %broadcast_in_dim.45.refs_0_, s32[8,1024]{1,0:T(8,128)S(1)} %broadcast_in_dim.82.refs_1_, bf16[3,1024,1024]{2,1,0:T(8,128)(2,1)} %get-tuple-element.52.refs_2_, f32[4,8,1024]{2,1,0:T(8,128)S(1)} %get-tuple-element.54.refs_3_.refs_4_), custom_call_target="tpu_custom_call" | custom-call | flops 24149999616 | bytes 1048576 | tf_op jit(solution)/shard_map/attend/pallas_call | solution.py:72
  180.6 1.6 all-to-all-done.2
  182.2 1.7 fusion.20
  184.3 1.6 collective-permute-start.20
  185.9 13.6 %mix_out.1 = (f32[1024,1024]{1,0:T(8,128)}, bf16[1024,1024]{1,0:T(8,128)(2,1)}, bf16[640,1024]{1,0:T(8,128)(2,1)}, bf16[640,1024]{1,0:T(8,128)(2,1)}) custom-call(s32[12]{0:T(128)} %pad_add_fusion.refs_0_, s32[8,1024]{1,0:T(8,128)} %copy-done.3, f32[1024,1024]{1,0:T(8,128)} %refs_1_.3, f32[8,1024]{1,0:T(8,128)} %get-tuple-element.51.refs_3_.refs_1_.refs_0_, ...), custom_call_target="tpu_custom_call" | custom-call | flops 14949999616 | bytes 1048576 | tf_op jit(solution)/shard_map/mix_out/pallas_call | solution.py:72
  199.6 1.6 collective-permute-start.21
  201.1 16.8 %collective-permute-done.20.refs_9_.refs_10_ = bf16[1024,1024]{1,0:T(8,128)(2,1)} collective-permute-done((bf16[1024,1024]{1,0:T(8,128)(2,1)S(1)}, bf16[1024,1024]{1,0:T(8,128)(2,1)}, u32[]{:S(2)}, u32[]{:S(2)}) %collective-permute-start.20) | collective-permute-done | bytes 2097184 | tf_op jit(solution)/shard_map/ppermute | solution.py:99
  219.4 51.9 %experts.2 = (bf16[640,1024]{1,0:T(8,128)(2,1)}, bf16[640,1024]{1,0:T(8,128)(2,1)}, bf16[640,1024]{1,0:T(8,128)(2,1)}, bf16[640,1024]{1,0:T(8,128)(2,1)}, bf16[2...) custom-call(s32[12]{0:T(128)} %pad_add_fusion.refs_0_, bf16[640,1024]{1,0:T(8,128)(2,1)} %get-tuple-element.58.refs_1_, ...), custom_call_target="tpu_custom_call" | custom-call | flops 31050000384 | bytes 1048576 | tf_op jit(solution)/shard_map/experts/pallas_call | solution.py:72
  272.0 54.2 %experts.3 = (bf16[640,1024]{1,0:T(8,128)(2,1)}, bf16[640,1024]{1,0:T(8,128)(2,1)}, bf16[640,1024]{1,0:T(8,128)(2,1)}, bf16[640,1024]{1,0:T(8,128)(2,1)}, bf16[2...) custom-call(s32[12]{0:T(128)} %pad_add_fusion.refs_0_, bf16[640,1024]{1,0:T(8,128)(2,1)} %get-tuple-element.58.refs_1_, ...), custom_call_target="tpu_custom_call" | custom-call | flops 31050000384 | bytes 1048576 | tf_op jit(solution)/shard_map/experts/pallas_call | solution.py:72
  326.9 3.2 add_convert_fusion.5.refs_9_
  330.1 1.9 collective-permute-start.26
  334.0 17.6 %combine.1 = (f32[1024,1024]{1,0:T(8,128)}, f32[1024,1024]{1,0:T(8,128)}, bf16[1024,1024]{1,0:T(8,128)(2,1)}, bf16[1024,1024]{1,0:T(8,128)(2,1)}, f32[8,1024]{1,0:T(8,128)}) custom-call(s32[1024,128]{1,0:T(8,128)} %broadcast_in_dim.37.refs_0_, f32[8,1024]{1,0:T(8,128)} %get-tuple-element.51.refs_3_.refs_1_.refs_0_, f32[1024,1024]{1,0:T(8,128)} %get-tuple-element.56.refs_2_, ...), custom_call_target="tpu_custom_call" | custom-call | flops 9200000000 | bytes 1048576 | tf_op jit(solution)/shard_map/combine/pallas_call | solution.py:72
  351.7 5.6 weight_grads.3
  357.4 1.6 collective-permute-start.27
  360.5 3.7 add_convert_fusion.3
  366.0 22.2 %attend_back.2.refs_1_.refs_4_ = bf16[3,1024,512]{2,1,0:T(8,128)(2,1)} custom-call(s32[1024,128]{1,0:T(8,128)} %copy-done.1, s32[8,1024]{1,0:T(8,128)} %copy-done.2, bf16[3,1024,1024]{2,1,0:T(8,128)(2,1)} %get-tuple-element.52.refs_2_, bf16[1024,1024]{1,0:T(8,128)(2,1)} %get-tuple-element.75.refs_3_, f32[4,8,1024]{2,1,0:T(8,128)} %copy-done.15, ...), custom_call_target="tpu_custom_call" | custom-call | flops 12650000384 | bytes 1048576 | tf_op jit(solution)/shard_map/attend_back/pallas_call | solution.py:72
  388.2 8.4 %weight_grads.4 = (bf16[4,128,1536]{2,1,0:T(8,128)(2,1)S(1)}, bf16[4,128,1536]{2,1,0:T(8,128)(2,1)}) custom-call(s32[12]{0:T(128)S(1)} %copy-done.4, bf16[3,1024,512]{2,1,0:T(8,128)(2,1)} %attend_back.2.refs_1_.refs_4_, bf16[1024,1024]{1,0:T(8,128)(2,1)} %get-tuple-element.81.refs_2_, bf16[4,128,1024]{2,1,0:T(8,128)(2,1)S(1)} %add_convert_fusion.8.refs_3_), custom_call_target="tpu_custom_call" | custom-call | flops 4600000000 | bytes 1048576 | tf_op jit(solution)/shard_map/weight_grads/pallas_call | solution.py:72
  396.8 1.6 collective-permute-start.33
  398.4 13.4 %collective-permute-done.33 = bf16[2,128,1024]{2,1,0:T(8,128)(2,1)S(1)} collective-permute-done((bf16[2,128,1024]{2,1,0:T(8,128)(2,1)S(1)}, bf16[2,128,1024]{2,1,0:T(8,128)(2,1)S(1)}, u32[]{:S(2)}, u32[]{:S(2)}) %collective-permute-start.33) | collective-permute-done | bytes 524320 | tf_op jit(solution)/shard_map/ppermute | solution.py:99
  413.4 3.9 add_convert_fusion.2.refs_5_
  418.8 4.9 all-to-all-start.3
  423.7 1.8 add_convert_fusion.7
  425.6 1.6 collective-permute-start.31
  427.2 22.2 %attend_back.3.refs_1_.refs_5_ = bf16[3,1024,512]{2,1,0:T(8,128)(2,1)} custom-call(s32[1024,128]{1,0:T(8,128)} %copy-done.1, s32[8,1024]{1,0:T(8,128)} %copy-done.2, bf16[3,1024,1024]{2,1,0:T(8,128)(2,1)} %get-tuple-element.52.refs_2_, bf16[1024,1024]{1,0:T(8,128)(2,1)} %get-tuple-element.75.refs_3_, f32[4,8,1024]{2,1,0:T(8,128)} %copy-done.14, ...), custom_call_target="tpu_custom_call" | custom-call | flops 12650000384 | bytes 1048576 | tf_op jit(solution)/shard_map/attend_back/pallas_call | solution.py:72
  449.4 2.7 collective-permute-done.29
  452.1 4.3 add_convert_fusion
  459.0 5.4 collective-permute-done.32
  464.5 6.9 %all-to-all-done.3 = bf16[4,2,128,1024]{3,2,1,0:T(8,128)(2,1)} async-done(((bf16[4,2,128,1024]{3,2,1,0:T(8,128)(2,1)}), bf16[4,2,128,1024]{3,2,1,0:T(8,128)(2,1)}, u32[]{:S(2)}, u32[]{:S(2)}) %all-to-all-start.3) | async-done | bytes 2097184 | tf_op jit(solution)/shard_map/all_to_all | solution.py:131
  471.4 2.1 convert_reduce_fusion.1.refs_3_
  473.5 7.7 %weight_grads.5 = (bf16[4,128,1536]{2,1,0:T(8,128)(2,1)S(1)}, bf16[4,128,1536]{2,1,0:T(8,128)(2,1)S(1)}) custom-call(s32[12]{0:T(128)S(1)} %copy-done.4, bf16[3,1024,512]{2,1,0:T(8,128)(2,1)} %attend_back.3.refs_1_.refs_5_, bf16[1024,1024]{1,0:T(8,128)(2,1)} %get-tuple-element.81.refs_2_, f32[2,128,1024]{2,1,0:T(8,128)S(1)} %convert_reduce_fusion.1.refs_3_, ...), custom_call_target="tpu_custom_call" | custom-call | flops 4600000000 | bytes 1048576 | tf_op jit(solution)/shard_map/weight_grads/pallas_call | solution.py:72
  481.3 14.5 %token_grads.1 = (f32[1024,1024]{1,0:T(8,128)}, f32[8,1024]{1,0:T(8,128)S(1)}) custom-call(f32[8,1024]{1,0:T(8,128)S(1)} %copy-done.13, f32[1024,1024]{1,0:T(8,128)} %refs_1_.3, f32[1024,1024]{1,0:T(8,128)} %get-tuple-element.73.refs_2_, bf16[1024,3072]{1,0:T(8,128)(2,1)} %get-tuple-element.74.refs_3_, bf16[3,1024,512]{2,1,0:T(8,128)(2,1)S(1)} %copy-done.7, ...), custom_call_target="tpu_custom_call" | custom-call | flops 9200000000 | bytes 1048576 | tf_op jit(solution)/shard_map/token_grads/pallas_call | solution.py:72
  496.0 10.6 %all_to_all.30 = f32[32,1,128]{2,1,0:T(1,128)S(1)} all-to-all(f32[32,1,128]{2,1,0:T(1,128)S(1)} %reshape.241), channel_id=1, replica_groups=mesh['b0'=2,'b1'=2,'core'=2,'fsdp'=4] {'b0','b1','core','fsdp'}, dimensions={0} | all-to-all | bytes 32768 | tf_op jit(solution)/shard_map/all_to_all | solution.py:904
  506.5 4.4 all-to-all-start.5
  512.6 2.1 collective-permute-done.35
  521.8 37.7 %all-to-all-done.5 = bf16[4,2,128,1024]{3,2,1,0:T(8,128)(2,1)} async-done(((bf16[4,2,128,1024]{3,2,1,0:T(8,128)(2,1)}), bf16[4,2,128,1024]{3,2,1,0:T(8,128)(2,1)}, u32[]{:S(2)}, u32[]{:S(2)}) %all-to-all-start.5) | async-done | bytes 2097184 | tf_op jit(solution)/shard_map/all_to_all | solution.py:131
  559.5 2.1 convert_reduce_fusion
  564.3 6.4 %collective-permute-done.37 = bf16[1,128,1536]{2,1,0:T(8,128)(2,1)S(1)} collective-permute-done((bf16[1,128,1536]{2,1,0:T(8,128)(2,1)S(1)}, bf16[1,128,1536]{2,1,0:T(8,128)(2,1)S(1)}, u32[]{:S(2)}, u32[]{:S(2)}) %collective-permute-start.37) | collective-permute-done | bytes 393248 | tf_op jit(solution)/shard_map/ppermute | solution.py:99
  572.9 2.0 collective-permute-start.39
  574.9 1.8 collective-permute-start.40
  576.9 1.8 copy.101
  580.7 3.2 copy.102
  584.0 4.1 reshape.240
  588.1 6.2 %collective-permute-done.39 = bf16[32,4096]{1,0:T(8,128)(2,1)} collective-permute-done((bf16[32,4096]{1,0:T(8,128)(2,1)}, bf16[32,4096]{1,0:T(8,128)(2,1)}, u32[]{:S(2)}, u32[]{:S(2)}) %collective-permute-start.39) | collective-permute-done | bytes 262176 | tf_op jit(solution)/shard_map/ppermute | solution.py:126
  (233 shorter events, 60.3 us)
Async XLA Ops:
  3.0 10.2 %copy-start.27 = (f32[32,2,4096]{2,1,0:T(2,128)S(1)}, f32[32,2,4096]{2,1,0:T(2,128)}, u32[]{:S(2)}) copy-start(f32[32,2,4096]{2,1,0:T(2,128)} %param.25) | copy-start | bytes 3145732
  6.9 32.7 %all-to-all-start = ((bf16[4,32,4224]{2,1,0:T(8,128)(2,1)}), bf16[4,32,4224]{2,1,0:T(8,128)(2,1)S(1)}, u32[]{:S(2)}, u32[]{:S(2)}) async-start(bf16[4,32,4224]{2,1,0:T(8,128)(2,1)} %broadcast_in_dim.38), calls=%async_computation | async-start | bytes 2162688 | tf_op jit(solution)/shard_map/all_to_all | solution.py:103
  17.9 2.1 collective-permute-start.7
  20.2 23.6 %copy-start.20 = (bf16[2,2,128,1024]{3,2,1,0:T(8,128)(2,1)}, bf16[2,2,128,1024]{3,2,1,0:T(8,128)(2,1)S(1)}, u32[]{:S(2)}) copy-start(bf16[2,2,128,1024]{3,2,1,0:T(8,128)(2,1)S(1)} %maximum_select_fusion) | copy-start | bytes 3145732
  43.7 52.9 %all-to-all-start.1 = ((bf16[4,2,128,1024]{3,2,1,0:T(8,128)(2,1)}), bf16[4,2,128,1024]{3,2,1,0:T(8,128)(2,1)}, u32[]{:S(2)}, u32[]{:S(2)}) async-start(bf16[4,2,128,1024]{3,2,1,0:T(8,128)(2,1)} %broadcast_in_dim.39), calls=%async_computation.1 | async-start | bytes 4194304 | tf_op jit(solution)/shard_map/all_to_all | solution.py:103
  49.8 20.9 %collective-permute-start = (bf16[128,3200]{1,0:T(8,128)(2,1)}, bf16[128,3200]{1,0:T(8,128)(2,1)}, u32[]{:S(2)}, u32[]{:S(2)}) collective-permute-start(bf16[128,3200]{1,0:T(8,128)(2,1)} %slice.239.refs_2_), channel_id=1, source_target_pairs={{0,16},{4,12},{8,24},{12,4},{16,0},{20,28},{24,8},{28,20},{1,17},{... | collective-permute-start | bytes 2457608 | tf_op jit(solution)/shard_map/ppermute | solution.py:99
  52.6 36.4 %collective-permute-start.1 = (bf16[128,3200]{1,0:T(8,128)(2,1)}, bf16[128,3200]{1,0:T(8,128)(2,1)}, u32[]{:S(2)}, u32[]{:S(2)}) collective-permute-start(bf16[128,3200]{1,0:T(8,128)(2,1)} %slice.239.refs_2_), channel_id=1, source_target_pairs={{0,8},{4,20},{8,0},{12,28},{16,24},{20,4},{24,16},{28,12},{1,9},{5... | collective-permute-start | bytes 2457608 | tf_op jit(solution)/shard_map/ppermute | solution.py:99
  70.7 18.7 %collective-permute-start.2 = (bf16[128,3200]{1,0:T(8,128)(2,1)}, bf16[128,3200]{1,0:T(8,128)(2,1)}, u32[]{:S(2)}, u32[]{:S(2)}) collective-permute-start(bf16[128,3200]{1,0:T(8,128)(2,1)} %collective-permute-done.refs_3_), channel_id=1, source_target_pairs={{0,8},{4,20},{8,0},{12,28},{16,24},{20,4},{24,16},{28,12},{1,9},{5... | collective-permute-start | bytes 2457608 | tf_op jit(solution)/shard_map/ppermute | solution.py:99
  72.6 8.6 %copy-start.37 = (s32[1,8]{1,0:T(1,128)S(1)}, s32[1,8]{1,0:T(1,128)}, u32[]{:S(2)}) copy-start(s32[1,8]{1,0:T(1,128)} %param.27) | copy-start | bytes 100
  79.6 8.0 %collective-permute-start.10 = (bf16[128,1024]{1,0:T(8,128)(2,1)}, bf16[128,1024]{1,0:T(8,128)(2,1)S(1)}, u32[]{:S(2)}, u32[]{:S(2)}) collective-permute-start(bf16[128,1024]{1,0:T(8,128)(2,1)} %slice.244.refs_6_), channel_id=1, source_target_pairs={{0,16},{4,12},{8,24},{12,4},{16,0},{20,28},{24,8},{28,20},{1,17},{... | collective-permute-start | bytes 786440 | tf_op jit(solution)/shard_map/ppermute | solution.py:99
  81.1 7.8 %collective-permute-start.12 = (bf16[128,1024]{1,0:T(8,128)(2,1)}, bf16[128,1024]{1,0:T(8,128)(2,1)S(1)}, u32[]{:S(2)}, u32[]{:S(2)}) collective-permute-start(bf16[128,1024]{1,0:T(8,128)(2,1)} %slice.244.refs_6_), channel_id=1, source_target_pairs={{0,8},{4,20},{8,0},{12,28},{16,24},{20,4},{24,16},{28,12},{1,9},{5... | collective-permute-start | bytes 786440 | tf_op jit(solution)/shard_map/ppermute | solution.py:99
  81.4 19.7 %collective-permute-start.3 = (bf16[128,3200]{1,0:T(8,128)(2,1)}, bf16[128,3200]{1,0:T(8,128)(2,1)}, u32[]{:S(2)}, u32[]{:S(2)}) collective-permute-start(bf16[128,3200]{1,0:T(8,128)(2,1)} %slice.239.refs_2_), channel_id=1, source_target_pairs={{0,4},{4,0},{1,5},{5,1},{2,6},{6,2},{3,7},{7,3},{8,12},{12,8},{9,1... | collective-permute-start | bytes 2457608 | tf_op jit(solution)/shard_map/ppermute | solution.py:76
  87.6 11.2 %copy-start.35 = (bf16[128,1024]{1,0:T(8,128)(2,1)}, bf16[128,1024]{1,0:T(8,128)(2,1)S(1)}, u32[]{:S(2)}) copy-start(bf16[128,1024]{1,0:T(8,128)(2,1)S(1)} %collective-permute-done.10.refs_7_) | copy-start | bytes 786436
  87.6 11.2 %collective-permute-start.14 = (bf16[128,1024]{1,0:T(8,128)(2,1)S(1)}, bf16[128,1024]{1,0:T(8,128)(2,1)}, u32[]{:S(2)}, u32[]{:S(2)}) collective-permute-start(bf16[128,1024]{1,0:T(8,128)(2,1)S(1)} %collective-permute-done.10.refs_7_), channel_id=1, source_target_pairs={{0,8},{4,20},{8,0},{12,28},{16,24},{20,4},{24,16},{28,12},{1,9},{5... | collective-permute-start | bytes 786440 | tf_op jit(solution)/shard_map/ppermute | solution.py:99
  88.9 9.8 %copy-start.36 = (bf16[128,1024]{1,0:T(8,128)(2,1)}, bf16[128,1024]{1,0:T(8,128)(2,1)S(1)}, u32[]{:S(2)}) copy-start(bf16[128,1024]{1,0:T(8,128)(2,1)S(1)} %collective-permute-done.12.refs_8_) | copy-start | bytes 786436
  88.9 12.2 %collective-permute-start.4 = (bf16[128,3200]{1,0:T(8,128)(2,1)}, bf16[128,3200]{1,0:T(8,128)(2,1)}, u32[]{:S(2)}, u32[]{:S(2)}) collective-permute-start(bf16[128,3200]{1,0:T(8,128)(2,1)} %collective-permute-done.refs_3_), channel_id=1, source_target_pairs={{0,4},{4,0},{1,5},{5,1},{2,6},{6,2},{3,7},{7,3},{8,12},{12,8},{9,1... | collective-permute-start | bytes 2457608 | tf_op jit(solution)/shard_map/ppermute | solution.py:76
  88.9 12.7 %collective-permute-start.5 = (bf16[128,3200]{1,0:T(8,128)(2,1)}, bf16[128,3200]{1,0:T(8,128)(2,1)}, u32[]{:S(2)}, u32[]{:S(2)}) collective-permute-start(bf16[128,3200]{1,0:T(8,128)(2,1)} %collective-permute-done.1.refs_4_), channel_id=1, source_target_pairs={{0,4},{4,0},{1,5},{5,1},{2,6},{6,2},{3,7},{7,3},{8,12},{12,8},{9,1... | collective-permute-start | bytes 2457608 | tf_op jit(solution)/shard_map/ppermute | solution.py:76
  89.4 12.3 %collective-permute-start.6 = (bf16[128,3200]{1,0:T(8,128)(2,1)}, bf16[128,3200]{1,0:T(8,128)(2,1)}, u32[]{:S(2)}, u32[]{:S(2)}) collective-permute-start(bf16[128,3200]{1,0:T(8,128)(2,1)} %collective-permute-done.2.refs_5_), channel_id=1, source_target_pairs={{0,4},{4,0},{1,5},{5,1},{2,6},{6,2},{3,7},{7,3},{8,12},{12,8},{9,1... | collective-permute-start | bytes 2457608 | tf_op jit(solution)/shard_map/ppermute | solution.py:76
  98.8 26.1 %collective-permute-start.8 = (bf16[1024,1024]{1,0:T(8,128)(2,1)S(1)}, bf16[1024,1024]{1,0:T(8,128)(2,1)S(1)}, u32[]{:S(2)}, u32[]{:S(2)}) collective-permute-start(bf16[1024,1024]{1,0:T(8,128)(2,1)S(1)} %pad_maximum_fusion.refs_10_.refs_5_), channel_id=1, source_target_pairs={{0,16},{4,12},{8,24},{12,4},{16,0},{20,28},{24,8},{28,20},{1,17},{... | collective-permute-start | bytes 6291464 | tf_op jit(solution)/shard_map/ppermute | solution.py:99
  101.1 32.1 %collective-permute-start.9 = (bf16[128,1024]{1,0:T(8,128)(2,1)}, bf16[128,1024]{1,0:T(8,128)(2,1)}, u32[]{:S(2)}, u32[]{:S(2)}) collective-permute-start(bf16[128,1024]{1,0:T(8,128)(2,1)} %slice.244.refs_6_), channel_id=1, source_target_pairs={{0,4},{4,0},{1,5},{5,1},{2,6},{6,2},{3,7},{7,3},{8,12},{12,8},{9,1... | collective-permute-start | bytes 786440 | tf_op jit(solution)/shard_map/ppermute | solution.py:76
  101.2 33.5 %collective-permute-start.11 = (bf16[128,1024]{1,0:T(8,128)(2,1)}, bf16[128,1024]{1,0:T(8,128)(2,1)}, u32[]{:S(2)}, u32[]{:S(2)}) collective-permute-start(bf16[128,1024]{1,0:T(8,128)(2,1)} %copy-done.35), channel_id=1, source_target_pairs={{0,4},{4,0},{1,5},{5,1},{2,6},{6,2},{3,7},{7,3},{8,12},{12,8},{9,1... | collective-permute-start | bytes 786440 | tf_op jit(solution)/shard_map/ppermute | solution.py:76
  101.6 33.6 %collective-permute-start.13 = (bf16[128,1024]{1,0:T(8,128)(2,1)}, bf16[128,1024]{1,0:T(8,128)(2,1)}, u32[]{:S(2)}, u32[]{:S(2)}) collective-permute-start(bf16[128,1024]{1,0:T(8,128)(2,1)} %copy-done.36), channel_id=1, source_target_pairs={{0,4},{4,0},{1,5},{5,1},{2,6},{6,2},{3,7},{7,3},{8,12},{12,8},{9,1... | collective-permute-start | bytes 786440 | tf_op jit(solution)/shard_map/ppermute | solution.py:76
  101.7 33.5 %collective-permute-start.15 = (bf16[128,1024]{1,0:T(8,128)(2,1)}, bf16[128,1024]{1,0:T(8,128)(2,1)}, u32[]{:S(2)}, u32[]{:S(2)}) collective-permute-start(bf16[128,1024]{1,0:T(8,128)(2,1)} %collective-permute-done.14.refs_9_), channel_id=1, source_target_pairs={{0,4},{4,0},{1,5},{5,1},{2,6},{6,2},{3,7},{7,3},{8,12},{12,8},{9,1... | collective-permute-start | bytes 786440 | tf_op jit(solution)/shard_map/ppermute | solution.py:76
  124.9 10.6 %copy-start = (bf16[1024,1024]{1,0:T(8,128)(2,1)}, bf16[1024,1024]{1,0:T(8,128)(2,1)S(1)}, u32[]{:S(2)}) copy-start(bf16[1024,1024]{1,0:T(8,128)(2,1)S(1)} %collective-permute-done.8.refs_3_.refs_6_) | copy-start | bytes 6291460
  124.9 74.7 %collective-permute-start.17 = (bf16[640,1024]{1,0:T(8,128)(2,1)S(1)}, bf16[640,1024]{1,0:T(8,128)(2,1)}, u32[]{:S(2)}, u32[]{:S(2)}) collective-permute-start(bf16[640,1024]{1,0:T(8,128)(2,1)S(1)} %get-tuple-element.61), channel_id=1, source_target_pairs={{0,4},{4,0},{1,5},{5,1},{2,6},{6,2},{3,7},{7,3},{8,12},{12,8},{9,1... | collective-permute-start | bytes 3932168 | tf_op jit(solution)/shard_map/ppermute | solution.py:76
  128.5 53.7 %all-to-all-start.2 = ((bf16[4,2,128,1024]{3,2,1,0:T(8,128)(2,1)}), bf16[4,2,128,1024]{3,2,1,0:T(8,128)(2,1)}, u32[]{:S(2)}, u32[]{:S(2)}) async-start(bf16[4,2,128,1024]{3,2,1,0:T(8,128)(2,1)} %broadcast_in_dim.83), calls=%async_computation.2 | async-start | bytes 4194304 | tf_op jit(solution)/shard_map/all_to_all | solution.py:103
  133.1 86.3 %collective-permute-start.18 = (bf16[1024,1024]{1,0:T(8,128)(2,1)}, bf16[1024,1024]{1,0:T(8,128)(2,1)}, u32[]{:S(2)}, u32[]{:S(2)}) collective-permute-start(bf16[1024,1024]{1,0:T(8,128)(2,1)} %copy-done.24), channel_id=1, source_target_pairs={{0,8},{4,20},{8,0},{12,28},{16,24},{20,4},{24,16},{28,12},{1,9},{5... | collective-permute-start | bytes 6291464 | tf_op jit(solution)/shard_map/ppermute | solution.py:99
  134.7 84.7 %collective-permute-start.19 = (bf16[1024,1024]{1,0:T(8,128)(2,1)S(1)}, bf16[1024,1024]{1,0:T(8,128)(2,1)}, u32[]{:S(2)}, u32[]{:S(2)}) collective-permute-start(bf16[1024,1024]{1,0:T(8,128)(2,1)S(1)} %collective-permute-done.8.refs_3_.refs_6_), channel_id=1, source_target_pairs={{0,8},{4,20},{8,0},{12,28},{16,24},{20,4},{24,16},{28,12},{1,9},{5... | collective-permute-start | bytes 6291464 | tf_op jit(solution)/shard_map/ppermute | solution.py:99
  135.4 22.3 %copy-start.1 = (s32[1024,128]{1,0:T(8,128)}, s32[1024,128]{1,0:T(8,128)S(1)}, u32[]{:S(2)}) copy-start(s32[1024,128]{1,0:T(8,128)S(1)} %broadcast_in_dim.45.refs_0_) | copy-start | bytes 1572868
  135.5 22.3 %copy-start.2 = (s32[8,1024]{1,0:T(8,128)}, s32[8,1024]{1,0:T(8,128)S(1)}, u32[]{:S(2)}) copy-start(s32[8,1024]{1,0:T(8,128)S(1)} %broadcast_in_dim.82.refs_1_) | copy-start | bytes 98308
  157.7 21.2 %copy-start.15 = (f32[4,8,1024]{2,1,0:T(8,128)}, f32[4,8,1024]{2,1,0:T(8,128)S(1)}, u32[]{:S(2)}) copy-start(f32[4,8,1024]{2,1,0:T(8,128)S(1)} %get-tuple-element.54.refs_3_.refs_4_) | copy-start | bytes 393220
  184.3 33.6 %collective-permute-start.20 = (bf16[1024,1024]{1,0:T(8,128)(2,1)S(1)}, bf16[1024,1024]{1,0:T(8,128)(2,1)}, u32[]{:S(2)}, u32[]{:S(2)}) collective-permute-start(bf16[1024,1024]{1,0:T(8,128)(2,1)S(1)} %pad_maximum_fusion.1.refs_14_.refs_9_), channel_id=1, source_target_pairs={{0,16},{4,12},{8,24},{12,4},{16,0},{20,28},{24,8},{28,20},{1,17},{... | collective-permute-start | bytes 6291464 | tf_op jit(solution)/shard_map/ppermute | solution.py:99
  199.5 19.9 %collective-permute-start.16 = (bf16[640,1024]{1,0:T(8,128)(2,1)}, bf16[640,1024]{1,0:T(8,128)(2,1)}, u32[]{:S(2)}, u32[]{:S(2)}) collective-permute-start(bf16[640,1024]{1,0:T(8,128)(2,1)} %get-tuple-element.59), channel_id=1, source_target_pairs={{0,4},{4,0},{1,5},{5,1},{2,6},{6,2},{3,7},{7,3},{8,12},{12,8},{9,1... | collective-permute-start | bytes 3932168 | tf_op jit(solution)/shard_map/ppermute | solution.py:76
  199.6 72.4 %collective-permute-start.21 = (bf16[1024,1024]{1,0:T(8,128)(2,1)}, bf16[1024,1024]{1,0:T(8,128)(2,1)}, u32[]{:S(2)}, u32[]{:S(2)}) collective-permute-start(bf16[1024,1024]{1,0:T(8,128)(2,1)} %copy-done.25), channel_id=1, source_target_pairs={{0,8},{4,20},{8,0},{12,28},{16,24},{20,4},{24,16},{28,12},{1,9},{5... | collective-permute-start | bytes 6291464 | tf_op jit(solution)/shard_map/ppermute | solution.py:99
  217.9 54.1 %collective-permute-start.22 = (bf16[1024,1024]{1,0:T(8,128)(2,1)}, bf16[1024,1024]{1,0:T(8,128)(2,1)}, u32[]{:S(2)}, u32[]{:S(2)}) collective-permute-start(bf16[1024,1024]{1,0:T(8,128)(2,1)} %collective-permute-done.20.refs_9_.refs_10_), channel_id=1, source_target_pairs={{0,8},{4,20},{8,0},{12,28},{16,24},{20,4},{24,16},{28,12},{1,9},{5... | collective-permute-start | bytes 6291464 | tf_op jit(solution)/shard_map/ppermute | solution.py:99
  271.3 55.6 %collective-permute-start.25 = (bf16[2,1024,1024]{2,1,0:T(8,128)(2,1)}, bf16[2,1024,1024]{2,1,0:T(8,128)(2,1)}, u32[]{:S(2)}, u32[]{:S(2)}) collective-permute-start(bf16[2,1024,1024]{2,1,0:T(8,128)(2,1)} %get-tuple-element.71), channel_id=1, source_target_pairs={{0,8},{4,20},{8,0},{12,28},{16,24},{20,4},{24,16},{28,12},{1,9},{5... | collective-permute-start | bytes 12582920 | tf_op jit(solution)/shard_map/ppermute | solution.py:99
  326.3 5.6 collective-permute-start.23
  326.4 5.6 collective-permute-start.24
  330.1 30.4 %collective-permute-start.26 = (bf16[1,1024,1024]{2,1,0:T(8,128)(2,1)S(1)}, bf16[1,1024,1024]{2,1,0:T(8,128)(2,1)}, u32[]{:S(2)}, u32[]{:S(2)}) collective-permute-start(bf16[1,1024,1024]{2,1,0:T(8,128)(2,1)S(1)} %add_convert_fusion.5.refs_9_), channel_id=1, source_target_pairs={{0,16},{4,12},{8,24},{12,4},{16,0},{20,28},{24,8},{28,20},{1,17},{... | collective-permute-start | bytes 6291464 | tf_op jit(solution)/shard_map/ppermute | solution.py:99
  334.0 17.6 %copy-start.4 = (s32[12]{0:T(128)S(1)}, s32[12]{0:T(128)}, u32[]{:S(2)}) copy-start(s32[12]{0:T(128)} %pad_add_fusion.refs_0_) | copy-start | bytes 148
  334.0 17.6 %copy-start.9 = (bf16[1024,512]{1,0:T(8,128)(2,1)S(1)}, bf16[1024,512]{1,0:T(8,128)(2,1)}, u32[]{:S(2)}) copy-start(bf16[1024,512]{1,0:T(8,128)(2,1)} %copy-done.8) | copy-start | bytes 3145732
  334.0 17.6 %copy-start.11 = (bf16[1024,512]{1,0:T(8,128)(2,1)S(1)}, bf16[1024,512]{1,0:T(8,128)(2,1)}, u32[]{:S(2)}) copy-start(bf16[1024,512]{1,0:T(8,128)(2,1)} %copy-done.10) | copy-start | bytes 3145732
  351.7 8.8 %copy-start.19 = (bf16[2,1024,1024]{2,1,0:T(8,128)(2,1)S(1)}, bf16[2,1024,1024]{2,1,0:T(8,128)(2,1)}, u32[]{:S(2)}) copy-start(bf16[2,1024,1024]{2,1,0:T(8,128)(2,1)} %get-tuple-element.70) | copy-start | bytes 12582916
  357.3 2.7 collective-permute-start.28
  357.4 56.0 %collective-permute-start.27 = (bf16[2,1024,1024]{2,1,0:T(8,128)(2,1)}, bf16[2,1024,1024]{2,1,0:T(8,128)(2,1)}, u32[]{:S(2)}, u32[]{:S(2)}) collective-permute-start(bf16[2,1024,1024]{2,1,0:T(8,128)(2,1)} %get-tuple-element.80), channel_id=1, source_target_pairs={{0,8},{4,20},{8,0},{12,28},{16,24},{20,4},{24,16},{28,12},{1,9},{5... | collective-permute-start | bytes 12582920 | tf_op jit(solution)/shard_map/ppermute | solution.py:99
  388.2 25.2 %copy-start.18 = (bf16[2,1024,1024]{2,1,0:T(8,128)(2,1)S(1)}, bf16[2,1024,1024]{2,1,0:T(8,128)(2,1)}, u32[]{:S(2)}) copy-start(bf16[2,1024,1024]{2,1,0:T(8,128)(2,1)} %get-tuple-element.79) | copy-start | bytes 12582916
  396.6 27.1 %collective-permute-start.30 = (bf16[4,128,1536]{2,1,0:T(8,128)(2,1)}, bf16[4,128,1536]{2,1,0:T(8,128)(2,1)}, u32[]{:S(2)}, u32[]{:S(2)}) collective-permute-start(bf16[4,128,1536]{2,1,0:T(8,128)(2,1)} %get-tuple-element.83.refs_6_), channel_id=1, source_target_pairs={{0,4},{4,0},{1,5},{5,1},{2,6},{6,2},{3,7},{7,3},{8,12},{12,8},{9,1... | collective-permute-start | bytes 4718600 | tf_op jit(solution)/shard_map/ppermute | solution.py:76
  396.8 15.0 %collective-permute-start.33 = (bf16[2,128,1024]{2,1,0:T(8,128)(2,1)S(1)}, bf16[2,128,1024]{2,1,0:T(8,128)(2,1)S(1)}, u32[]{:S(2)}, u32[]{:S(2)}) collective-permute-start(bf16[2,128,1024]{2,1,0:T(8,128)(2,1)S(1)} %slice.263), channel_id=1, source_target_pairs={{0,8},{4,20},{8,0},{12,28},{16,24},{20,4},{24,16},{28,12},{1,9},{5... | collective-permute-start | bytes 1572872 | tf_op jit(solution)/shard_map/ppermute | solution.py:99
  411.9 6.8 %collective-permute-start.34 = (bf16[1,128,1024]{2,1,0:T(8,128)(2,1)S(1)}, bf16[1,128,1024]{2,1,0:T(8,128)(2,1)S(1)}, u32[]{:S(2)}, u32[]{:S(2)}) collective-permute-start(bf16[1,128,1024]{2,1,0:T(8,128)(2,1)S(1)} %add_convert_fusion.16), channel_id=1, source_target_pairs={{0,16},{4,12},{8,24},{12,4},{16,0},{20,28},{24,8},{28,20},{1,17},{... | collective-permute-start | bytes 786440 | tf_op jit(solution)/shard_map/ppermute | solution.py:99
  417.3 34.8 %collective-permute-start.29 = (bf16[1,1024,1024]{2,1,0:T(8,128)(2,1)}, bf16[1,1024,1024]{2,1,0:T(8,128)(2,1)}, u32[]{:S(2)}, u32[]{:S(2)}) collective-permute-start(bf16[1,1024,1024]{2,1,0:T(8,128)(2,1)} %add_convert_fusion.2.refs_5_), channel_id=1, source_target_pairs={{0,16},{4,12},{8,24},{12,4},{16,0},{20,28},{24,8},{28,20},{1,17},{... | collective-permute-start | bytes 6291464 | tf_op jit(solution)/shard_map/ppermute | solution.py:99
  418.8 52.6 %all-to-all-start.3 = ((bf16[4,2,128,1024]{3,2,1,0:T(8,128)(2,1)}), bf16[4,2,128,1024]{3,2,1,0:T(8,128)(2,1)}, u32[]{:S(2)}, u32[]{:S(2)}) async-start(bf16[4,2,128,1024]{3,2,1,0:T(8,128)(2,1)} %pad_maximum_fusion.2.refs_5_), calls=%async_computation.3 | async-start | bytes 4194304 | tf_op jit(solution)/shard_map/all_to_all | solution.py:131
  425.6 30.9 %collective-permute-start.31 = (bf16[2,128,1536]{2,1,0:T(8,128)(2,1)S(1)}, bf16[2,128,1536]{2,1,0:T(8,128)(2,1)S(1)}, u32[]{:S(2)}, u32[]{:S(2)}) collective-permute-start(bf16[2,128,1536]{2,1,0:T(8,128)(2,1)S(1)} %slice.258), channel_id=1, source_target_pairs={{0,8},{4,20},{8,0},{12,28},{16,24},{20,4},{24,16},{28,12},{1,9},{5... | collective-permute-start | bytes 2359304 | tf_op jit(solution)/shard_map/ppermute | solution.py:99
  456.6 7.8 %collective-permute-start.32 = (bf16[1,128,1536]{2,1,0:T(8,128)(2,1)S(1)}, bf16[1,128,1536]{2,1,0:T(8,128)(2,1)S(1)}, u32[]{:S(2)}, u32[]{:S(2)}) collective-permute-start(bf16[1,128,1536]{2,1,0:T(8,128)(2,1)S(1)} %add_convert_fusion.13), channel_id=1, source_target_pairs={{0,16},{4,12},{8,24},{12,4},{16,0},{20,28},{24,8},{28,20},{1,17},{... | collective-permute-start | bytes 1179656 | tf_op jit(solution)/shard_map/ppermute | solution.py:99
  481.2 14.5 %copy-start.5 = (bf16[4,128,1536]{2,1,0:T(8,128)(2,1)}, bf16[4,128,1536]{2,1,0:T(8,128)(2,1)S(1)}, u32[]{:S(2)}) copy-start(bf16[4,128,1536]{2,1,0:T(8,128)(2,1)S(1)} %get-tuple-element.84.refs_6_) | copy-start | bytes 4718596
  506.5 52.9 %all-to-all-start.5 = ((bf16[4,2,128,1024]{3,2,1,0:T(8,128)(2,1)}), bf16[4,2,128,1024]{3,2,1,0:T(8,128)(2,1)}, u32[]{:S(2)}, u32[]{:S(2)}) async-start(bf16[4,2,128,1024]{3,2,1,0:T(8,128)(2,1)} %pad_maximum_fusion.3.refs_4_), calls=%async_computation.5 | async-start | bytes 4194304 | tf_op jit(solution)/shard_map/all_to_all | solution.py:131
  511.0 3.7 collective-permute-start.35
  512.1 7.5 %collective-permute-start.41 = (f32[128,1024]{1,0:T(8,128)}, f32[128,1024]{1,0:T(8,128)S(1)}, u32[]{:S(2)}, u32[]{:S(2)}) collective-permute-start(f32[128,1024]{1,0:T(8,128)} %get-tuple-element.153), channel_id=1, source_target_pairs={{0,4},{4,0},{1,5},{5,1},{2,6},{6,2},{3,7},{7,3},{8,12},{12,8},{9,1... | collective-permute-start | bytes 1572872 | tf_op jit(solution)/shard_map/ppermute | solution.py:76
  517.2 44.6 %collective-permute-start.36 = (bf16[2,128,1536]{2,1,0:T(8,128)(2,1)}, bf16[2,128,1536]{2,1,0:T(8,128)(2,1)}, u32[]{:S(2)}, u32[]{:S(2)}) collective-permute-start(bf16[2,128,1536]{2,1,0:T(8,128)(2,1)} %slice.268), channel_id=1, source_target_pairs={{0,8},{4,20},{8,0},{12,28},{16,24},{20,4},{24,16},{28,12},{1,9},{5... | collective-permute-start | bytes 2359304 | tf_op jit(solution)/shard_map/ppermute | solution.py:99
  521.7 40.0 %copy-start.17 = (bf16[4,128,1536]{2,1,0:T(8,128)(2,1)S(1)}, bf16[4,128,1536]{2,1,0:T(8,128)(2,1)}, u32[]{:S(2)}) copy-start(bf16[4,128,1536]{2,1,0:T(8,128)(2,1)} %copy-done.16) | copy-start | bytes 4718596
  561.7 2.3 collective-permute-start.42
  562.9 7.8 %collective-permute-start.37 = (bf16[1,128,1536]{2,1,0:T(8,128)(2,1)S(1)}, bf16[1,128,1536]{2,1,0:T(8,128)(2,1)S(1)}, u32[]{:S(2)}, u32[]{:S(2)}) collective-permute-start(bf16[1,128,1536]{2,1,0:T(8,128)(2,1)S(1)} %add_convert_fusion.10), channel_id=1, source_target_pairs={{0,16},{4,12},{8,24},{12,4},{16,0},{20,28},{24,8},{28,20},{1,17},{... | collective-permute-start | bytes 1179656 | tf_op jit(solution)/shard_map/ppermute | solution.py:99
  572.9 15.2 %collective-permute-start.38 = (bf16[32,4096]{1,0:T(8,128)(2,1)}, bf16[32,4096]{1,0:T(8,128)(2,1)}, u32[]{:S(2)}, u32[]{:S(2)}) collective-permute-start(bf16[32,4096]{1,0:T(8,128)(2,1)} %get-tuple-element.156), channel_id=1, source_target_pairs={{0,1},{1,2},{2,3},{3,0},{4,5},{5,6},{6,7},{7,4},{8,9},{9,10},{10,1... | collective-permute-start | bytes 786440 | tf_op jit(solution)/shard_map/ppermute | solution.py:126
  572.9 21.4 %collective-permute-start.39 = (bf16[32,4096]{1,0:T(8,128)(2,1)}, bf16[32,4096]{1,0:T(8,128)(2,1)}, u32[]{:S(2)}, u32[]{:S(2)}) collective-permute-start(bf16[32,4096]{1,0:T(8,128)(2,1)} %get-tuple-element.158), channel_id=1, source_target_pairs={{0,2},{1,3},{2,0},{3,1},{4,6},{5,7},{6,4},{7,5},{8,10},{9,11},{10,... | collective-permute-start | bytes 786440 | tf_op jit(solution)/shard_map/ppermute | solution.py:126
  574.9 19.4 %collective-permute-start.40 = (bf16[32,4096]{1,0:T(8,128)(2,1)S(1)}, bf16[32,4096]{1,0:T(8,128)(2,1)}, u32[]{:S(2)}, u32[]{:S(2)}) collective-permute-start(bf16[32,4096]{1,0:T(8,128)(2,1)S(1)} %get-tuple-element.157), channel_id=1, source_target_pairs={{0,3},{1,0},{2,1},{3,2},{4,7},{5,4},{6,5},{7,6},{8,11},{9,8},{10,9... | collective-permute-start | bytes 786440 | tf_op jit(solution)/shard_map/ppermute | solution.py:126
  (22 other events, 81.2 us)

commit v2 on v1

--- a/solution.py
+++ b/solution.py
@@ -12,7 +12,6 @@
 HEADS = 16
 HEAD_DIM = 64
 CAP = 640
-CHUNKS = 2
 PARTS = 2
 MIB = 1 << 20
 
@@ -53,23 +52,36 @@
     return pl.BlockSpec(shape, lambda *_: zeros, pipeline_mode=pl.Buffered(buffers))
 
 
-def run_kernel(kernel, *, in_specs, inputs, deps=(), prefetch=None, grid=(), out_specs, scratch_shapes=(), **rest):
-    start = len(inputs) + (prefetch is not None)
-    deps = list(deps)
+def run_kernel(
+    kernel, *, in_specs, inputs, out_specs, out_shape, deps=(), through=(), prefetch=None, grid=(), scratch_shapes=(), **rest
+):
+    first_args = [] if prefetch is None else [prefetch]
+    deps, through = list(deps), list(through)
+    out_specs = list(out_specs) if isinstance(out_specs, (list, tuple)) else [out_specs]
+    out_shape = list(out_shape) if isinstance(out_shape, (list, tuple)) else [out_shape]
+    a = len(first_args) + len(inputs)
+    b = a + len(deps) + len(through)
+    c = b + len(out_shape)
 
     def body(*refs):
-        kernel(*refs[:start], *refs[start + len(deps) :])
-
-    in_specs = list(in_specs) + [pl.BlockSpec(memory_space=pl.ANY)] * len(deps)
+        kernel(*refs[:a], *refs[b:c], *refs[c + len(through) :])
+
+    far = pl.BlockSpec(memory_space=pl.ANY)
     spec = pltpu.PrefetchScalarGridSpec(
-        num_scalar_prefetch=int(prefetch is not None),
+        num_scalar_prefetch=len(first_args),
         grid=grid,
-        in_specs=in_specs,
-        out_specs=out_specs,
+        in_specs=list(in_specs) + [far] * (b - a),
+        out_specs=out_specs + [far] * len(through),
         scratch_shapes=list(scratch_shapes),
     )
-    first_args = [] if prefetch is None else [prefetch]
-    return pl.pallas_call(body, grid_spec=spec, **rest)(*first_args, *inputs, *deps)
+    made = pl.pallas_call(
+        body,
+        grid_spec=spec,
+        out_shape=out_shape + [jax.ShapeDtypeStruct(t.shape, t.dtype) for t in through],
+        input_output_aliases={a + len(deps) + i: len(out_shape) + i for i in range(len(through))},
+        **rest,
+    )(*first_args, *inputs, *deps, *through)
+    return made if len(made) > 1 else made[0]
 
 
 def swap(value, axis):
@@ -108,8 +120,8 @@
             pieces = pieces + [self.swap(p, t) for p in pieces]
         return pieces
 
-    def reduce_chips(self, keep, send):
-        for t in reversed(range(self.bits)):
+    def reduce_chips(self, keep, send, steps):
+        for t in reversed(range(steps)):
             got = self.swap(send, t)
             if t > 0:
                 half = keep.shape[0] // 2
@@ -163,8 +175,8 @@
     @pl.when(pl.program_id(0) == 0)
     def _():
         def store(at, piece):
-            w_ref[pl.ds(at, rows), :] = piece[:, : 3 * width]
-            norms[pl.ds(at, rows), :] = piece[:, 3 * width :].astype(f32)
+            w_ref[pl.ds(at, rows), :] = piece[:, width : 4 * width]
+            norms[pl.ds(at, rows), :] = piece[:, 4 * width :].astype(f32)
 
         load_rows(ids, pieces, rows, store)
         g_ref[...] = jnp.transpose(norms[...])[:8]
@@ -337,7 +349,7 @@
             pltpu.VMEM((n, 128), f32),
         ],
         compiler_params=params(56),
-        cost_estimate=cost(11),
+        cost_estimate=cost(22),
         name="attend_back",
     )
 
@@ -362,7 +374,7 @@
         out_specs=[whole((CAP, d))] * 2,
         out_shape=[jax.ShapeDtypeStruct((CAP, d), bf16)] * 2,
         compiler_params=pltpu.CompilerParams(vmem_limit_bytes=48 * MIB),
-        cost_estimate=cost(5),
+        cost_estimate=cost(0.1),
         name="pack",
     )(slot_row, values)
 
@@ -397,7 +409,7 @@
 
 def second(ids, slot_row, mixed, tokens, gains, pieces, deps):
     n, d = tokens.shape
-    rows, _ = pieces[0].shape
+    rows = pieces[0].shape[0]
     tile = 256
     return run_kernel(
         functools.partial(
@@ -430,24 +442,23 @@
             jax.ShapeDtypeStruct((CAP, d), bf16),
         ],
         compiler_params=params(56),
-        cost_estimate=cost(13),
+        cost_estimate=cost(1),
         name="mix_out",
     )
 
 
 def expert_kernel(ids, *refs, count, rows, tile, first_chunk, block):
-    half = count // 2
     xs, ys = refs[0:2], refs[2:4]
     pos = 4
     prior = None
     if not first_chunk:
-        prior = refs[pos : pos + 4]
-        pos += 4
+        prior = refs[pos : pos + 2]
+        pos += 2
     pieces = refs[pos : pos + count]
     pos += count
-    y_out, h_out = refs[pos : pos + 2], refs[pos + 2 : pos + 4]
-    keep, send = refs[pos + 4 : pos + 6]
-    x_s, dy_s, win_s, wout_s, y_acc, h_acc, a_s, du_s, sems = refs[pos + 6 :]
+    near, far, keep, send = refs[pos : pos + 4]
+    x_s, dy_s, win_s, wout_s, y_acc, h_acc, a_s, du_s, sems = refs[pos + 4 :]
+    half = count // 2
     step = pl.program_id(0)
     d = x_s.shape[1]
     slabs = win_s.shape[1] // d
@@ -482,8 +493,8 @@
         else:
             for side in range(2):
                 span = slice(side * CAP, (side + 1) * CAP)
-                y_acc[span, :] = prior[side][...].astype(f32)
-                h_acc[span, :] = prior[2 + side][...].astype(f32)
+                y_acc[span, :] = prior[side][0].astype(f32)
+                h_acc[span, :] = prior[side][1].astype(f32)
         for copy in copies:
             copy.wait()
 
@@ -508,45 +519,38 @@
     lax.fori_loop(0, total // block, one_block, 0)
     grad = tn_dot(a_s[...], dy_s[...]).astype(bf16)
 
-    @pl.when(step < half)
-    def _():
-        keep[step, slabs * rows :, :] = grad
-
-    @pl.when(step >= half)
-    def _():
-        send[step - half, slabs * rows :, :] = grad
+    for i in range(count):
+
+        @pl.when(step == i)
+        def _():
+            (keep if i < half else send)[i % half, slabs * rows :, :] = grad
 
     slab = at // d
     row = pl.multiple_of(slab * rows, rows)
     col = pl.multiple_of(at - slab * d, tile)
 
-    def one_piece(i, carry):
-        for out, index in ((keep, i), (send, i + half)):
-            src = pl.multiple_of(ids[index] * rows, rows)
-            out[i, pl.ds(row, rows), pl.ds(col, tile)] = tn_dot(
-                x_s[:, pl.ds(src, rows)], du_s[...]
-            ).astype(bf16)
-        return carry
-
-    lax.fori_loop(0, half, one_piece, 0)
+    for i in range(count):
+        src = pl.multiple_of(ids[i] * rows, rows)
+        (keep if i < half else send)[i % half, pl.ds(row, rows), pl.ds(col, tile)] = tn_dot(
+            x_s[:, pl.ds(src, rows)], du_s[...]
+        ).astype(bf16)
 
     @pl.when(step == count - 1)
     def _():
         for side in range(2):
             span = slice(side * CAP, (side + 1) * CAP)
-            y_out[side][...] = y_acc[span, :].astype(bf16)
-            h_out[side][...] = h_acc[span, :].astype(bf16)
+            (near, far)[side][0] = y_acc[span, :].astype(bf16)
+            (near, far)[side][1] = h_acc[span, :].astype(bf16)
 
 
 def expert(ids, xs, ys, prior, pieces, rows, tile, deps):
     count = len(pieces)
-    half = count // 2
     d = xs[0].shape[1]
     hc = count * tile
     total = 2 * CAP
     first_chunk = prior is None
     far = pl.BlockSpec(memory_space=pl.ANY)
-    both = (half,) + pieces[0].shape
+    part = (count // 2,) + pieces[0].shape
     return run_kernel(
         functools.partial(
             expert_kernel, count=count, rows=rows, tile=tile, first_chunk=first_chunk, block=320
@@ -556,9 +560,9 @@
         deps=deps,
         grid=(count,),
         in_specs=[far] * 4
-        + ([] if first_chunk else [whole((CAP, d), 1)] * 4)
+        + ([] if first_chunk else [whole((2, CAP, d), 1)] * 2)
         + [far] * count,
-        out_specs=[whole((CAP, d), 1)] * 4 + [whole(both, 1)] * 2,
+        out_specs=[whole((2, CAP, d), 1)] * 2 + [whole(part, 1)] * 2,
         scratch_shapes=[
             pltpu.VMEM((total, d), bf16),
             pltpu.VMEM((total, d), bf16),
@@ -570,24 +574,23 @@
             pltpu.VMEM((total, tile), bf16),
             pltpu.SemaphoreType.DMA((4 + (hc // d + 1) * count,)),
         ],
-        out_shape=[jax.ShapeDtypeStruct((CAP, d), bf16)] * 4
-        + [jax.ShapeDtypeStruct(both, bf16)] * 2,
+        out_shape=[jax.ShapeDtypeStruct((2, CAP, d), bf16)] * 2
+        + [jax.ShapeDtypeStruct(part, bf16)] * 2,
         compiler_params=params(60),
-        cost_estimate=cost(27),
+        cost_estimate=cost(53),
         name="experts",
     )
 
 
 def third_kernel(slot_col, gains, x_ref, cot, w_ref, *refs):
-    y_own, y_other, h_own, h_other = refs[:4]
-    out_ref, mid_ref, dz_ref, do_ref, g_ref = refs[4:]
+    near, far, out_ref, mid_ref, dz_ref, do_ref, g_ref = refs
     tile = x_ref.shape[0]
     at = lax.broadcasted_iota(jnp.int32, (tile, CAP), 1)
     own = jnp.where(slot_col[:, 0:1] == at, 1.0, 0.0).astype(bf16)
     other = jnp.where(slot_col[:, 0:1] == at + CAP, 1.0, 0.0).astype(bf16)
     x = x_ref[...]
-    out_ref[...] = x + nn_dot(own, y_own[...]) + nn_dot(other, y_other[...])
-    dh = nn_dot(own, h_own[...]) + nn_dot(other, h_other[...])
+    out_ref[...] = x + nn_dot(own, near[0]) + nn_dot(other, far[0])
+    dh = nn_dot(own, near[1]) + nn_dot(other, far[1])
     scaled, inverse = norm_rows(x)
     mid = cot[...] + norm_back(dh, scaled, inverse, gains[2:3, :])
     mid_ref[...] = mid
@@ -603,7 +606,7 @@
     g_ref[1:2, :] += jnp.sum(dh, axis=0, keepdims=True)
 
 
-def third(slot_col, gains, middle, cot, w_out, returned, deps):
+def third(slot_col, gains, middle, cot, w_out, returned, deps, through):
     n, d = middle.shape
     tile = 256
     row = pl.BlockSpec((tile, d), lambda i: (i, 0))
@@ -611,6 +614,7 @@
         third_kernel,
         inputs=[slot_col, gains, middle, cot, w_out, *returned],
         deps=deps,
+        through=through,
         grid=(n // tile,),
         in_specs=[
             pl.BlockSpec((tile, slot_col.shape[1]), lambda i: (i, 0)),
@@ -619,7 +623,7 @@
             row,
             whole((d, d), 1),
         ]
-        + [whole((CAP, d), 1)] * 4,
+        + [whole((2, CAP, d), 1)] * 2,
         out_specs=[row, row, row, row, whole((8, d))],
         out_shape=[
             jax.ShapeDtypeStruct((n, d), f32),
@@ -629,47 +633,75 @@
             jax.ShapeDtypeStruct((8, d), f32),
         ],
         compiler_params=params(56),
-        cost_estimate=cost(8),
+        cost_estimate=cost(17),
         name="combine",
     )
 
 
-def weights_kernel(ids, right, *refs, count, rows, lefts):
-    keep, send, left_t, res = refs[lefts:]
-
-    @pl.when(pl.program_id(0) == 0)
+def weights_kernel(ids, *refs, count, rows, groups, steps):
+    total = sum(groups)
+    lefts, rights = refs[:total], refs[total : total + len(groups)]
+    keep, send, res, *turned = refs[total + len(groups) :]
+    step = pl.program_id(0)
+
+    @pl.when(step == 0)
     def _():
-        wide = refs[0].shape[1]
-        for i in range(lefts):
-            left_t[i * wide : (i + 1) * wide, :] = jnp.transpose(refs[i][...])
-
-    res[...] = nn_dot(left_t[...], right[0])
+        k = 0
+        for size, left_t in zip(groups, turned):
+            wide = lefts[k].shape[1]
+            for i in range(size):
+                left_t[i * wide : (i + 1) * wide, :] = jnp.transpose(lefts[k + i][...])
+            k += size
+
+    start = 0
+    for right, left_t, size in zip(rights, turned, steps):
+
+        @pl.when((step >= start) & (step < start + size))
+        def _():
+            res[...] = nn_dot(left_t[...], right[0])
+
+        start += size
     for i in range(count):
         for out, r in ((keep, count + i), (send, 2 * count + i)):
             src = pl.multiple_of(ids[r] * rows, rows)
             out[i] = res[pl.ds(src, rows), :].astype(bf16)
 
 
-def weights(ids, lefts, right, count, deps=(), tile=512):
-    n = right.shape[1]
-    d = sum(left.shape[1] for left in lefts)
-    parts, _, wide = right.shape
-    per = wide // tile
+def weights(ids, products, count, us, deps=(), tile=512):
+    n = products[0][1].shape[1]
+    d = sum(left.shape[1] for left in products[0][0])
     rows = d // (2 * count)
+    steps = [right.shape[0] * right.shape[2] // tile for _, right in products]
+    in_specs = [whole(left.shape, 1) for lefts, _ in products for left in lefts]
+    start = 0
+    for (_, right), size in zip(products, steps):
+        per = right.shape[2] // tile
+
+        def place(j, s, start=start, size=size, per=per):
+            at = jnp.clip(j - start, 0, size - 1)
+            return at // per, 0, at % per
+
+        in_specs.append(pl.BlockSpec((1, n, tile), place))
+        start += size
     out = pl.BlockSpec((count, rows, tile), lambda j, s: (0, 0, j))
     return run_kernel(
-        functools.partial(weights_kernel, count=count, rows=rows, lefts=len(lefts)),
+        functools.partial(
+            weights_kernel,
+            count=count,
+            rows=rows,
+            groups=[len(lefts) for lefts, _ in products],
+            steps=steps,
+        ),
         prefetch=ids,
-        inputs=[right, *lefts],
+        inputs=[left for lefts, _ in products for left in lefts] + [right for _, right in products],
         deps=deps,
-        grid=(parts * per,),
-        in_specs=[pl.BlockSpec((1, n, tile), lambda j, s: (j // per, 0, j % per))]
-        + [whole(left.shape, 1) for left in lefts],
+        grid=(start,),
+        in_specs=in_specs,
         out_specs=[out, out],
-        scratch_shapes=[pltpu.VMEM((d, n), bf16), pltpu.VMEM((d, tile), f32)],
-        out_shape=[jax.ShapeDtypeStruct((count, rows, parts * wide), bf16)] * 2,
+        scratch_shapes=[pltpu.VMEM((d, tile), f32)] + [pltpu.VMEM((d, n), bf16) for _ in products],
+        out_shape=[jax.ShapeDtypeStruct((count, rows, start * tile), bf16)] * 2,
         compiler_params=params(48),
-        cost_estimate=cost(4),
+        cost_estimate=cost(us),
         name="weight_grads",
     )
 
@@ -714,7 +746,7 @@
         out_specs=[row, whole((8, d))],
         out_shape=[jax.ShapeDtypeStruct((n, d), f32), jax.ShapeDtypeStruct((8, d), f32)],
         compiler_params=params(48),
-        cost_estimate=cost(8),
+        cost_estimate=cost(1),
         name="token_grads",
     )
 
@@ -723,9 +755,11 @@
     return lax.dynamic_index_in_dim(value, index, axis, keepdims=False)
 
 
-def after(value, other):
-    mark = other.reshape(-1)[0] * jnp.zeros((), other.dtype)
-    return value + mark.astype(value.dtype)
+def after(value, *others):
+    for other in others:
+        mark = lax.slice(other, (0,) * other.ndim, (1,) * other.ndim).reshape(()) * jnp.zeros((), other.dtype)
+        value = value + mark.astype(value.dtype)
+    return value
 
 
 def in_order(core, mine, theirs):
@@ -757,8 +791,7 @@
     owned = expert_out.shape[0]
     chips = 1 << bits
     devices = 2 * chips * fs
-    per = owned // CHUNKS
-    hc = hidden // CHUNKS
+    hc = hidden // 2
     links = Links(bits, fs)
     core = lax.axis_index("core")
     zed = lax.axis_index("fsdp")
@@ -771,34 +804,31 @@
 
     norms = jnp.stack([gain_one, shift_one, gain_two, shift_two], axis=1)
     norms = jnp.pad(norms, ((0, 0), (0, 124)))
-    shard = jnp.concatenate([w_query, w_key, w_value, norms, w_output], axis=1).astype(bf16)
+    shard = jnp.concatenate([w_output, w_query, w_key, w_value, norms], axis=1).astype(bf16)
     line = links.gather_line(shard).reshape(fs * share, -1)
 
     def gather_attention(block):
         own = links.gather_chips(block)
         return own + [swap(piece, "core") for piece in own]
 
-    qkv_pieces = gather_attention(line[:, : 3 * d + 128])
-    out_pieces = gather_attention(line[:, 3 * d + 128 :])
+    pieces = gather_attention(line)
 
     slabs = hc // d
-    in_rows, out_rows = 2 * fs * share, 2 * fs * per
-    in_low = expert_in.astype(bf16).transpose(1, 0, 2).reshape(2, share, devices, CHUNKS, per)
-    in_low = in_low.transpose(0, 3, 1, 2, 4).reshape(2, CHUNKS, share, slabs, d)
-    in_low = in_low.transpose(0, 1, 3, 2, 4).reshape(2, CHUNKS, slabs * share, d)
-    out_low = expert_out.astype(bf16).transpose(1, 0, 2).reshape(2, CHUNKS, per, d)
-    low = jnp.concatenate([in_low, out_low], axis=2)
+    in_rows, out_rows = 2 * fs * share, fs * owned
+    in_low = expert_in.astype(bf16).reshape(share, 2, chips, 2, fs * owned).transpose(1, 3, 0, 2, 4)
+    in_low = in_low.reshape(2, 2, share, slabs, d).transpose(0, 1, 3, 2, 4).reshape(2, -1, d)
+    low = jnp.concatenate([in_low, expert_out.astype(bf16).transpose(1, 0, 2)], axis=1)
     pair = in_order(core, pick(low, core, 0), swap(pick(low, 1 - core, 0), "core"))
-    chunks, lines = [], []
-    before = line
-    for j in range(CHUNKS):
-        got = links.gather_line(after(pair[:, j], before))
-        in_part = got[:, :, : slabs * share].reshape(fs, 2, slabs, share, d)
+    in_pair = pair[:, : 2 * slabs * share].reshape(2, 2, slabs * share, d)
+    out_pair = pair[:, 2 * slabs * share :]
+
+    def gather_experts(j, before, gate):
+        mine = jnp.concatenate([in_pair[:, j].reshape(-1, d), out_pair[j]], axis=0)
+        got = after(links.gather_line(after(mine, before)), gate)
+        in_part = got[:, : 2 * slabs * share].reshape(fs, 2, slabs, share, d)
         in_part = in_part.transpose(2, 1, 0, 3, 4).reshape(slabs * in_rows, d)
-        out_part = got[:, :, slabs * share :].transpose(1, 0, 2, 3).reshape(out_rows, d)
-        lines.append(jnp.concatenate([in_part, out_part], axis=0))
-        chunks.append(links.gather_chips(lines[-1]))
-        before = chunks[-1][1]
+        out_part = got[:, 2 * slabs * share :].reshape(out_rows, d)
+        return jnp.concatenate([in_part, out_part], axis=0)
 
     spots = jnp.arange(n, dtype=jnp.int32)
     eight = jnp.arange(lengths.shape[1])
@@ -819,88 +849,116 @@
 
     dy_own, dy_other = pack(slot_row, cotangent)
     dys = (dy_own, swap(dy_other, "core"))
-    h1, qkv, w_qkv, gains = first(ids, tokens, qkv_pieces, [lines[0]])
+    lines = [gather_experts(0, line, pieces[1])]
+    h1, qkv, w_qkv, gains = first(ids, tokens, pieces, lines[:1])
+
+    def spread_chunk(block, hold):
+        pieces = [block]
+        for t in range(bits):
+            if t == bits - 1:
+                pieces = [after(block, pieces[-1] if hold is None else hold)] + pieces[1:]
+            pieces = pieces + [links.swap(p, t) for p in pieces]
+        return [block] + pieces[1:]
+
+    chunks = [spread_chunk(lines[0], h1)]
+    lines.append(gather_experts(1, lines[0], h1))
     mixed, lse = [], []
-    needs = [[chunks[0][1], *out_pieces[chips:]], []]
     for i in range(PARTS):
-        made = attend(kseg, qseg, qkv, i, PARTS, needs[i] + lse[-1:])
+        needs = [*lse[-1:], *chunks[0][2:-1], lines[1]] if i else [chunks[0][1]]
+        made = attend(kseg, qseg, qkv, i, PARTS, needs)
         mixed.append(made[0])
         lse.append(made[1])
-    middle, w_out, x_own, x_other = second(ids, slot_row, mixed, tokens, gains, out_pieces, [lines[1]])
+    chunks.append(spread_chunk(lines[1], None))
+    middle, w_out, x_own, x_other = second(
+        ids, slot_row, mixed, tokens, gains, pieces, []
+    )
     xs = (x_own, swap(x_other, "core"))
 
-    def chip_rows(keep, send):
-        t = bits - 1
-        got = links.swap(send, t)
-        while t > 0:
-            half = keep.shape[0] // 2
-            send, keep = add_low(keep[half:], got[half:]), add_low(keep[:half], got[:half])
-            yield send
-            t -= 1
+    def line_rows(total):
+        in_part = total[: slabs * in_rows].reshape(slabs, 2, fs, share, d)
+        in_part = in_part.transpose(2, 1, 0, 3, 4).reshape(fs, 2 * slabs * share, d)
+        return jnp.concatenate([in_part, total[slabs * in_rows :].reshape(fs, owned, d)], axis=1)
+
+    def chip_sum(keep, send, gate):
+        got = links.swap(send, bits - 1)
+        for t in reversed(range(bits - 1)):
+            top = keep.shape[0] // 2
+            send = add_low(keep[top:], got[top:])
+            total = keep[:top].astype(f32) + got[:top].astype(f32)
+            first_send.append(send)
             got = links.swap(send, t)
-        total = add_low(keep[0], got[0])
-        in_part = total[: slabs * in_rows].reshape(slabs, 2, fs, share, d)
-        in_part = in_part.transpose(2, 1, 0, 3, 4).reshape(fs, 2, slabs * share, d)
-        out_part = total[slabs * in_rows :].reshape(2, fs, per, d).transpose(1, 0, 2, 3)
-        total = jnp.concatenate([in_part, out_part], axis=2)
-        yield total
-        yield links.reduce_line(total)
-
-    made = expert(ids, xs, dys, None, chunks[0], in_rows, out_rows, [chunks[1][1]])
-    stages = [list(chip_rows(made[4], made[5]))]
-    made = expert(ids, xs, dys, made[:4], chunks[1], in_rows, out_rows, [])
-    stages.append(list(chip_rows(made[4], made[5])))
-    y_own, y_far, h_own, h_far = made[:4]
-    returned = (y_own, swap(y_far, "core"), h_own, swap(h_far, "core"))
-
-    output, grad_middle, dz, grad_mixed, sums_two = third(
-        slot_col, gains, middle, cotangent, w_out, returned, [stages[0][0]]
-    )
-
-    def attention_rows(keep, send):
-        keep = add_low(keep, swap(send, "core"))
-        half = chips // 2
-        yield keep
-        got = links.reduce_chips(keep[:half], keep[half:])
-        yield got.reshape(fs, share, -1)
+            if t:
+                keep = total.astype(bf16)
+            else:
+                return after((total + got.astype(f32)).astype(bf16)[0], *gate)
+        return after(add_low(keep[0], got[0]), *gate)
+
+    half = chips // 2
+    near, far, keep_a, send_a = expert(ids, xs, dys, None, chunks[0], in_rows, out_rows, [chunks[1][1]])
+    near, far, keep_b, send_b = expert(ids, xs, dys, [near, far], chunks[1], in_rows, out_rows, [])
+    returned = (near, swap(far, "core"))
+
+    first_send = []
+    chunk_a = chip_sum(keep_a, send_a, [])
+    output, grad_middle, dz, grad_mixed, sums_two, send_b = third(
+        slot_col, gains, middle, cotangent, w_out, returned, first_send, [send_b]
+    )
+
+    def core_sum(made):
+        return add_low(made[0], swap(made[1], "core"))
+
+    def split_sum(total):
+        got = links.swap(total[half:], bits - 1)
+        return add_low(total[:half], got)
+
+    def rest_sum(total):
+        if bits > 1:
+            top = total.shape[0] // 2
+            total = links.reduce_chips(total[:top], total[top:], bits - 1)
+        else:
+            total = total[0]
+        return total.reshape(fs, share, -1)
 
     wide = d // PARTS
-    made = weights(ids, mixed, dz[None], chips)
-    out_stages = list(attention_rows(*made))
-    grads, qkv_stages = [], []
-    needs = [[stages[0][-2]], [stages[1][0]]]
-    for i in range(PARTS):
-        grads.append(
-            attend_back(kseg, qseg, qkv, grad_mixed, lse[i], i, PARTS, needs[i] + [made[1]])
-        )
-        made = weights(ids, [h1], grads[i], chips, [[out_stages[0]], [stages[0][-1], stages[1][-2]]][i])
-        qkv_stages.append(list(attention_rows(*made)))
-    grad_tokens, sums_one = last(
-        gains, tokens, grad_middle, grads, w_qkv, [made[1], qkv_stages[0][-1], out_stages[-1]]
-    )
-    ready = [g[-1] for g in qkv_stages] + [out_stages[-1]]
-    ready = links.reduce_line_direct(jnp.concatenate(ready, axis=2), zed)
+    chunk_a = line_rows(after(chunk_a, dz))
+    line_a = links.reduce_line(chunk_a)
+    grads = [attend_back(kseg, qseg, qkv, grad_mixed, lse[0], 0, PARTS, [chunk_a])]
+    made_a = weights(ids, [(mixed, dz[None]), ([h1], grads[0])], chips, 0.1)
+    first_send = []
+    chunk_b = chip_sum(keep_b, send_b, [])
+    grads.append(
+        attend_back(kseg, qseg, qkv, grad_mixed, lse[1], 1, PARTS, [made_a[1], *first_send])
+    )
+    chunk_b = line_rows(after(chunk_b, grads[1]))
+    line_b = links.reduce_line(chunk_b)
+    core_a = after(core_sum(made_a), grads[1])
+    made_b = weights(ids, [([h1], grads[1])], chips, 0.1, [core_a, chunk_b])
+    core_b = core_sum(made_b)
+    split_a, split_b = split_sum(core_a), split_sum(core_b)
+    ready = [rest_sum(split_a), rest_sum(split_b)]
+    grad_tokens, sums_one = last(gains, tokens, grad_middle, grads, w_qkv, [core_b])
+    ready = links.reduce_line_direct(after(jnp.concatenate(ready, axis=2), line_b), zed)
+    grad_output = ready[:, :d]
     grad_qkv = [
         jnp.concatenate(
-            [ready[:, (3 * j + i) * wide : (3 * j + i + 1) * wide] for j in range(PARTS)], axis=1
+            [ready[:, d + (3 * j + i) * wide : d + (3 * j + i + 1) * wide] for j in range(PARTS)],
+            axis=1,
         )
         for i in range(3)
     ]
-    grad_output = ready[:, 3 * d :]
-
-    def settle(rows):
-        return in_order(core, pick(rows, core, 0), swap(pick(rows, 1 - core, 0), "core"))
-
-    totals = [settle(s[-1]) for s in stages]
-    grad_expert_in = jnp.stack(
-        [g[:, : slabs * share].reshape(2, slabs, share, d) for g in totals], axis=0
-    )
-    grad_expert_in = grad_expert_in.transpose(3, 1, 0, 2, 4).reshape(share, 2, CHUNKS, devices, per)
-    grad_expert_in = grad_expert_in.transpose(0, 1, 3, 2, 4).reshape(share, 2, hidden)
-    grad_expert_out = jnp.stack([g[:, slabs * share :] for g in totals], axis=1)
-    grad_expert_out = grad_expert_out.reshape(2, owned, d).transpose(1, 0, 2)
+
+    ins = jnp.stack([t[: 2 * slabs * share].reshape(2, slabs * share, d) for t in (line_a, line_b)])
+    outs = jnp.stack([t[2 * slabs * share :] for t in (line_a, line_b)])
+    theirs = jnp.concatenate([pick(ins, 1 - core, 1).reshape(-1, d), pick(outs, 1 - core, 0)], axis=0)
+    got = swap(theirs, "core")
+    in_grad = in_order(core, pick(ins, core, 1).reshape(-1, d), got[: 2 * slabs * share])
+    in_grad = in_grad.reshape(2, 2, slabs, share, d // (fs * owned), fs * owned)
+    grad_expert_in = in_grad.transpose(3, 0, 2, 4, 1, 5).reshape(share, 2, hidden)
+    out_grad = in_order(core, pick(outs, core, 0), got[2 * slabs * share :])
+    grad_expert_out = out_grad.transpose(1, 0, 2)
 
     sums = jnp.concatenate([sums_one[:2], sums_two[:2]]).reshape(4, devices, share).transpose(1, 0, 2)
+    sums = after(sums, line_b)
     sums = jnp.sum(lax.all_to_all(sums, links.axes + ("fsdp",), 0, 0), axis=0)
 
     return (

time: 606 us -> 543 us (0.90)
  waiting for transfers between devices: 160 us -> 105 us
  blocking collectives: 10.6 us -> 0 us
  other arithmetic: 43.8 us -> 53.7 us
    all_to_all x2, waiting for transfers between devices: 44.6 us -> 11.1 us  [reduce_line(): got = lax.all_to_all(value, 'fsdp', 0, 0)]
    ppermute x22 -> x17, waiting for transfers between devices: 75.3 us -> 59 us  [swap(): return lax.ppermute(value, self.axes, pairs)]
    add x2 -> x11, other arithmetic: 0.08 us -> 14.5 us  [after(): value = value + mark.astype(value.dtype)]
    all_to_all x1 -> x0, blocking collectives: 10.6 us -> none  [local(): sums = jnp.sum(lax.all_to_all(sums, links.axes + ('fsdp',), 0, 0), axis=0)]
    all_to_all x0 -> x1, waiting for transfers between devices: none -> 10.2 us  [local(): sums = jnp.sum(lax.all_to_all(sums, links.axes + ('fsdp',), 0, 0), axis=0)]
    unnamed x84 -> x79, local copies, waits for them, and re-layouts: 17 us -> 7.13 us
    convert_element_type x13 -> x7, other arithmetic: 20.4 us -> 11.1 us  [add_low(): return (a.astype(f32) + b.astype(f32)).astype(bf16)]
    ppermute x22 -> x17, starting transfers between devices: 26.2 us -> 18.3 us  [swap(): return lax.ppermute(value, self.axes, pairs)]
  transfers between devices with their start and end apart: 48 -> 37, of which waited for: 18 -> 13; matrix products, arithmetic and copies ran while one was open for 10% -> 12% of each run, Pallas kernels for 43% -> 52%
where the time goes in v2:
time: 543 us; the launch traced here: 536 us
  Pallas kernels  278 us (51%)
  waiting for transfers between devices  105 us (19%)
  other arithmetic  53.7 us (10%)
  starting transfers between devices  53.7 us (10%)
  local copies, waits for them, and re-layouts  37.2 us (7%)
  between operations  7.43 us (1%)
    pallas_call x12, Pallas kernels, run_kernel(): pl.pallas_call(body, grid_spec=spec, out_shape=out_shape + [jax.ShapeDtyp...  273 us
    ppermute x17, waiting for transfers between devices, swap(): return lax.ppermute(value, self.axes, pairs)  59 us
    all_to_all x3, waiting for transfers between devices, gather_line(): return lax.all_to_all(spread, 'fsdp', 0, 0)  22.9 us
    ppermute x17, starting transfers between devices, swap(): return lax.ppermute(value, self.axes, pairs)  18.3 us
    all_to_all x3, starting transfers between devices, gather_line(): return lax.all_to_all(spread, 'fsdp', 0, 0)  15.3 us
    add x11, other arithmetic, after(): value = value + mark.astype(value.dtype)  14.5 us
    convert_element_type x7, other arithmetic, add_low(): return (a.astype(f32) + b.astype(f32)).astype(bf16)  11.1 us
    all_to_all x2, waiting for transfers between devices, reduce_line(): got = lax.all_to_all(value, 'fsdp', 0, 0)  11.1 us
  transfers between devices with their start and end apart: 37, of which 13 were waited for; matrix products, arithmetic and copies ran while one was open for 12% of the time, Pallas kernels for 52%

profile of v2, /device:TPU:0, one launch (start us, length us, event | category | flops | bytes accessed | tf_op | source)
XLA Modules:
  0.0 536.1 jit_solution(11966561506449021620)
XLA Ops:
  6.9 6.3 %all-to-all-start = ((bf16[4,32,4224]{2,1,0:T(8,128)(2,1)}), bf16[4,32,4224]{2,1,0:T(8,128)(2,1)}, u32[]{:S(2)}, u32[]{:S(2)}) async-start(bf16[4,32,4224]{2,1,0:T(8,128)(2,1)} %broadcast_in_dim.38), calls=%async_computation | async-start | bytes 2162688 | tf_op jit(solution)/shard_map/all_to_all | solution.py:115
  15.4 1.9 collective-permute-done.7
  19.0 20.8 %all-to-all-done = bf16[4,32,4224]{2,1,0:T(8,128)(2,1)} async-done(((bf16[4,32,4224]{2,1,0:T(8,128)(2,1)}), bf16[4,32,4224]{2,1,0:T(8,128)(2,1)}, u32[]{:S(2)}, u32[]{:S(2)}) %all-to-all-start) | async-done | bytes 1081376 | tf_op jit(solution)/shard_map/all_to_all | solution.py:115
  41.7 1.6 broadcast_in_dim.39
  43.3 3.8 all-to-all-start.1
  47.1 1.6 collective-permute-start
  48.7 1.5 collective-permute-start.1
  50.2 23.9 %collective-permute-done.refs_3_.refs_7_ = bf16[128,4224]{1,0:T(8,128)(2,1)} collective-permute-done((bf16[128,4224]{1,0:T(8,128)(2,1)}, bf16[128,4224]{1,0:T(8,128)(2,1)}, u32[]{:S(2)}, u32[]{:S(2)}) %collective-permute-start) | collective-permute-done | bytes 1081376 | tf_op jit(solution)/shard_map/ppermute | solution.py:111
  76.1 13.5 %collective-permute-done.2.refs_5_.refs_9_ = bf16[128,4224]{1,0:T(8,128)(2,1)} collective-permute-done((bf16[128,4224]{1,0:T(8,128)(2,1)}, bf16[128,4224]{1,0:T(8,128)(2,1)}, u32[]{:S(2)}, u32[]{:S(2)}) %collective-permute-start.2) | collective-permute-done | bytes 1081376 | tf_op jit(solution)/shard_map/ppermute | solution.py:111
  89.6 5.1 pack.1
  98.0 1.6 pad_maximum_fusion.refs_10_.refs_5_
  99.6 1.5 collective-permute-start.8
  103.0 1.6 broadcast_in_dim.83
  104.6 5.2 all-to-all-start.2
  109.9 17.0 %qkv.1 = (bf16[1024,1024]{1,0:T(8,128)(2,1)}, bf16[3,1024,1024]{2,1,0:T(8,128)(2,1)}, bf16[1024,3072]{1,0:T(8,128)(2,1)}, f32[8,1024]{1,0:T(8,128)}) custom-call(s32[12]{0:T(128)} %pad_add_fusion.refs_0_, f32[1024,1024]{1,0:T(8,128)} %refs_1_.3, bf16[128,4224]{1,0:T(8,128)(2,1)} %bitcast.8.refs_2_.refs_6_, ...), custom_call_target="tpu_custom_call" | custom-call | flops 18400000000 | bytes 1048576 | tf_op jit(solution)/shard_map/qkv/pallas_call | solution.py:77
  128.8 1.8 broadcast_add_fusion.2
  131.0 1.6 collective-permute-start.12
  132.9 21.3 %attend.2 = (bf16[1024,512]{1,0:T(8,128)(2,1)S(1)}, f32[4,8,1024]{2,1,0:T(8,128)S(1)}) custom-call(s32[1024,128]{1,0:T(8,128)S(1)} %broadcast_in_dim.45.refs_0_, s32[8,1024]{1,0:T(8,128)S(1)} %broadcast_in_dim.82.refs_1_, bf16[3,1024,1024]{2,1,0:T(8,128)(2,1)} %get-tuple-element.47.refs_2_, bf16[1024,1024]{1,0:T(8,128)(2,1)} %collective-permute-done.8.refs_3_.refs_6_), custom_call_target="tpu_custom_call" | custom-call | flops 24149999616 | bytes 1048576 | tf_op jit(solution)/shard_map/attend/pallas_call | solution.py:77
  155.1 2.1 all-to-all-done.2
  157.2 1.7 broadcast_add_fusion.1
  160.1 1.5 collective-permute-start.13
  161.6 21.1 %attend.3 = (bf16[1024,512]{1,0:T(8,128)(2,1)S(1)}, f32[4,8,1024]{2,1,0:T(8,128)S(1)}) custom-call(s32[1024,128]{1,0:T(8,128)S(1)} %broadcast_in_dim.45.refs_0_, s32[8,1024]{1,0:T(8,128)S(1)} %broadcast_in_dim.82.refs_1_, bf16[3,1024,1024]{2,1,0:T(8,128)(2,1)} %get-tuple-element.47.refs_2_, f32[4,8,1024]{2,1,0:T(8,128)S(1)} %get-tuple-element.49.refs_3_.refs_4_, ...), custom_call_target="tpu_custom_call" | custom-call | flops 24149999616 | bytes 1048576 | tf_op jit(solution)/shard_map/attend/pallas_call | solution.py:77
  184.4 13.6 %mix_out.1 = (f32[1024,1024]{1,0:T(8,128)}, bf16[1024,1024]{1,0:T(8,128)(2,1)}, bf16[640,1024]{1,0:T(8,128)(2,1)}, bf16[640,1024]{1,0:T(8,128)(2,1)}) custom-call(s32[12]{0:T(128)} %pad_add_fusion.refs_0_, s32[8,1024]{1,0:T(8,128)} %copy-done.8, f32[1024,1024]{1,0:T(8,128)} %refs_1_.3, f32[8,1024]{1,0:T(8,128)} %get-tuple-element.46.refs_3_.refs_1_.refs_0_, ...), custom_call_target="tpu_custom_call" | custom-call | flops 1150000000 | bytes 1048576 | tf_op jit(solution)/shard_map/mix_out/pallas_call | solution.py:77
  198.1 3.3 collective-permute-done.13.refs_9_.refs_8_
  203.8 2.0 collective-permute-start.15
  205.9 51.0 %experts.2 = (bf16[2,640,1024]{2,1,0:T(8,128)(2,1)}, bf16[2,640,1024]{2,1,0:T(8,128)(2,1)}, bf16[2,1024,1024]{2,1,0:T(8,128)(2,1)}, bf16[2,1024,1024]{2,1,0:T(8,128)(2,1)}) custom-call(s32[12]{0:T(128)} %pad_add_fusion.refs_0_, bf16[640,1024]{1,0:T(8,128)(2,1)} %get-tuple-element.54.refs_1_, bf16[640,1024]{1,0:T(8,128)(2,1)} %collective-permute-done.10.refs_2_, ...), custom_call_target="tpu_custom_call" | custom-call | flops 60949999616 | bytes 1048576 | tf_op jit(solution)/shard_map/experts/pallas_call | solution.py:77
  257.0 53.7 %experts.3 = (bf16[2,640,1024]{2,1,0:T(8,128)(2,1)}, bf16[2,640,1024]{2,1,0:T(8,128)(2,1)}, bf16[2,1024,1024]{2,1,0:T(8,128)(2,1)}, bf16[2,1024,1024]{2,1,0:T(8,128)(2,1)}) custom-call(s32[12]{0:T(128)} %pad_add_fusion.refs_0_, bf16[640,1024]{1,0:T(8,128)(2,1)} %get-tuple-element.54.refs_1_, bf16[640,1024]{1,0:T(8,128)(2,1)} %collective-permute-done.10.refs_2_, ...), custom_call_target="tpu_custom_call" | custom-call | flops 60949999616 | bytes 1048576 | tf_op jit(solution)/shard_map/experts/pallas_call | solution.py:77
  310.8 3.2 add_convert_fusion.4.refs_7_
  314.0 1.5 collective-permute-start.18
  317.6 17.5 %combine.1 = (f32[1024,1024]{1,0:T(8,128)}, f32[1024,1024]{1,0:T(8,128)}, bf16[1024,1024]{1,0:T(8,128)(2,1)}, bf16[1024,1024]{1,0:T(8,128)(2,1)}, f32[8,1024]{1,0:T(8,128)}, /*index=5*/bf16[2,1024,1024]{2,1,0:T(8,128)(2,1)}) custom-call(s32[1024,128]{1,0:T(8,128)} %broadcast_in_dim.37.refs_0_, ...), custom_call_target="tpu_custom_call", output_to_operand_aliasing={{5}: (8, {})} | custom-call | flops 19549999104 | bytes 1048576 | tf_op jit(solution)/shard_map/combine/pallas_call | solution.py:77
  335.1 2.0 collective-permute-start.19
  337.1 1.2 slice.204
  339.0 3.0 collective-permute-done.18
  342.0 3.7 fusion.2
  346.0 1.6 pad_maximum_fusion.2.refs_5_
  347.6 5.3 all-to-all-start.5
  352.9 22.3 %attend_back.2.refs_5_.refs_4_ = bf16[3,1024,512]{2,1,0:T(8,128)(2,1)} custom-call(s32[1024,128]{1,0:T(8,128)} %copy-done.7, s32[8,1024]{1,0:T(8,128)} %copy-done.10, bf16[3,1024,1024]{2,1,0:T(8,128)(2,1)} %get-tuple-element.47.refs_2_, bf16[1024,1024]{1,0:T(8,128)(2,1)} %get-tuple-element.68.refs_3_, f32[4,8,1024]{2,1,0:T(8,128)} %copy-done.14, ...), custom_call_target="tpu_custom_call" | custom-call | flops 25300000768 | bytes 1048576 | tf_op jit(solution)/shard_map/attend_back/pallas_call | solution.py:77
  375.2 11.8 %weight_grads.2 = (bf16[4,128,2560]{2,1,0:T(8,128)(2,1)}, bf16[4,128,2560]{2,1,0:T(8,128)(2,1)}) custom-call(s32[12]{0:T(128)S(1)} %copy-done.11, bf16[1024,512]{1,0:T(8,128)(2,1)S(1)} %copy-done.3, bf16[1024,512]{1,0:T(8,128)(2,1)S(1)} %copy-done.5, bf16[1024,1024]{1,0:T(8,128)(2,1)S(1)} %copy-done.1, bf16[1,1024,1024]{2,1,0:T(8,128)(2,1)} %bitcast.124, ...), custom_call_target="tpu_custom_call" | custom-call | flops 115000000 | bytes 1048576 | tf_op jit(solution)/shard_map/weight_grads/pallas_call | solution.py:77
  387.1 3.9 add_convert_fusion.2.refs_6_
  391.0 1.7 collective-permute-start.21
  392.7 22.6 %attend_back.3.refs_2_.refs_5_ = bf16[3,1024,512]{2,1,0:T(8,128)(2,1)} custom-call(s32[1024,128]{1,0:T(8,128)} %copy-done.7, s32[8,1024]{1,0:T(8,128)} %copy-done.10, bf16[3,1024,1024]{2,1,0:T(8,128)(2,1)} %get-tuple-element.47.refs_2_, bf16[1024,1024]{1,0:T(8,128)(2,1)} %get-tuple-element.68.refs_3_, f32[4,8,1024]{2,1,0:T(8,128)} %copy-done.13, ...), custom_call_target="tpu_custom_call" | custom-call | flops 25300000768 | bytes 1048576 | tf_op jit(solution)/shard_map/attend_back/pallas_call | solution.py:77
  415.3 1.2 slice.262
  417.2 2.4 fusion.1.refs_3_
  420.3 3.7 fusion.3
  424.4 1.5 pad_maximum_fusion.3.refs_4_
  425.9 7.0 %weight_grads.3 = (bf16[4,128,1536]{2,1,0:T(8,128)(2,1)S(1)}, bf16[4,128,1536]{2,1,0:T(8,128)(2,1)S(1)}) custom-call(s32[12]{0:T(128)S(1)} %copy-done.11, bf16[1024,1024]{1,0:T(8,128)(2,1)S(1)} %copy-done.1, bf16[3,1024,512]{2,1,0:T(8,128)(2,1)} %attend_back.3.refs_2_.refs_5_, bf16[4,128,2560]{2,1,0:T(8,128)(2,1)} %fusion.1.refs_3_, ...), custom_call_target="tpu_custom_call" | custom-call | flops 115000000 | bytes 1048576 | tf_op jit(solution)/shard_map/weight_grads/pallas_call | solution.py:77
  436.0 3.0 convert_reduce_fusion
  439.1 5.4 all-to-all-start.3
  444.4 1.9 add_convert_fusion.5.refs_6_
  446.5 1.8 collective-permute-start.25
  448.3 4.6 collective-permute-done.23
  452.9 1.6 add_convert_fusion.6
  456.2 9.7 %collective-permute-done.25 = bf16[2,128,1536]{2,1,0:T(8,128)(2,1)S(1)} collective-permute-done((bf16[2,128,1536]{2,1,0:T(8,128)(2,1)S(1)}, bf16[2,128,1536]{2,1,0:T(8,128)(2,1)S(1)}, u32[]{:S(2)}, u32[]{:S(2)}) %collective-permute-start.25) | collective-permute-done | bytes 786464 | tf_op jit(solution)/shard_map/ppermute | solution.py:111
  467.5 14.0 %token_grads.1 = (f32[1024,1024]{1,0:T(8,128)}, f32[8,1024]{1,0:T(8,128)S(1)}) custom-call(f32[8,1024]{1,0:T(8,128)S(1)} %copy-done.9, f32[1024,1024]{1,0:T(8,128)} %refs_1_.3, f32[1024,1024]{1,0:T(8,128)} %get-tuple-element.66.refs_2_, bf16[1024,3072]{1,0:T(8,128)(2,1)} %get-tuple-element.67.refs_3_, bf16[3,1024,512]{2,1,0:T(8,128)(2,1)S(1)} %copy-done, ...), custom_call_target="tpu_custom_call" | custom-call | flops 1150000000 | bytes 1048576 | tf_op jit(solution)/shard_map/token_grads/pallas_call | solution.py:77
  481.6 11.1 %all-to-all-done.3 = bf16[4,256,1024]{2,1,0:T(8,128)(2,1)} async-done(((bf16[4,256,1024]{2,1,0:T(8,128)(2,1)}), bf16[4,256,1024]{2,1,0:T(8,128)(2,1)}, u32[]{:S(2)}, u32[]{:S(2)}) %all-to-all-start.3) | async-done | bytes 2097184 | tf_op jit(solution)/shard_map/all_to_all | solution.py:143
  492.6 2.1 convert_reduce_fusion.1
  497.9 1.4 collective-permute-start.29
  500.8 5.3 all-to-all-start.4
  506.5 3.0 fusion.8
  511.5 10.2 %all-to-all-done.4 = f32[32,1,128]{2,1,0:T(1,128)S(1)} async-done(((f32[32,1,128]{2,1,0:T(1,128)}), f32[32,1,128]{2,1,0:T(1,128)S(1)}, u32[]{:S(2)}, u32[]{:S(2)}) %all-to-all-start.4) | async-done | bytes 16416 | tf_op jit(solution)/shard_map/all_to_all | solution.py:962
  523.6 1.2 fusion.16
  527.6 1.3 fusion.30
  530.6 2.2 reshape.270
  533.2 2.5 fusion.6
  (210 shorter events, 47.4 us)
Async XLA Ops:
  1.6 11.7 %copy-start.27 = (f32[32,2,4096]{2,1,0:T(2,128)S(1)}, f32[32,2,4096]{2,1,0:T(2,128)}, u32[]{:S(2)}) copy-start(f32[32,2,4096]{2,1,0:T(2,128)} %param.25) | copy-start | bytes 3145732
  6.9 32.9 %all-to-all-start = ((bf16[4,32,4224]{2,1,0:T(8,128)(2,1)}), bf16[4,32,4224]{2,1,0:T(8,128)(2,1)}, u32[]{:S(2)}, u32[]{:S(2)}) async-start(bf16[4,32,4224]{2,1,0:T(8,128)(2,1)} %broadcast_in_dim.38), calls=%async_computation | async-start | bytes 2162688 | tf_op jit(solution)/shard_map/all_to_all | solution.py:115
  15.3 2.0 collective-permute-start.7
  43.3 5.4 %copy-start.36 = (s32[1,8]{1,0:T(1,128)S(1)}, s32[1,8]{1,0:T(1,128)}, u32[]{:S(2)}) copy-start(s32[1,8]{1,0:T(1,128)} %param.27) | copy-start | bytes 100
  43.3 30.9 %copy-start.34 = (s32[2,4]{1,0:T(2,128)S(1)}, s32[2,4]{1,0:T(2,128)}, u32[]{:S(2)}) copy-start(s32[2,4]{1,0:T(2,128)} %constant.105.clone) | copy-start | bytes 100
  43.3 30.9 %copy-start.32 = (s32[1024,1]{0,1:T(1,128)S(1)}, s32[1024,1]{0,1:T(1,128)}, u32[]{:S(2)}) copy-start(s32[1024,1]{0,1:T(1,128)} %param.28) | copy-start | bytes 12292
  43.3 31.6 %copy-start.33 = (s32[1024]{0:T(1024)S(1)}, s32[1024]{0:T(1024)}, u32[]{:S(2)}) copy-start(s32[1024]{0:T(1024)} %param.29) | copy-start | bytes 12292
  43.3 54.3 %all-to-all-start.1 = ((bf16[4,256,1024]{2,1,0:T(8,128)(2,1)}), bf16[4,256,1024]{2,1,0:T(8,128)(2,1)S(1)}, u32[]{:S(2)}, u32[]{:S(2)}) async-start(bf16[4,256,1024]{2,1,0:T(8,128)(2,1)} %broadcast_in_dim.39), calls=%async_computation.1 | async-start | bytes 4194304 | tf_op jit(solution)/shard_map/all_to_all | solution.py:115
  47.1 27.1 %collective-permute-start = (bf16[128,4224]{1,0:T(8,128)(2,1)}, bf16[128,4224]{1,0:T(8,128)(2,1)}, u32[]{:S(2)}, u32[]{:S(2)}) collective-permute-start(bf16[128,4224]{1,0:T(8,128)(2,1)} %bitcast.8.refs_2_.refs_6_), channel_id=1, source_target_pairs={{0,16},{4,12},{8,24},{12,4},{16,0},{20,28},{24,8},{28,20},{1,17},{... | collective-permute-start | bytes 3244040 | tf_op jit(solution)/shard_map/ppermute | solution.py:111
  48.7 27.3 %collective-permute-start.1 = (bf16[128,4224]{1,0:T(8,128)(2,1)}, bf16[128,4224]{1,0:T(8,128)(2,1)}, u32[]{:S(2)}, u32[]{:S(2)}) collective-permute-start(bf16[128,4224]{1,0:T(8,128)(2,1)} %bitcast.8.refs_2_.refs_6_), channel_id=1, source_target_pairs={{0,8},{4,20},{8,0},{12,28},{16,24},{20,4},{24,16},{28,12},{1,9},{5... | collective-permute-start | bytes 3244040 | tf_op jit(solution)/shard_map/ppermute | solution.py:111
  74.1 15.5 %collective-permute-start.2 = (bf16[128,4224]{1,0:T(8,128)(2,1)}, bf16[128,4224]{1,0:T(8,128)(2,1)}, u32[]{:S(2)}, u32[]{:S(2)}) collective-permute-start(bf16[128,4224]{1,0:T(8,128)(2,1)} %collective-permute-done.refs_3_.refs_7_), channel_id=1, source_target_pairs={{0,8},{4,20},{8,0},{12,28},{16,24},{20,4},{24,16},{28,12},{1,9},{5... | collective-permute-start | bytes 3244040 | tf_op jit(solution)/shard_map/ppermute | solution.py:111
  75.5 34.3 %collective-permute-start.3 = (bf16[128,4224]{1,0:T(8,128)(2,1)}, bf16[128,4224]{1,0:T(8,128)(2,1)}, u32[]{:S(2)}, u32[]{:S(2)}) collective-permute-start(bf16[128,4224]{1,0:T(8,128)(2,1)} %bitcast.8.refs_2_.refs_6_), channel_id=1, source_target_pairs={{0,4},{4,0},{1,5},{5,1},{2,6},{6,2},{3,7},{7,3},{8,12},{12,8},{9,1... | collective-permute-start | bytes 3244040 | tf_op jit(solution)/shard_map/ppermute | solution.py:88
  75.5 34.4 %collective-permute-start.4 = (bf16[128,4224]{1,0:T(8,128)(2,1)}, bf16[128,4224]{1,0:T(8,128)(2,1)}, u32[]{:S(2)}, u32[]{:S(2)}) collective-permute-start(bf16[128,4224]{1,0:T(8,128)(2,1)} %collective-permute-done.refs_3_.refs_7_), channel_id=1, source_target_pairs={{0,4},{4,0},{1,5},{5,1},{2,6},{6,2},{3,7},{7,3},{8,12},{12,8},{9,1... | collective-permute-start | bytes 3244040 | tf_op jit(solution)/shard_map/ppermute | solution.py:88
  76.0 33.9 %collective-permute-start.5 = (bf16[128,4224]{1,0:T(8,128)(2,1)}, bf16[128,4224]{1,0:T(8,128)(2,1)}, u32[]{:S(2)}, u32[]{:S(2)}) collective-permute-start(bf16[128,4224]{1,0:T(8,128)(2,1)} %collective-permute-done.1.refs_4_.refs_8_), channel_id=1, source_target_pairs={{0,4},{4,0},{1,5},{5,1},{2,6},{6,2},{3,7},{7,3},{8,12},{12,8},{9,1... | collective-permute-start | bytes 3244040 | tf_op jit(solution)/shard_map/ppermute | solution.py:88
  89.6 20.3 %collective-permute-start.6 = (bf16[128,4224]{1,0:T(8,128)(2,1)}, bf16[128,4224]{1,0:T(8,128)(2,1)}, u32[]{:S(2)}, u32[]{:S(2)}) collective-permute-start(bf16[128,4224]{1,0:T(8,128)(2,1)} %collective-permute-done.2.refs_5_.refs_9_), channel_id=1, source_target_pairs={{0,4},{4,0},{1,5},{5,1},{2,6},{6,2},{3,7},{7,3},{8,12},{12,8},{9,1... | collective-permute-start | bytes 3244040 | tf_op jit(solution)/shard_map/ppermute | solution.py:88
  89.6 5.1 copy-start.8
  98.0 4.9 copy-start.29
  98.0 4.9 copy-start.30
  99.6 31.4 %collective-permute-start.8 = (bf16[1024,1024]{1,0:T(8,128)(2,1)}, bf16[1024,1024]{1,0:T(8,128)(2,1)}, u32[]{:S(2)}, u32[]{:S(2)}) collective-permute-start(bf16[1024,1024]{1,0:T(8,128)(2,1)} %pad_maximum_fusion.refs_10_.refs_5_), channel_id=1, source_target_pairs={{0,16},{4,12},{8,24},{12,4},{16,0},{20,28},{24,8},{28,20},{1,17},{... | collective-permute-start | bytes 6291464 | tf_op jit(solution)/shard_map/ppermute | solution.py:111
  104.6 52.6 %all-to-all-start.2 = ((bf16[4,256,1024]{2,1,0:T(8,128)(2,1)}), bf16[4,256,1024]{2,1,0:T(8,128)(2,1)}, u32[]{:S(2)}, u32[]{:S(2)}) async-start(bf16[4,256,1024]{2,1,0:T(8,128)(2,1)} %broadcast_in_dim.83), calls=%async_computation.2 | async-start | bytes 4194304 | tf_op jit(solution)/shard_map/all_to_all | solution.py:115
  109.8 96.1 %collective-permute-start.11 = (bf16[640,1024]{1,0:T(8,128)(2,1)S(1)}, bf16[640,1024]{1,0:T(8,128)(2,1)}, u32[]{:S(2)}, u32[]{:S(2)}) collective-permute-start(bf16[640,1024]{1,0:T(8,128)(2,1)S(1)} %get-tuple-element.57), channel_id=1, source_target_pairs={{0,4},{4,0},{1,5},{5,1},{2,6},{6,2},{3,7},{7,3},{8,12},{12,8},{9,1... | collective-permute-start | bytes 3932168 | tf_op jit(solution)/shard_map/ppermute | solution.py:88
  130.6 31.0 %collective-permute-start.9 = (bf16[1024,1024]{1,0:T(8,128)(2,1)}, bf16[1024,1024]{1,0:T(8,128)(2,1)}, u32[]{:S(2)}, u32[]{:S(2)}) collective-permute-start(bf16[1024,1024]{1,0:T(8,128)(2,1)} %broadcast_add_fusion.2), channel_id=1, source_target_pairs={{0,8},{4,20},{8,0},{12,28},{16,24},{20,4},{24,16},{28,12},{1,9},{5... | collective-permute-start | bytes 6291464 | tf_op jit(solution)/shard_map/ppermute | solution.py:111
  131.0 74.9 %collective-permute-start.12 = (bf16[1024,1024]{1,0:T(8,128)(2,1)}, bf16[1024,1024]{1,0:T(8,128)(2,1)}, u32[]{:S(2)}, u32[]{:S(2)}) collective-permute-start(bf16[1024,1024]{1,0:T(8,128)(2,1)} %collective-permute-done.8.refs_3_.refs_6_), channel_id=1, source_target_pairs={{0,8},{4,20},{8,0},{12,28},{16,24},{20,4},{24,16},{28,12},{1,9},{5... | collective-permute-start | bytes 6291464 | tf_op jit(solution)/shard_map/ppermute | solution.py:111
  132.8 28.8 %copy-start.7 = (s32[1024,128]{1,0:T(8,128)}, s32[1024,128]{1,0:T(8,128)S(1)}, u32[]{:S(2)}) copy-start(s32[1024,128]{1,0:T(8,128)S(1)} %broadcast_in_dim.45.refs_0_) | copy-start | bytes 1572868
  132.8 28.8 %copy-start.10 = (s32[8,1024]{1,0:T(8,128)}, s32[8,1024]{1,0:T(8,128)S(1)}, u32[]{:S(2)}) copy-start(s32[8,1024]{1,0:T(8,128)S(1)} %broadcast_in_dim.82.refs_1_) | copy-start | bytes 98308
  155.1 6.5 %copy-start.14 = (f32[4,8,1024]{2,1,0:T(8,128)}, f32[4,8,1024]{2,1,0:T(8,128)S(1)}, u32[]{:S(2)}) copy-start(f32[4,8,1024]{2,1,0:T(8,128)S(1)} %get-tuple-element.49.refs_3_.refs_4_) | copy-start | bytes 393220
  160.1 22.7 %copy-start.6 = (bf16[1024,1024]{1,0:T(8,128)(2,1)}, bf16[1024,1024]{1,0:T(8,128)(2,1)S(1)}, u32[]{:S(2)}) copy-start(bf16[1024,1024]{1,0:T(8,128)(2,1)S(1)} %pad_maximum_fusion.1.refs_5_.refs_7_) | copy-start | bytes 6291460
  160.1 41.3 %collective-permute-start.13 = (bf16[1024,1024]{1,0:T(8,128)(2,1)S(1)}, bf16[1024,1024]{1,0:T(8,128)(2,1)}, u32[]{:S(2)}, u32[]{:S(2)}) collective-permute-start(bf16[1024,1024]{1,0:T(8,128)(2,1)S(1)} %pad_maximum_fusion.1.refs_5_.refs_7_), channel_id=1, source_target_pairs={{0,16},{4,12},{8,24},{12,4},{16,0},{20,28},{24,8},{28,20},{1,17},{... | collective-permute-start | bytes 6291464 | tf_op jit(solution)/shard_map/ppermute | solution.py:111
  184.4 18.8 %copy-start.18 = (bf16[4,128,1024]{2,1,0:T(8,128)(2,1)S(1)}, bf16[4,128,1024]{2,1,0:T(8,128)(2,1)}, u32[]{:S(2)}) copy-start(bf16[4,128,1024]{2,1,0:T(8,128)(2,1)} %copy-done.17) | copy-start | bytes 3145732
  198.1 7.8 %collective-permute-start.10 = (bf16[640,1024]{1,0:T(8,128)(2,1)}, bf16[640,1024]{1,0:T(8,128)(2,1)}, u32[]{:S(2)}, u32[]{:S(2)}) collective-permute-start(bf16[640,1024]{1,0:T(8,128)(2,1)} %get-tuple-element.55), channel_id=1, source_target_pairs={{0,4},{4,0},{1,5},{5,1},{2,6},{6,2},{3,7},{7,3},{8,12},{12,8},{9,1... | collective-permute-start | bytes 3932168 | tf_op jit(solution)/shard_map/ppermute | solution.py:88
  203.8 53.3 %collective-permute-start.14 = (bf16[1024,1024]{1,0:T(8,128)(2,1)S(1)}, bf16[1024,1024]{1,0:T(8,128)(2,1)}, u32[]{:S(2)}, u32[]{:S(2)}) collective-permute-start(bf16[1024,1024]{1,0:T(8,128)(2,1)S(1)} %broadcast_add_fusion), channel_id=1, source_target_pairs={{0,8},{4,20},{8,0},{12,28},{16,24},{20,4},{24,16},{28,12},{1,9},{5... | collective-permute-start | bytes 6291464 | tf_op jit(solution)/shard_map/ppermute | solution.py:111
  203.8 53.2 %collective-permute-start.15 = (bf16[1024,1024]{1,0:T(8,128)(2,1)}, bf16[1024,1024]{1,0:T(8,128)(2,1)}, u32[]{:S(2)}, u32[]{:S(2)}) collective-permute-start(bf16[1024,1024]{1,0:T(8,128)(2,1)} %collective-permute-done.13.refs_9_.refs_8_), channel_id=1, source_target_pairs={{0,8},{4,20},{8,0},{12,28},{16,24},{20,4},{24,16},{28,12},{1,9},{5... | collective-permute-start | bytes 6291464 | tf_op jit(solution)/shard_map/ppermute | solution.py:111
  256.9 53.9 %collective-permute-start.17 = (bf16[2,1024,1024]{2,1,0:T(8,128)(2,1)}, bf16[2,1024,1024]{2,1,0:T(8,128)(2,1)}, u32[]{:S(2)}, u32[]{:S(2)}) collective-permute-start(bf16[2,1024,1024]{2,1,0:T(8,128)(2,1)} %get-tuple-element.63), channel_id=1, source_target_pairs={{0,8},{4,20},{8,0},{12,28},{16,24},{20,4},{24,16},{28,12},{1,9},{5... | collective-permute-start | bytes 12582920 | tf_op jit(solution)/shard_map/ppermute | solution.py:111
  310.7 5.2 collective-permute-start.16
  310.8 5.1 copy-start.31
  314.0 3.5 copy-start.24
  314.0 28.0 %collective-permute-start.18 = (bf16[1,1024,1024]{2,1,0:T(8,128)(2,1)S(1)}, bf16[1,1024,1024]{2,1,0:T(8,128)(2,1)}, u32[]{:S(2)}, u32[]{:S(2)}) collective-permute-start(bf16[1,1024,1024]{2,1,0:T(8,128)(2,1)S(1)} %add_convert_fusion.4.refs_7_), channel_id=1, source_target_pairs={{0,16},{4,12},{8,24},{12,4},{16,0},{20,28},{24,8},{28,20},{1,17},{... | collective-permute-start | bytes 6291464 | tf_op jit(solution)/shard_map/ppermute | solution.py:111
  317.6 24.4 %copy-start.22 = (bf16[2,1024,1024]{2,1,0:T(8,128)(2,1)S(1)}, bf16[2,1024,1024]{2,1,0:T(8,128)(2,1)}, u32[]{:S(2)}) copy-start(bf16[2,1024,1024]{2,1,0:T(8,128)(2,1)} %get-tuple-element.62) | copy-start | bytes 12582916
  335.1 52.0 %collective-permute-start.19 = (bf16[2,1024,1024]{2,1,0:T(8,128)(2,1)}, bf16[2,1024,1024]{2,1,0:T(8,128)(2,1)}, u32[]{:S(2)}, u32[]{:S(2)}) collective-permute-start(bf16[2,1024,1024]{2,1,0:T(8,128)(2,1)} %get-tuple-element.73), channel_id=1, source_target_pairs={{0,8},{4,20},{8,0},{12,28},{16,24},{20,4},{24,16},{28,12},{1,9},{5... | collective-permute-start | bytes 12582920 | tf_op jit(solution)/shard_map/ppermute | solution.py:111
  347.6 88.5 %all-to-all-start.5 = ((bf16[4,256,1024]{2,1,0:T(8,128)(2,1)}), bf16[4,256,1024]{2,1,0:T(8,128)(2,1)}, u32[]{:S(2)}, u32[]{:S(2)}) async-start(bf16[4,256,1024]{2,1,0:T(8,128)(2,1)} %pad_maximum_fusion.2.refs_5_), calls=%async_computation.5 | async-start | bytes 4194304 | tf_op jit(solution)/shard_map/all_to_all | solution.py:143
  352.8 22.4 %copy-start.1 = (bf16[1024,1024]{1,0:T(8,128)(2,1)S(1)}, bf16[1024,1024]{1,0:T(8,128)(2,1)}, u32[]{:S(2)}) copy-start(bf16[1024,1024]{1,0:T(8,128)(2,1)} %get-tuple-element.50.refs_3_.refs_1_) | copy-start | bytes 6291460
  352.8 22.4 %copy-start.3 = (bf16[1024,512]{1,0:T(8,128)(2,1)S(1)}, bf16[1024,512]{1,0:T(8,128)(2,1)}, u32[]{:S(2)}) copy-start(bf16[1024,512]{1,0:T(8,128)(2,1)} %copy-done.2) | copy-start | bytes 3145732
  352.8 22.4 %copy-start.5 = (bf16[1024,512]{1,0:T(8,128)(2,1)S(1)}, bf16[1024,512]{1,0:T(8,128)(2,1)}, u32[]{:S(2)}) copy-start(bf16[1024,512]{1,0:T(8,128)(2,1)} %copy-done.4) | copy-start | bytes 3145732
  352.9 22.4 %copy-start.11 = (s32[12]{0:T(128)S(1)}, s32[12]{0:T(128)}, u32[]{:S(2)}) copy-start(s32[12]{0:T(128)} %pad_add_fusion.refs_0_) | copy-start | bytes 148
  375.2 11.8 %copy-start.20 = (bf16[2,1024,1024]{2,1,0:T(8,128)(2,1)S(1)}, bf16[2,1024,1024]{2,1,0:T(8,128)(2,1)}, u32[]{:S(2)}) copy-start(bf16[2,1024,1024]{2,1,0:T(8,128)(2,1)} %get-tuple-element.72) | copy-start | bytes 12582916
  387.1 30.1 %collective-permute-start.20 = (bf16[4,128,2560]{2,1,0:T(8,128)(2,1)}, bf16[4,128,2560]{2,1,0:T(8,128)(2,1)S(1)}, u32[]{:S(2)}, u32[]{:S(2)}) collective-permute-start(bf16[4,128,2560]{2,1,0:T(8,128)(2,1)} %get-tuple-element.71.refs_5_), channel_id=1, source_target_pairs={{0,4},{4,0},{1,5},{5,1},{2,6},{6,2},{3,7},{7,3},{8,12},{12,8},{9,1... | collective-permute-start | bytes 7864328 | tf_op jit(solution)/shard_map/ppermute | solution.py:88
  391.0 28.6 %collective-permute-start.21 = (bf16[1,1024,1024]{2,1,0:T(8,128)(2,1)}, bf16[1,1024,1024]{2,1,0:T(8,128)(2,1)}, u32[]{:S(2)}, u32[]{:S(2)}) collective-permute-start(bf16[1,1024,1024]{2,1,0:T(8,128)(2,1)} %add_convert_fusion.2.refs_6_), channel_id=1, source_target_pairs={{0,16},{4,12},{8,24},{12,4},{16,0},{20,28},{24,8},{28,20},{1,17},{... | collective-permute-start | bytes 6291464 | tf_op jit(solution)/shard_map/ppermute | solution.py:111
  392.7 24.5 %copy-start.23 = (bf16[4,128,2560]{2,1,0:T(8,128)(2,1)S(1)}, bf16[4,128,2560]{2,1,0:T(8,128)(2,1)}, u32[]{:S(2)}) copy-start(bf16[4,128,2560]{2,1,0:T(8,128)(2,1)} %get-tuple-element.74) | copy-start | bytes 7864324
  425.9 7.9 %copy-start.15 = (bf16[4,128,2560]{2,1,0:T(8,128)(2,1)S(1)}, bf16[4,128,2560]{2,1,0:T(8,128)(2,1)}, u32[]{:S(2)}) copy-start(bf16[4,128,2560]{2,1,0:T(8,128)(2,1)} %fusion.1.refs_3_) | copy-start | bytes 7864324
  432.9 11.6 %collective-permute-start.22 = (bf16[4,128,1536]{2,1,0:T(8,128)(2,1)S(1)}, bf16[4,128,1536]{2,1,0:T(8,128)(2,1)}, u32[]{:S(2)}, u32[]{:S(2)}) collective-permute-start(bf16[4,128,1536]{2,1,0:T(8,128)(2,1)S(1)} %get-tuple-element.76), channel_id=1, source_target_pairs={{0,4},{4,0},{1,5},{5,1},{2,6},{6,2},{3,7},{7,3},{8,12},{12,8},{9,1... | collective-permute-start | bytes 4718600 | tf_op jit(solution)/shard_map/ppermute | solution.py:88
  434.9 17.9 %collective-permute-start.23 = (bf16[2,128,2560]{2,1,0:T(8,128)(2,1)}, bf16[2,128,2560]{2,1,0:T(8,128)(2,1)}, u32[]{:S(2)}, u32[]{:S(2)}) collective-permute-start(bf16[2,128,2560]{2,1,0:T(8,128)(2,1)} %slice.267), channel_id=1, source_target_pairs={{0,8},{4,20},{8,0},{12,28},{16,24},{20,4},{24,16},{28,12},{1,9},{5... | collective-permute-start | bytes 3932168 | tf_op jit(solution)/shard_map/ppermute | solution.py:111
  439.1 53.6 %all-to-all-start.3 = ((bf16[4,256,1024]{2,1,0:T(8,128)(2,1)}), bf16[4,256,1024]{2,1,0:T(8,128)(2,1)}, u32[]{:S(2)}, u32[]{:S(2)}) async-start(bf16[4,256,1024]{2,1,0:T(8,128)(2,1)} %pad_maximum_fusion.3.refs_4_), calls=%async_computation.3 | async-start | bytes 4194304 | tf_op jit(solution)/shard_map/all_to_all | solution.py:143
  444.4 8.5 %copy-start.16 = (bf16[4,128,2560]{2,1,0:T(8,128)(2,1)S(1)}, bf16[4,128,2560]{2,1,0:T(8,128)(2,1)}, u32[]{:S(2)}) copy-start(bf16[4,128,2560]{2,1,0:T(8,128)(2,1)} %fusion.1.refs_3_) | copy-start | bytes 7864324
  446.4 8.5 %copy-start.19 = (f32[256,1024]{1,0:T(8,128)S(1)}, f32[256,1024]{1,0:T(8,128)}, u32[]{:S(2)}) copy-start(f32[256,1024]{1,0:T(8,128)} %convert_reduce_fusion) | copy-start | bytes 3145732
  446.5 19.5 %collective-permute-start.25 = (bf16[2,128,1536]{2,1,0:T(8,128)(2,1)S(1)}, bf16[2,128,1536]{2,1,0:T(8,128)(2,1)S(1)}, u32[]{:S(2)}, u32[]{:S(2)}) collective-permute-start(bf16[2,128,1536]{2,1,0:T(8,128)(2,1)S(1)} %slice.271), channel_id=1, source_target_pairs={{0,8},{4,20},{8,0},{12,28},{16,24},{20,4},{24,16},{28,12},{1,9},{5... | collective-permute-start | bytes 2359304 | tf_op jit(solution)/shard_map/ppermute | solution.py:111
  454.6 12.7 %collective-permute-start.24 = (bf16[1,128,2560]{2,1,0:T(8,128)(2,1)S(1)}, bf16[1,128,2560]{2,1,0:T(8,128)(2,1)S(1)}, u32[]{:S(2)}, u32[]{:S(2)}) collective-permute-start(bf16[1,128,2560]{2,1,0:T(8,128)(2,1)S(1)} %slice.269), channel_id=1, source_target_pairs={{0,16},{4,12},{8,24},{12,4},{16,0},{20,28},{24,8},{28,20},{1,17},{... | collective-permute-start | bytes 1966088 | tf_op jit(solution)/shard_map/ppermute | solution.py:111
  456.2 11.3 %copy-start = (bf16[3,1024,512]{2,1,0:T(8,128)(2,1)S(1)}, bf16[3,1024,512]{2,1,0:T(8,128)(2,1)}, u32[]{:S(2)}) copy-start(bf16[3,1024,512]{2,1,0:T(8,128)(2,1)} %attend_back.2.refs_5_.refs_4_) | copy-start | bytes 9437188
  456.2 11.3 %copy-start.9 = (f32[8,1024]{1,0:T(8,128)S(1)}, f32[8,1024]{1,0:T(8,128)}, u32[]{:S(2)}) copy-start(f32[8,1024]{1,0:T(8,128)} %get-tuple-element.46.refs_3_.refs_1_.refs_0_) | copy-start | bytes 98308
  466.2 15.3 %collective-permute-start.26 = (bf16[1,128,1536]{2,1,0:T(8,128)(2,1)S(1)}, bf16[1,128,1536]{2,1,0:T(8,128)(2,1)S(1)}, u32[]{:S(2)}, u32[]{:S(2)}) collective-permute-start(bf16[1,128,1536]{2,1,0:T(8,128)(2,1)S(1)} %slice.273), channel_id=1, source_target_pairs={{0,16},{4,12},{8,24},{12,4},{16,0},{20,28},{24,8},{28,20},{1,17},{... | collective-permute-start | bytes 1179656 | tf_op jit(solution)/shard_map/ppermute | solution.py:111
  497.9 25.7 %collective-permute-start.29 = (bf16[32,4096]{1,0:T(8,128)(2,1)}, bf16[32,4096]{1,0:T(8,128)(2,1)}, u32[]{:S(2)}, u32[]{:S(2)}) collective-permute-start(bf16[32,4096]{1,0:T(8,128)(2,1)} %get-tuple-element.101), channel_id=1, source_target_pairs={{0,3},{1,0},{2,1},{3,2},{4,7},{5,4},{6,5},{7,6},{8,11},{9,8},{10,9... | collective-permute-start | bytes 786440 | tf_op jit(solution)/shard_map/ppermute | solution.py:138
  499.3 24.3 %collective-permute-start.28 = (bf16[32,4096]{1,0:T(8,128)(2,1)}, bf16[32,4096]{1,0:T(8,128)(2,1)}, u32[]{:S(2)}, u32[]{:S(2)}) collective-permute-start(bf16[32,4096]{1,0:T(8,128)(2,1)} %get-tuple-element.102), channel_id=1, source_target_pairs={{0,2},{1,3},{2,0},{3,1},{4,6},{5,7},{6,4},{7,5},{8,10},{9,11},{10,... | collective-permute-start | bytes 786440 | tf_op jit(solution)/shard_map/ppermute | solution.py:138
  499.3 24.3 %collective-permute-start.27 = (bf16[32,4096]{1,0:T(8,128)(2,1)S(1)}, bf16[32,4096]{1,0:T(8,128)(2,1)}, u32[]{:S(2)}, u32[]{:S(2)}) collective-permute-start(bf16[32,4096]{1,0:T(8,128)(2,1)S(1)} %get-tuple-element.100), channel_id=1, source_target_pairs={{0,1},{1,2},{2,3},{3,0},{4,5},{5,6},{6,7},{7,4},{8,9},{9,10},{10,1... | collective-permute-start | bytes 786440 | tf_op jit(solution)/shard_map/ppermute | solution.py:138
  500.8 20.9 %all-to-all-start.4 = ((f32[32,1,128]{2,1,0:T(1,128)}), f32[32,1,128]{2,1,0:T(1,128)S(1)}, u32[]{:S(2)}, u32[]{:S(2)}) async-start(f32[32,1,128]{2,1,0:T(1,128)} %reshape.272), calls=%async_computation.4 | async-start | bytes 32768 | tf_op jit(solution)/shard_map/all_to_all | solution.py:962
  510.7 16.8 %collective-permute-start.30 = (f32[256,1024]{1,0:T(8,128)}, f32[256,1024]{1,0:T(8,128)}, u32[]{:S(2)}, u32[]{:S(2)}) collective-permute-start(f32[256,1024]{1,0:T(8,128)} %pad_maximum_fusion.4), channel_id=1, source_target_pairs={{0,4},{4,0},{1,5},{5,1},{2,6},{6,2},{3,7},{7,3},{8,12},{12,8},{9,1... | collective-permute-start | bytes 3145736 | tf_op jit(solution)/shard_map/ppermute | solution.py:88
  (10 other events, 17.6 us)

commit v3 on v2

--- a/solution.py
+++ b/solution.py
@@ -131,8 +131,8 @@
                 keep = add_low(keep[0], got[0])
         return keep
 
-    def reduce_line_direct(self, value, zed):
-        total = pick(value, zed, 0).astype(f32)
+    def reduce_line_direct(self, value, zed, hold):
+        total = after(pick(value, zed, 0).astype(f32), *hold)
         for t in range(1, self.fs):
             pairs = [(z, (z + t) % self.fs) for z in range(self.fs)]
             part = lax.ppermute(pick(value, (zed + t) % self.fs, 0), "fsdp", pairs)
@@ -516,7 +516,7 @@
         h_acc[span, :] += nt_dot(du, win_s[:, pl.ds(at, tile)])
         return carry
 
-    lax.fori_loop(0, total // block, one_block, 0)
+    lax.fori_loop(0, total // block, one_block, 0, unroll=True)
     grad = tn_dot(a_s[...], dy_s[...]).astype(bf16)
 
     for i in range(count):
@@ -934,19 +934,9 @@
     core_a = after(core_sum(made_a), grads[1])
     made_b = weights(ids, [([h1], grads[1])], chips, 0.1, [core_a, chunk_b])
     core_b = core_sum(made_b)
-    split_a, split_b = split_sum(core_a), split_sum(core_b)
+    split_a, split_b = split_sum(core_a), after(split_sum(core_b), line_b)
     ready = [rest_sum(split_a), rest_sum(split_b)]
     grad_tokens, sums_one = last(gains, tokens, grad_middle, grads, w_qkv, [core_b])
-    ready = links.reduce_line_direct(after(jnp.concatenate(ready, axis=2), line_b), zed)
-    grad_output = ready[:, :d]
-    grad_qkv = [
-        jnp.concatenate(
-            [ready[:, d + (3 * j + i) * wide : d + (3 * j + i + 1) * wide] for j in range(PARTS)],
-            axis=1,
-        )
-        for i in range(3)
-    ]
-
     ins = jnp.stack([t[: 2 * slabs * share].reshape(2, slabs * share, d) for t in (line_a, line_b)])
     outs = jnp.stack([t[2 * slabs * share :] for t in (line_a, line_b)])
     theirs = jnp.concatenate([pick(ins, 1 - core, 1).reshape(-1, d), pick(outs, 1 - core, 0)], axis=0)
@@ -956,6 +946,16 @@
     grad_expert_in = in_grad.transpose(3, 0, 2, 4, 1, 5).reshape(share, 2, hidden)
     out_grad = in_order(core, pick(outs, core, 0), got[2 * slabs * share :])
     grad_expert_out = out_grad.transpose(1, 0, 2)
+
+    ready = links.reduce_line_direct(jnp.concatenate(ready, axis=2), zed, [grad_expert_in, grad_expert_out])
+    grad_output = ready[:, :d]
+    grad_qkv = [
+        jnp.concatenate(
+            [ready[:, d + (3 * j + i) * wide : d + (3 * j + i + 1) * wide] for j in range(PARTS)],
+            axis=1,
+        )
+        for i in range(3)
+    ]
 
     sums = jnp.concatenate([sums_one[:2], sums_two[:2]]).reshape(4, devices, share).transpose(1, 0, 2)
     sums = after(sums, line_b)

time: 543 us -> 536 us (0.987)
  waiting for transfers between devices: 105 us -> 95.8 us
    ppermute x3, waiting for transfers between devices: 0.01 us -> 13.2 us  [reduce_line_direct(): part = lax.ppermute(pick(value, (zed + t) % self.fs, 0), 'fsdp', pairs)]
    all_to_all x1, waiting for transfers between devices: 10.2 us -> 0.01 us  [local(): sums = jnp.sum(lax.all_to_all(sums, links.axes + ('fsdp',), 0, 0), axis=0)]
    ppermute x17, waiting for transfers between devices: 59 us -> 49.7 us  [swap(): return lax.ppermute(value, self.axes, pairs)]
    convert_element_type x7 -> x6, other arithmetic: 11.1 us -> 10.5 us  [add_low(): return (a.astype(f32) + b.astype(f32)).astype(bf16)]
  transfers between devices with their start and end apart: 37 -> 37, of which waited for: 13 -> 11; matrix products, arithmetic and copies ran while one was open for 12% -> 14% of each run, Pallas kernels for 52% -> 52%
where the time goes in v3:
time: 536 us; the launch traced here: 529 us
  Pallas kernels  273 us (51%)
  waiting for transfers between devices  95.8 us (18%)
  other arithmetic  55.8 us (10%)
  starting transfers between devices  55.2 us (10%)
  local copies, waits for them, and re-layouts  39.9 us (7%)
  between operations  8.39 us (2%)
    pallas_call x12, Pallas kernels, run_kernel(): pl.pallas_call(body, grid_spec=spec, out_shape=out_shape + [jax.ShapeDtyp...  268 us
    ppermute x17, waiting for transfers between devices, swap(): return lax.ppermute(value, self.axes, pairs)  49.7 us
    all_to_all x3, waiting for transfers between devices, gather_line(): return lax.all_to_all(spread, 'fsdp', 0, 0)  22.9 us
    ppermute x17, starting transfers between devices, swap(): return lax.ppermute(value, self.axes, pairs)  20.4 us
    add x11, other arithmetic, after(): value = value + mark.astype(value.dtype)  15.9 us
    all_to_all x3, starting transfers between devices, gather_line(): return lax.all_to_all(spread, 'fsdp', 0, 0)  15.6 us
    ppermute x3, waiting for transfers between devices, reduce_line_direct(): part = lax.ppermute(pick(value, (zed + t) % self.fs, 0), 'fsdp', pairs)  13.2 us
  transfers between devices with their start and end apart: 37, of which 11 were waited for; matrix products, arithmetic and copies ran while one was open for 14% of the time, Pallas kernels for 52%

profile of v3, /device:TPU:0, one launch (start us, length us, event | category | flops | bytes accessed | tf_op | source)
XLA Modules:
  0.0 528.9 jit_solution(15689314652425547719)
XLA Ops:
  6.9 6.3 %all-to-all-start = ((bf16[4,32,4224]{2,1,0:T(8,128)(2,1)}), bf16[4,32,4224]{2,1,0:T(8,128)(2,1)}, u32[]{:S(2)}, u32[]{:S(2)}) async-start(bf16[4,32,4224]{2,1,0:T(8,128)(2,1)} %broadcast_in_dim.38), calls=%async_computation | async-start | bytes 2162688 | tf_op jit(solution)/shard_map/all_to_all | solution.py:115
  15.4 1.9 collective-permute-done.7
  19.0 20.8 %all-to-all-done = bf16[4,32,4224]{2,1,0:T(8,128)(2,1)} async-done(((bf16[4,32,4224]{2,1,0:T(8,128)(2,1)}), bf16[4,32,4224]{2,1,0:T(8,128)(2,1)}, u32[]{:S(2)}, u32[]{:S(2)}) %all-to-all-start) | async-done | bytes 1081376 | tf_op jit(solution)/shard_map/all_to_all | solution.py:115
  41.7 1.6 broadcast_in_dim.39
  43.3 3.8 all-to-all-start.1
  47.1 1.6 collective-permute-start
  48.8 1.5 collective-permute-start.1
  50.3 23.9 %collective-permute-done.refs_3_.refs_7_ = bf16[128,4224]{1,0:T(8,128)(2,1)} collective-permute-done((bf16[128,4224]{1,0:T(8,128)(2,1)}, bf16[128,4224]{1,0:T(8,128)(2,1)}, u32[]{:S(2)}, u32[]{:S(2)}) %collective-permute-start) | collective-permute-done | bytes 1081376 | tf_op jit(solution)/shard_map/ppermute | solution.py:111
  76.1 13.5 %collective-permute-done.2.refs_5_.refs_9_ = bf16[128,4224]{1,0:T(8,128)(2,1)} collective-permute-done((bf16[128,4224]{1,0:T(8,128)(2,1)}, bf16[128,4224]{1,0:T(8,128)(2,1)}, u32[]{:S(2)}, u32[]{:S(2)}) %collective-permute-start.2) | collective-permute-done | bytes 1081376 | tf_op jit(solution)/shard_map/ppermute | solution.py:111
  89.7 5.1 pack.1
  98.1 1.5 pad_maximum_fusion.refs_10_.refs_5_
  99.6 1.5 collective-permute-start.8
  103.0 1.6 broadcast_in_dim.83
  104.6 5.5 %all-to-all-start.2 = ((bf16[4,256,1024]{2,1,0:T(8,128)(2,1)}), bf16[4,256,1024]{2,1,0:T(8,128)(2,1)}, u32[]{:S(2)}, u32[]{:S(2)}) async-start(bf16[4,256,1024]{2,1,0:T(8,128)(2,1)} %broadcast_in_dim.83), calls=%async_computation.2 | async-start | bytes 4194304 | tf_op jit(solution)/shard_map/all_to_all | solution.py:115
  110.3 17.0 %qkv.1 = (bf16[1024,1024]{1,0:T(8,128)(2,1)}, bf16[3,1024,1024]{2,1,0:T(8,128)(2,1)}, bf16[1024,3072]{1,0:T(8,128)(2,1)}, f32[8,1024]{1,0:T(8,128)}) custom-call(s32[12]{0:T(128)} %pad_add_fusion.refs_0_, f32[1024,1024]{1,0:T(8,128)} %refs_1_.3, bf16[128,4224]{1,0:T(8,128)(2,1)} %bitcast.8.refs_2_.refs_6_, ...), custom_call_target="tpu_custom_call" | custom-call | flops 18400000000 | bytes 1048576 | tf_op jit(solution)/shard_map/qkv/pallas_call | solution.py:77
  129.1 1.8 broadcast_add_fusion.2
  131.4 1.6 collective-permute-start.12
  133.2 21.3 %attend.2 = (bf16[1024,512]{1,0:T(8,128)(2,1)S(1)}, f32[4,8,1024]{2,1,0:T(8,128)S(1)}) custom-call(s32[1024,128]{1,0:T(8,128)S(1)} %broadcast_in_dim.45.refs_0_, s32[8,1024]{1,0:T(8,128)S(1)} %broadcast_in_dim.82.refs_1_, bf16[3,1024,1024]{2,1,0:T(8,128)(2,1)} %get-tuple-element.47.refs_2_, bf16[1024,1024]{1,0:T(8,128)(2,1)} %collective-permute-done.8.refs_3_.refs_6_), custom_call_target="tpu_custom_call" | custom-call | flops 24149999616 | bytes 1048576 | tf_op jit(solution)/shard_map/attend/pallas_call | solution.py:77
  155.5 2.1 all-to-all-done.2
  157.6 1.7 broadcast_add_fusion.1
  160.4 1.5 collective-permute-start.13
  162.0 21.1 %attend.3 = (bf16[1024,512]{1,0:T(8,128)(2,1)S(1)}, f32[4,8,1024]{2,1,0:T(8,128)S(1)}) custom-call(s32[1024,128]{1,0:T(8,128)S(1)} %broadcast_in_dim.45.refs_0_, s32[8,1024]{1,0:T(8,128)S(1)} %broadcast_in_dim.82.refs_1_, bf16[3,1024,1024]{2,1,0:T(8,128)(2,1)} %get-tuple-element.47.refs_2_, f32[4,8,1024]{2,1,0:T(8,128)S(1)} %get-tuple-element.49.refs_3_.refs_4_, ...), custom_call_target="tpu_custom_call" | custom-call | flops 24149999616 | bytes 1048576 | tf_op jit(solution)/shard_map/attend/pallas_call | solution.py:77
  184.8 13.6 %mix_out.1 = (f32[1024,1024]{1,0:T(8,128)}, bf16[1024,1024]{1,0:T(8,128)(2,1)}, bf16[640,1024]{1,0:T(8,128)(2,1)}, bf16[640,1024]{1,0:T(8,128)(2,1)}) custom-call(s32[12]{0:T(128)} %pad_add_fusion.refs_0_, s32[8,1024]{1,0:T(8,128)} %copy-done.10, f32[1024,1024]{1,0:T(8,128)} %refs_1_.3, f32[8,1024]{1,0:T(8,128)} %get-tuple-element.46.refs_3_.refs_1_.refs_0_, ...), custom_call_target="tpu_custom_call" | custom-call | flops 1150000000 | bytes 1048576 | tf_op jit(solution)/shard_map/mix_out/pallas_call | solution.py:77
  198.4 3.3 collective-permute-done.13.refs_9_.refs_8_
  204.2 2.0 collective-permute-start.15
  206.2 48.2 %experts.2 = (bf16[2,640,1024]{2,1,0:T(8,128)(2,1)}, bf16[2,640,1024]{2,1,0:T(8,128)(2,1)}, bf16[2,1024,1024]{2,1,0:T(8,128)(2,1)}, bf16[2,1024,1024]{2,1,0:T(8,128)(2,1)}) custom-call(s32[12]{0:T(128)} %pad_add_fusion.refs_0_, bf16[640,1024]{1,0:T(8,128)(2,1)} %get-tuple-element.54.refs_1_, bf16[640,1024]{1,0:T(8,128)(2,1)} %collective-permute-done.10.refs_2_, ...), custom_call_target="tpu_custom_call" | custom-call | flops 60949999616 | bytes 1048576 | tf_op jit(solution)/shard_map/experts/pallas_call | solution.py:77
  254.6 51.0 %experts.3 = (bf16[2,640,1024]{2,1,0:T(8,128)(2,1)}, bf16[2,640,1024]{2,1,0:T(8,128)(2,1)}, bf16[2,1024,1024]{2,1,0:T(8,128)(2,1)}, bf16[2,1024,1024]{2,1,0:T(8,128)(2,1)}) custom-call(s32[12]{0:T(128)} %pad_add_fusion.refs_0_, bf16[640,1024]{1,0:T(8,128)(2,1)} %get-tuple-element.54.refs_1_, bf16[640,1024]{1,0:T(8,128)(2,1)} %collective-permute-done.10.refs_2_, ...), custom_call_target="tpu_custom_call" | custom-call | flops 60949999616 | bytes 1048576 | tf_op jit(solution)/shard_map/experts/pallas_call | solution.py:77
  305.7 3.2 add_convert_fusion.4.refs_7_
  308.9 1.5 collective-permute-start.18
  312.4 17.6 %combine.1 = (f32[1024,1024]{1,0:T(8,128)}, f32[1024,1024]{1,0:T(8,128)}, bf16[1024,1024]{1,0:T(8,128)(2,1)}, bf16[1024,1024]{1,0:T(8,128)(2,1)}, f32[8,1024]{1,0:T(8,128)}, /*index=5*/bf16[2,1024,1024]{2,1,0:T(8,128)(2,1)}) custom-call(s32[1024,128]{1,0:T(8,128)} %broadcast_in_dim.37.refs_0_, ...), custom_call_target="tpu_custom_call", output_to_operand_aliasing={{5}: (8, {})} | custom-call | flops 19549999104 | bytes 1048576 | tf_op jit(solution)/shard_map/combine/pallas_call | solution.py:77
  330.0 2.0 collective-permute-start.19
  333.8 2.9 collective-permute-done.18
  336.8 3.7 fusion.2
  340.8 1.5 pad_maximum_fusion.2.refs_5_
  342.3 5.1 all-to-all-start.4
  347.4 22.4 %attend_back.2.refs_5_.refs_4_ = bf16[3,1024,512]{2,1,0:T(8,128)(2,1)} custom-call(s32[1024,128]{1,0:T(8,128)} %copy-done.9, s32[8,1024]{1,0:T(8,128)} %copy-done.12, bf16[3,1024,1024]{2,1,0:T(8,128)(2,1)} %get-tuple-element.47.refs_2_, bf16[1024,1024]{1,0:T(8,128)(2,1)} %get-tuple-element.68.refs_3_, f32[4,8,1024]{2,1,0:T(8,128)} %copy-done.16, ...), custom_call_target="tpu_custom_call" | custom-call | flops 25300000768 | bytes 1048576 | tf_op jit(solution)/shard_map/attend_back/pallas_call | solution.py:77
  369.8 11.8 %weight_grads.2 = (bf16[4,128,2560]{2,1,0:T(8,128)(2,1)}, bf16[4,128,2560]{2,1,0:T(8,128)(2,1)}) custom-call(s32[12]{0:T(128)S(1)} %copy-done.13, bf16[1024,512]{1,0:T(8,128)(2,1)S(1)} %copy-done.3, bf16[1024,512]{1,0:T(8,128)(2,1)S(1)} %copy-done.5, bf16[1024,1024]{1,0:T(8,128)(2,1)S(1)} %copy-done.1, bf16[1,1024,1024]{2,1,0:T(8,128)(2,1)} %bitcast.132, ...), custom_call_target="tpu_custom_call" | custom-call | flops 115000000 | bytes 1048576 | tf_op jit(solution)/shard_map/weight_grads/pallas_call | solution.py:77
  381.6 2.6 add_convert_fusion.2.refs_6_
  384.2 1.7 collective-permute-start.21
  385.9 22.6 %attend_back.3.refs_2_.refs_5_ = bf16[3,1024,512]{2,1,0:T(8,128)(2,1)} custom-call(s32[1024,128]{1,0:T(8,128)} %copy-done.9, s32[8,1024]{1,0:T(8,128)} %copy-done.12, bf16[3,1024,1024]{2,1,0:T(8,128)(2,1)} %get-tuple-element.47.refs_2_, bf16[1024,1024]{1,0:T(8,128)(2,1)} %get-tuple-element.68.refs_3_, f32[4,8,1024]{2,1,0:T(8,128)} %copy-done.15, ...), custom_call_target="tpu_custom_call" | custom-call | flops 25300000768 | bytes 1048576 | tf_op jit(solution)/shard_map/attend_back/pallas_call | solution.py:77
  410.4 2.7 fusion.1.refs_3_
  413.1 1.3 slice.275
  414.3 1.7 collective-permute-start.23
  416.1 3.7 fusion.3
  420.1 1.5 pad_maximum_fusion.3.refs_4_
  421.5 5.5 %all-to-all-start.3 = ((bf16[4,256,1024]{2,1,0:T(8,128)(2,1)}), bf16[4,256,1024]{2,1,0:T(8,128)(2,1)}, u32[]{:S(2)}, u32[]{:S(2)}) async-start(bf16[4,256,1024]{2,1,0:T(8,128)(2,1)} %pad_maximum_fusion.3.refs_4_), calls=%async_computation.3 | async-start | bytes 4194304 | tf_op jit(solution)/shard_map/all_to_all | solution.py:143
  427.1 7.5 %weight_grads.3 = (bf16[4,128,1536]{2,1,0:T(8,128)(2,1)S(1)}, bf16[4,128,1536]{2,1,0:T(8,128)(2,1)}) custom-call(s32[12]{0:T(128)S(1)} %copy-done.13, bf16[1024,1024]{1,0:T(8,128)(2,1)S(1)} %copy-done.1, bf16[3,1024,512]{2,1,0:T(8,128)(2,1)} %attend_back.3.refs_2_.refs_5_, bf16[4,128,2560]{2,1,0:T(8,128)(2,1)} %copy-done.17, ...), custom_call_target="tpu_custom_call" | custom-call | flops 115000000 | bytes 1048576 | tf_op jit(solution)/shard_map/weight_grads/pallas_call | solution.py:77
  436.6 2.1 convert_reduce_fusion
  438.7 1.6 add_convert_fusion.6
  443.4 1.8 add_convert_fusion.5.refs_6_
  447.3 6.0 %collective-permute-done.24 = bf16[1,128,2560]{2,1,0:T(8,128)(2,1)S(1)} collective-permute-done((bf16[1,128,2560]{2,1,0:T(8,128)(2,1)S(1)}, bf16[1,128,2560]{2,1,0:T(8,128)(2,1)S(1)}, u32[]{:S(2)}, u32[]{:S(2)}) %collective-permute-start.24) | collective-permute-done | bytes 655392 | tf_op jit(solution)/shard_map/ppermute | solution.py:111
  453.6 14.0 %token_grads.1 = (f32[1024,1024]{1,0:T(8,128)}, f32[8,1024]{1,0:T(8,128)S(1)}) custom-call(f32[8,1024]{1,0:T(8,128)S(1)} %copy-done.11, f32[1024,1024]{1,0:T(8,128)} %refs_1_.3, f32[1024,1024]{1,0:T(8,128)} %get-tuple-element.66.refs_2_, bf16[1024,3072]{1,0:T(8,128)(2,1)} %get-tuple-element.67.refs_3_, bf16[3,1024,512]{2,1,0:T(8,128)(2,1)S(1)} %copy-done, ...), custom_call_target="tpu_custom_call" | custom-call | flops 1150000000 | bytes 1048576 | tf_op jit(solution)/shard_map/token_grads/pallas_call | solution.py:77
  467.6 7.6 %all-to-all-done.3 = bf16[4,256,1024]{2,1,0:T(8,128)(2,1)} async-done(((bf16[4,256,1024]{2,1,0:T(8,128)(2,1)}), bf16[4,256,1024]{2,1,0:T(8,128)(2,1)}, u32[]{:S(2)}, u32[]{:S(2)}) %all-to-all-start.3) | async-done | bytes 2097184 | tf_op jit(solution)/shard_map/all_to_all | solution.py:143
  475.2 2.1 convert_reduce_fusion.1
  479.3 1.4 fusion.7
  483.8 2.7 all-to-all-start.5
  486.5 4.2 fusion.9
  490.7 1.3 fusion.15
  497.7 3.7 collective-permute-start.30
  502.5 1.3 fusion.38
  504.1 1.5 fusion.6
  508.3 1.3 reshape.279
  511.5 13.2 %collective-permute-done.29 = bf16[32,4096]{1,0:T(8,128)(2,1)} collective-permute-done((bf16[32,4096]{1,0:T(8,128)(2,1)}, bf16[32,4096]{1,0:T(8,128)(2,1)}, u32[]{:S(2)}, u32[]{:S(2)}) %collective-permute-start.29) | collective-permute-done | bytes 262176 | tf_op jit(solution)/shard_map/ppermute | solution.py:138
  524.7 1.3 fusion.17
  (215 shorter events, 54.7 us)
Async XLA Ops:
  1.6 11.7 %copy-start.28 = (f32[32,2,4096]{2,1,0:T(2,128)S(1)}, f32[32,2,4096]{2,1,0:T(2,128)}, u32[]{:S(2)}) copy-start(f32[32,2,4096]{2,1,0:T(2,128)} %param.25) | copy-start | bytes 3145732
  6.9 32.9 %all-to-all-start = ((bf16[4,32,4224]{2,1,0:T(8,128)(2,1)}), bf16[4,32,4224]{2,1,0:T(8,128)(2,1)}, u32[]{:S(2)}, u32[]{:S(2)}) async-start(bf16[4,32,4224]{2,1,0:T(8,128)(2,1)} %broadcast_in_dim.38), calls=%async_computation | async-start | bytes 2162688 | tf_op jit(solution)/shard_map/all_to_all | solution.py:115
  15.3 2.0 collective-permute-start.7
  43.3 5.4 %copy-start.38 = (s32[1,8]{1,0:T(1,128)S(1)}, s32[1,8]{1,0:T(1,128)}, u32[]{:S(2)}) copy-start(s32[1,8]{1,0:T(1,128)} %param.27) | copy-start | bytes 100
  43.3 30.9 %copy-start.36 = (s32[2,4]{1,0:T(2,128)S(1)}, s32[2,4]{1,0:T(2,128)}, u32[]{:S(2)}) copy-start(s32[2,4]{1,0:T(2,128)} %constant.108.clone) | copy-start | bytes 100
  43.3 30.9 %copy-start.34 = (s32[1024,1]{0,1:T(1,128)S(1)}, s32[1024,1]{0,1:T(1,128)}, u32[]{:S(2)}) copy-start(s32[1024,1]{0,1:T(1,128)} %param.28) | copy-start | bytes 12292
  43.3 31.6 %copy-start.35 = (s32[1024]{0:T(1024)S(1)}, s32[1024]{0:T(1024)}, u32[]{:S(2)}) copy-start(s32[1024]{0:T(1024)} %param.29) | copy-start | bytes 12292
  43.3 54.3 %all-to-all-start.1 = ((bf16[4,256,1024]{2,1,0:T(8,128)(2,1)}), bf16[4,256,1024]{2,1,0:T(8,128)(2,1)S(1)}, u32[]{:S(2)}, u32[]{:S(2)}) async-start(bf16[4,256,1024]{2,1,0:T(8,128)(2,1)} %broadcast_in_dim.39), calls=%async_computation.1 | async-start | bytes 4194304 | tf_op jit(solution)/shard_map/all_to_all | solution.py:115
  47.1 27.1 %collective-permute-start = (bf16[128,4224]{1,0:T(8,128)(2,1)}, bf16[128,4224]{1,0:T(8,128)(2,1)}, u32[]{:S(2)}, u32[]{:S(2)}) collective-permute-start(bf16[128,4224]{1,0:T(8,128)(2,1)} %bitcast.8.refs_2_.refs_6_), channel_id=1, source_target_pairs={{0,16},{4,12},{8,24},{12,4},{16,0},{20,28},{24,8},{28,20},{1,17},{... | collective-permute-start | bytes 3244040 | tf_op jit(solution)/shard_map/ppermute | solution.py:111
  48.8 27.3 %collective-permute-start.1 = (bf16[128,4224]{1,0:T(8,128)(2,1)}, bf16[128,4224]{1,0:T(8,128)(2,1)}, u32[]{:S(2)}, u32[]{:S(2)}) collective-permute-start(bf16[128,4224]{1,0:T(8,128)(2,1)} %bitcast.8.refs_2_.refs_6_), channel_id=1, source_target_pairs={{0,8},{4,20},{8,0},{12,28},{16,24},{20,4},{24,16},{28,12},{1,9},{5... | collective-permute-start | bytes 3244040 | tf_op jit(solution)/shard_map/ppermute | solution.py:111
  74.2 15.5 %collective-permute-start.2 = (bf16[128,4224]{1,0:T(8,128)(2,1)}, bf16[128,4224]{1,0:T(8,128)(2,1)}, u32[]{:S(2)}, u32[]{:S(2)}) collective-permute-start(bf16[128,4224]{1,0:T(8,128)(2,1)} %collective-permute-done.refs_3_.refs_7_), channel_id=1, source_target_pairs={{0,8},{4,20},{8,0},{12,28},{16,24},{20,4},{24,16},{28,12},{1,9},{5... | collective-permute-start | bytes 3244040 | tf_op jit(solution)/shard_map/ppermute | solution.py:111
  75.5 34.6 %collective-permute-start.3 = (bf16[128,4224]{1,0:T(8,128)(2,1)}, bf16[128,4224]{1,0:T(8,128)(2,1)}, u32[]{:S(2)}, u32[]{:S(2)}) collective-permute-start(bf16[128,4224]{1,0:T(8,128)(2,1)} %bitcast.8.refs_2_.refs_6_), channel_id=1, source_target_pairs={{0,4},{4,0},{1,5},{5,1},{2,6},{6,2},{3,7},{7,3},{8,12},{12,8},{9,1... | collective-permute-start | bytes 3244040 | tf_op jit(solution)/shard_map/ppermute | solution.py:88
  75.5 34.7 %collective-permute-start.4 = (bf16[128,4224]{1,0:T(8,128)(2,1)}, bf16[128,4224]{1,0:T(8,128)(2,1)}, u32[]{:S(2)}, u32[]{:S(2)}) collective-permute-start(bf16[128,4224]{1,0:T(8,128)(2,1)} %collective-permute-done.refs_3_.refs_7_), channel_id=1, source_target_pairs={{0,4},{4,0},{1,5},{5,1},{2,6},{6,2},{3,7},{7,3},{8,12},{12,8},{9,1... | collective-permute-start | bytes 3244040 | tf_op jit(solution)/shard_map/ppermute | solution.py:88
  76.1 34.2 %collective-permute-start.5 = (bf16[128,4224]{1,0:T(8,128)(2,1)}, bf16[128,4224]{1,0:T(8,128)(2,1)}, u32[]{:S(2)}, u32[]{:S(2)}) collective-permute-start(bf16[128,4224]{1,0:T(8,128)(2,1)} %collective-permute-done.1.refs_4_.refs_8_), channel_id=1, source_target_pairs={{0,4},{4,0},{1,5},{5,1},{2,6},{6,2},{3,7},{7,3},{8,12},{12,8},{9,1... | collective-permute-start | bytes 3244040 | tf_op jit(solution)/shard_map/ppermute | solution.py:88
  89.7 20.6 %collective-permute-start.6 = (bf16[128,4224]{1,0:T(8,128)(2,1)}, bf16[128,4224]{1,0:T(8,128)(2,1)}, u32[]{:S(2)}, u32[]{:S(2)}) collective-permute-start(bf16[128,4224]{1,0:T(8,128)(2,1)} %collective-permute-done.2.refs_5_.refs_9_), channel_id=1, source_target_pairs={{0,4},{4,0},{1,5},{5,1},{2,6},{6,2},{3,7},{7,3},{8,12},{12,8},{9,1... | collective-permute-start | bytes 3244040 | tf_op jit(solution)/shard_map/ppermute | solution.py:88
  89.7 5.1 copy-start.10
  98.1 4.8 copy-start.31
  98.1 4.8 copy-start.32
  99.6 31.7 %collective-permute-start.8 = (bf16[1024,1024]{1,0:T(8,128)(2,1)}, bf16[1024,1024]{1,0:T(8,128)(2,1)}, u32[]{:S(2)}, u32[]{:S(2)}) collective-permute-start(bf16[1024,1024]{1,0:T(8,128)(2,1)} %pad_maximum_fusion.refs_10_.refs_5_), channel_id=1, source_target_pairs={{0,16},{4,12},{8,24},{12,4},{16,0},{20,28},{24,8},{28,20},{1,17},{... | collective-permute-start | bytes 6291464 | tf_op jit(solution)/shard_map/ppermute | solution.py:111
  104.6 52.9 %all-to-all-start.2 = ((bf16[4,256,1024]{2,1,0:T(8,128)(2,1)}), bf16[4,256,1024]{2,1,0:T(8,128)(2,1)}, u32[]{:S(2)}, u32[]{:S(2)}) async-start(bf16[4,256,1024]{2,1,0:T(8,128)(2,1)} %broadcast_in_dim.83), calls=%async_computation.2 | async-start | bytes 4194304 | tf_op jit(solution)/shard_map/all_to_all | solution.py:115
  110.1 96.0 %collective-permute-start.11 = (bf16[640,1024]{1,0:T(8,128)(2,1)S(1)}, bf16[640,1024]{1,0:T(8,128)(2,1)}, u32[]{:S(2)}, u32[]{:S(2)}) collective-permute-start(bf16[640,1024]{1,0:T(8,128)(2,1)S(1)} %get-tuple-element.57), channel_id=1, source_target_pairs={{0,4},{4,0},{1,5},{5,1},{2,6},{6,2},{3,7},{7,3},{8,12},{12,8},{9,1... | collective-permute-start | bytes 3932168 | tf_op jit(solution)/shard_map/ppermute | solution.py:88
  130.9 31.0 %collective-permute-start.9 = (bf16[1024,1024]{1,0:T(8,128)(2,1)}, bf16[1024,1024]{1,0:T(8,128)(2,1)}, u32[]{:S(2)}, u32[]{:S(2)}) collective-permute-start(bf16[1024,1024]{1,0:T(8,128)(2,1)} %broadcast_add_fusion.2), channel_id=1, source_target_pairs={{0,8},{4,20},{8,0},{12,28},{16,24},{20,4},{24,16},{28,12},{1,9},{5... | collective-permute-start | bytes 6291464 | tf_op jit(solution)/shard_map/ppermute | solution.py:111
  131.4 74.8 %collective-permute-start.12 = (bf16[1024,1024]{1,0:T(8,128)(2,1)}, bf16[1024,1024]{1,0:T(8,128)(2,1)}, u32[]{:S(2)}, u32[]{:S(2)}) collective-permute-start(bf16[1024,1024]{1,0:T(8,128)(2,1)} %collective-permute-done.8.refs_3_.refs_6_), channel_id=1, source_target_pairs={{0,8},{4,20},{8,0},{12,28},{16,24},{20,4},{24,16},{28,12},{1,9},{5... | collective-permute-start | bytes 6291464 | tf_op jit(solution)/shard_map/ppermute | solution.py:111
  133.2 28.8 %copy-start.9 = (s32[1024,128]{1,0:T(8,128)}, s32[1024,128]{1,0:T(8,128)S(1)}, u32[]{:S(2)}) copy-start(s32[1024,128]{1,0:T(8,128)S(1)} %broadcast_in_dim.45.refs_0_) | copy-start | bytes 1572868
  133.2 28.8 %copy-start.12 = (s32[8,1024]{1,0:T(8,128)}, s32[8,1024]{1,0:T(8,128)S(1)}, u32[]{:S(2)}) copy-start(s32[8,1024]{1,0:T(8,128)S(1)} %broadcast_in_dim.82.refs_1_) | copy-start | bytes 98308
  155.5 6.5 %copy-start.16 = (f32[4,8,1024]{2,1,0:T(8,128)}, f32[4,8,1024]{2,1,0:T(8,128)S(1)}, u32[]{:S(2)}) copy-start(f32[4,8,1024]{2,1,0:T(8,128)S(1)} %get-tuple-element.49.refs_3_.refs_4_) | copy-start | bytes 393220
  160.4 22.7 %copy-start.6 = (bf16[1024,1024]{1,0:T(8,128)(2,1)}, bf16[1024,1024]{1,0:T(8,128)(2,1)S(1)}, u32[]{:S(2)}) copy-start(bf16[1024,1024]{1,0:T(8,128)(2,1)S(1)} %pad_maximum_fusion.1.refs_5_.refs_7_) | copy-start | bytes 6291460
  160.4 41.3 %collective-permute-start.13 = (bf16[1024,1024]{1,0:T(8,128)(2,1)S(1)}, bf16[1024,1024]{1,0:T(8,128)(2,1)}, u32[]{:S(2)}, u32[]{:S(2)}) collective-permute-start(bf16[1024,1024]{1,0:T(8,128)(2,1)S(1)} %pad_maximum_fusion.1.refs_5_.refs_7_), channel_id=1, source_target_pairs={{0,16},{4,12},{8,24},{12,4},{16,0},{20,28},{24,8},{28,20},{1,17},{... | collective-permute-start | bytes 6291464 | tf_op jit(solution)/shard_map/ppermute | solution.py:111
  184.8 18.8 %copy-start.20 = (bf16[4,128,1024]{2,1,0:T(8,128)(2,1)S(1)}, bf16[4,128,1024]{2,1,0:T(8,128)(2,1)}, u32[]{:S(2)}) copy-start(bf16[4,128,1024]{2,1,0:T(8,128)(2,1)} %copy-done.19) | copy-start | bytes 3145732
  198.4 7.8 %collective-permute-start.10 = (bf16[640,1024]{1,0:T(8,128)(2,1)}, bf16[640,1024]{1,0:T(8,128)(2,1)}, u32[]{:S(2)}, u32[]{:S(2)}) collective-permute-start(bf16[640,1024]{1,0:T(8,128)(2,1)} %get-tuple-element.55), channel_id=1, source_target_pairs={{0,4},{4,0},{1,5},{5,1},{2,6},{6,2},{3,7},{7,3},{8,12},{12,8},{9,1... | collective-permute-start | bytes 3932168 | tf_op jit(solution)/shard_map/ppermute | solution.py:88
  204.1 50.5 %collective-permute-start.14 = (bf16[1024,1024]{1,0:T(8,128)(2,1)S(1)}, bf16[1024,1024]{1,0:T(8,128)(2,1)}, u32[]{:S(2)}, u32[]{:S(2)}) collective-permute-start(bf16[1024,1024]{1,0:T(8,128)(2,1)S(1)} %broadcast_add_fusion), channel_id=1, source_target_pairs={{0,8},{4,20},{8,0},{12,28},{16,24},{20,4},{24,16},{28,12},{1,9},{5... | collective-permute-start | bytes 6291464 | tf_op jit(solution)/shard_map/ppermute | solution.py:111
  204.2 50.4 %collective-permute-start.15 = (bf16[1024,1024]{1,0:T(8,128)(2,1)}, bf16[1024,1024]{1,0:T(8,128)(2,1)}, u32[]{:S(2)}, u32[]{:S(2)}) collective-permute-start(bf16[1024,1024]{1,0:T(8,128)(2,1)} %collective-permute-done.13.refs_9_.refs_8_), channel_id=1, source_target_pairs={{0,8},{4,20},{8,0},{12,28},{16,24},{20,4},{24,16},{28,12},{1,9},{5... | collective-permute-start | bytes 6291464 | tf_op jit(solution)/shard_map/ppermute | solution.py:111
  254.4 51.3 %collective-permute-start.17 = (bf16[2,1024,1024]{2,1,0:T(8,128)(2,1)}, bf16[2,1024,1024]{2,1,0:T(8,128)(2,1)}, u32[]{:S(2)}, u32[]{:S(2)}) collective-permute-start(bf16[2,1024,1024]{2,1,0:T(8,128)(2,1)} %get-tuple-element.63), channel_id=1, source_target_pairs={{0,8},{4,20},{8,0},{12,28},{16,24},{20,4},{24,16},{28,12},{1,9},{5... | collective-permute-start | bytes 12582920 | tf_op jit(solution)/shard_map/ppermute | solution.py:111
  305.6 5.2 collective-permute-start.16
  305.7 5.1 copy-start.33
  308.9 3.5 copy-start.25
  308.9 27.9 %collective-permute-start.18 = (bf16[1,1024,1024]{2,1,0:T(8,128)(2,1)S(1)}, bf16[1,1024,1024]{2,1,0:T(8,128)(2,1)}, u32[]{:S(2)}, u32[]{:S(2)}) collective-permute-start(bf16[1,1024,1024]{2,1,0:T(8,128)(2,1)S(1)} %add_convert_fusion.4.refs_7_), channel_id=1, source_target_pairs={{0,16},{4,12},{8,24},{12,4},{16,0},{20,28},{24,8},{28,20},{1,17},{... | collective-permute-start | bytes 6291464 | tf_op jit(solution)/shard_map/ppermute | solution.py:111
  312.4 24.3 %copy-start.23 = (bf16[2,1024,1024]{2,1,0:T(8,128)(2,1)S(1)}, bf16[2,1024,1024]{2,1,0:T(8,128)(2,1)}, u32[]{:S(2)}) copy-start(bf16[2,1024,1024]{2,1,0:T(8,128)(2,1)} %get-tuple-element.62) | copy-start | bytes 12582916
  330.0 51.6 %collective-permute-start.19 = (bf16[2,1024,1024]{2,1,0:T(8,128)(2,1)}, bf16[2,1024,1024]{2,1,0:T(8,128)(2,1)}, u32[]{:S(2)}, u32[]{:S(2)}) collective-permute-start(bf16[2,1024,1024]{2,1,0:T(8,128)(2,1)} %get-tuple-element.73), channel_id=1, source_target_pairs={{0,8},{4,20},{8,0},{12,28},{16,24},{20,4},{24,16},{28,12},{1,9},{5... | collective-permute-start | bytes 12582920 | tf_op jit(solution)/shard_map/ppermute | solution.py:111
  342.3 79.2 %all-to-all-start.4 = ((bf16[4,256,1024]{2,1,0:T(8,128)(2,1)}), bf16[4,256,1024]{2,1,0:T(8,128)(2,1)}, u32[]{:S(2)}, u32[]{:S(2)}) async-start(bf16[4,256,1024]{2,1,0:T(8,128)(2,1)} %pad_maximum_fusion.2.refs_5_), calls=%async_computation.4 | async-start | bytes 4194304 | tf_op jit(solution)/shard_map/all_to_all | solution.py:143
  347.4 22.4 %copy-start.1 = (bf16[1024,1024]{1,0:T(8,128)(2,1)S(1)}, bf16[1024,1024]{1,0:T(8,128)(2,1)}, u32[]{:S(2)}) copy-start(bf16[1024,1024]{1,0:T(8,128)(2,1)} %get-tuple-element.50.refs_3_.refs_1_) | copy-start | bytes 6291460
  347.4 22.4 %copy-start.3 = (bf16[1024,512]{1,0:T(8,128)(2,1)S(1)}, bf16[1024,512]{1,0:T(8,128)(2,1)}, u32[]{:S(2)}) copy-start(bf16[1024,512]{1,0:T(8,128)(2,1)} %copy-done.2) | copy-start | bytes 3145732
  347.4 22.4 %copy-start.5 = (bf16[1024,512]{1,0:T(8,128)(2,1)S(1)}, bf16[1024,512]{1,0:T(8,128)(2,1)}, u32[]{:S(2)}) copy-start(bf16[1024,512]{1,0:T(8,128)(2,1)} %copy-done.4) | copy-start | bytes 3145732
  347.4 22.4 %copy-start.13 = (s32[12]{0:T(128)S(1)}, s32[12]{0:T(128)}, u32[]{:S(2)}) copy-start(s32[12]{0:T(128)} %pad_add_fusion.refs_0_) | copy-start | bytes 148
  369.8 11.8 %copy-start.21 = (bf16[2,1024,1024]{2,1,0:T(8,128)(2,1)S(1)}, bf16[2,1024,1024]{2,1,0:T(8,128)(2,1)}, u32[]{:S(2)}) copy-start(bf16[2,1024,1024]{2,1,0:T(8,128)(2,1)} %get-tuple-element.72) | copy-start | bytes 12582916
  381.6 28.7 %collective-permute-start.20 = (bf16[4,128,2560]{2,1,0:T(8,128)(2,1)}, bf16[4,128,2560]{2,1,0:T(8,128)(2,1)}, u32[]{:S(2)}, u32[]{:S(2)}) collective-permute-start(bf16[4,128,2560]{2,1,0:T(8,128)(2,1)} %get-tuple-element.71.refs_5_), channel_id=1, source_target_pairs={{0,4},{4,0},{1,5},{5,1},{2,6},{6,2},{3,7},{7,3},{8,12},{12,8},{9,1... | collective-permute-start | bytes 7864328 | tf_op jit(solution)/shard_map/ppermute | solution.py:88
  384.2 31.8 %collective-permute-start.21 = (bf16[1,1024,1024]{2,1,0:T(8,128)(2,1)S(1)}, bf16[1,1024,1024]{2,1,0:T(8,128)(2,1)}, u32[]{:S(2)}, u32[]{:S(2)}) collective-permute-start(bf16[1,1024,1024]{2,1,0:T(8,128)(2,1)S(1)} %add_convert_fusion.2.refs_6_), channel_id=1, source_target_pairs={{0,16},{4,12},{8,24},{12,4},{16,0},{20,28},{24,8},{28,20},{1,17},{... | collective-permute-start | bytes 6291464 | tf_op jit(solution)/shard_map/ppermute | solution.py:111
  385.9 24.5 %copy-start.24 = (bf16[4,128,2560]{2,1,0:T(8,128)(2,1)S(1)}, bf16[4,128,2560]{2,1,0:T(8,128)(2,1)}, u32[]{:S(2)}) copy-start(bf16[4,128,2560]{2,1,0:T(8,128)(2,1)} %get-tuple-element.74) | copy-start | bytes 7864324
  410.4 5.7 %copy-start.22 = (bf16[2,1024,1024]{2,1,0:T(8,128)(2,1)S(1)}, bf16[2,1024,1024]{2,1,0:T(8,128)(2,1)}, u32[]{:S(2)}) copy-start(bf16[2,1024,1024]{2,1,0:T(8,128)(2,1)} %get-tuple-element.72) | copy-start | bytes 12582916
  413.1 6.7 %copy-start.17 = (bf16[4,128,2560]{2,1,0:T(8,128)(2,1)}, bf16[4,128,2560]{2,1,0:T(8,128)(2,1)S(1)}, u32[]{:S(2)}) copy-start(bf16[4,128,2560]{2,1,0:T(8,128)(2,1)S(1)} %fusion.1.refs_3_) | copy-start | bytes 7864324
  414.3 24.4 %collective-permute-start.23 = (bf16[2,128,2560]{2,1,0:T(8,128)(2,1)}, bf16[2,128,2560]{2,1,0:T(8,128)(2,1)}, u32[]{:S(2)}, u32[]{:S(2)}) collective-permute-start(bf16[2,128,2560]{2,1,0:T(8,128)(2,1)} %slice.275), channel_id=1, source_target_pairs={{0,8},{4,20},{8,0},{12,28},{16,24},{20,4},{24,16},{28,12},{1,9},{5... | collective-permute-start | bytes 3932168 | tf_op jit(solution)/shard_map/ppermute | solution.py:111
  421.5 53.7 %all-to-all-start.3 = ((bf16[4,256,1024]{2,1,0:T(8,128)(2,1)}), bf16[4,256,1024]{2,1,0:T(8,128)(2,1)}, u32[]{:S(2)}, u32[]{:S(2)}) async-start(bf16[4,256,1024]{2,1,0:T(8,128)(2,1)} %pad_maximum_fusion.3.refs_4_), calls=%async_computation.3 | async-start | bytes 4194304 | tf_op jit(solution)/shard_map/all_to_all | solution.py:143
  435.7 7.7 %collective-permute-start.22 = (bf16[4,128,1536]{2,1,0:T(8,128)(2,1)}, bf16[4,128,1536]{2,1,0:T(8,128)(2,1)}, u32[]{:S(2)}, u32[]{:S(2)}) collective-permute-start(bf16[4,128,1536]{2,1,0:T(8,128)(2,1)} %get-tuple-element.76), channel_id=1, source_target_pairs={{0,4},{4,0},{1,5},{5,1},{2,6},{6,2},{3,7},{7,3},{8,12},{12,8},{9,1... | collective-permute-start | bytes 4718600 | tf_op jit(solution)/shard_map/ppermute | solution.py:88
  440.4 13.0 %collective-permute-start.24 = (bf16[1,128,2560]{2,1,0:T(8,128)(2,1)S(1)}, bf16[1,128,2560]{2,1,0:T(8,128)(2,1)S(1)}, u32[]{:S(2)}, u32[]{:S(2)}) collective-permute-start(bf16[1,128,2560]{2,1,0:T(8,128)(2,1)S(1)} %slice.277), channel_id=1, source_target_pairs={{0,16},{4,12},{8,24},{12,4},{16,0},{20,28},{24,8},{28,20},{1,17},{... | collective-permute-start | bytes 1966088 | tf_op jit(solution)/shard_map/ppermute | solution.py:111
  445.2 8.4 %copy-start = (bf16[3,1024,512]{2,1,0:T(8,128)(2,1)S(1)}, bf16[3,1024,512]{2,1,0:T(8,128)(2,1)}, u32[]{:S(2)}) copy-start(bf16[3,1024,512]{2,1,0:T(8,128)(2,1)} %attend_back.2.refs_5_.refs_4_) | copy-start | bytes 9437188
  445.2 8.4 %copy-start.11 = (f32[8,1024]{1,0:T(8,128)S(1)}, f32[8,1024]{1,0:T(8,128)}, u32[]{:S(2)}) copy-start(f32[8,1024]{1,0:T(8,128)} %get-tuple-element.46.refs_3_.refs_1_.refs_0_) | copy-start | bytes 98308
  446.1 33.2 %collective-permute-start.25 = (bf16[2,128,1536]{2,1,0:T(8,128)(2,1)}, bf16[2,128,1536]{2,1,0:T(8,128)(2,1)}, u32[]{:S(2)}, u32[]{:S(2)}) collective-permute-start(bf16[2,128,1536]{2,1,0:T(8,128)(2,1)} %slice.279), channel_id=1, source_target_pairs={{0,8},{4,20},{8,0},{12,28},{16,24},{20,4},{24,16},{28,12},{1,9},{5... | collective-permute-start | bytes 2359304 | tf_op jit(solution)/shard_map/ppermute | solution.py:111
  481.5 14.2 %collective-permute-start.26 = (bf16[1,128,1536]{2,1,0:T(8,128)(2,1)}, bf16[1,128,1536]{2,1,0:T(8,128)(2,1)}, u32[]{:S(2)}, u32[]{:S(2)}) collective-permute-start(bf16[1,128,1536]{2,1,0:T(8,128)(2,1)} %slice.282), channel_id=1, source_target_pairs={{0,16},{4,12},{8,24},{12,4},{16,0},{20,28},{24,8},{28,20},{1,17},{... | collective-permute-start | bytes 1179656 | tf_op jit(solution)/shard_map/ppermute | solution.py:111
  483.8 10.0 %all-to-all-start.5 = ((f32[32,1,128]{2,1,0:T(1,128)}), f32[32,1,128]{2,1,0:T(1,128)S(1)}, u32[]{:S(2)}, u32[]{:S(2)}) async-start(f32[32,1,128]{2,1,0:T(1,128)} %reshape.280), calls=%async_computation.5 | async-start | bytes 32768 | tf_op jit(solution)/shard_map/all_to_all | solution.py:962
  493.1 9.4 %collective-permute-start.27 = (f32[256,1024]{1,0:T(8,128)}, f32[256,1024]{1,0:T(8,128)}, u32[]{:S(2)}, u32[]{:S(2)}) collective-permute-start(f32[256,1024]{1,0:T(8,128)} %pad_maximum_fusion.4), channel_id=1, source_target_pairs={{0,4},{4,0},{1,5},{5,1},{2,6},{6,2},{3,7},{7,3},{8,12},{12,8},{9,1... | collective-permute-start | bytes 3145736 | tf_op jit(solution)/shard_map/ppermute | solution.py:88
  497.7 13.7 %collective-permute-start.30 = (bf16[32,4096]{1,0:T(8,128)(2,1)}, bf16[32,4096]{1,0:T(8,128)(2,1)}, u32[]{:S(2)}, u32[]{:S(2)}) collective-permute-start(bf16[32,4096]{1,0:T(8,128)(2,1)} %get-tuple-element.102), channel_id=1, source_target_pairs={{0,3},{1,0},{2,1},{3,2},{4,7},{5,4},{6,5},{7,6},{8,11},{9,8},{10,9... | collective-permute-start | bytes 786440 | tf_op jit(solution)/shard_map/ppermute | solution.py:138
  501.4 23.3 %collective-permute-start.29 = (bf16[32,4096]{1,0:T(8,128)(2,1)}, bf16[32,4096]{1,0:T(8,128)(2,1)}, u32[]{:S(2)}, u32[]{:S(2)}) collective-permute-start(bf16[32,4096]{1,0:T(8,128)(2,1)} %get-tuple-element.101), channel_id=1, source_target_pairs={{0,2},{1,3},{2,0},{3,1},{4,6},{5,7},{6,4},{7,5},{8,10},{9,11},{10,... | collective-permute-start | bytes 786440 | tf_op jit(solution)/shard_map/ppermute | solution.py:138
  501.4 23.3 %collective-permute-start.28 = (bf16[32,4096]{1,0:T(8,128)(2,1)}, bf16[32,4096]{1,0:T(8,128)(2,1)}, u32[]{:S(2)}, u32[]{:S(2)}) collective-permute-start(bf16[32,4096]{1,0:T(8,128)(2,1)} %get-tuple-element.100), channel_id=1, source_target_pairs={{0,1},{1,2},{2,3},{3,0},{4,5},{5,6},{6,7},{7,4},{8,9},{9,10},{10,1... | collective-permute-start | bytes 786440 | tf_op jit(solution)/shard_map/ppermute | solution.py:138
  509.6 19.1 %copy-start.30 = (f32[32,2,4096]{2,1,0:T(2,128)}, f32[32,2,4096]{2,1,0:T(2,128)S(1)}, u32[]{:S(2)}) copy-start(f32[32,2,4096]{2,1,0:T(2,128)S(1)} %reshape.279) | copy-start | bytes 3145732
  (12 other events, 17.4 us)

commit v4 on v3

--- a/solution.py
+++ b/solution.py
@@ -366,17 +366,19 @@
     other[...] = nn_dot(slot_hot(slot_row[0:1, :], CAP, CAP), low).astype(bf16)
 
 
-def pack(slot_row, values):
+def pack(slot_row, values, deps):
     n, d = values.shape
-    return pl.pallas_call(
+    return run_kernel(
         pack_kernel,
+        inputs=[slot_row, values],
+        deps=deps,
         in_specs=[whole(slot_row.shape), whole((n, d))],
         out_specs=[whole((CAP, d))] * 2,
         out_shape=[jax.ShapeDtypeStruct((CAP, d), bf16)] * 2,
         compiler_params=pltpu.CompilerParams(vmem_limit_bytes=48 * MIB),
         cost_estimate=cost(0.1),
         name="pack",
-    )(slot_row, values)
+    )
 
 
 def second_kernel(ids, slot_row, tok, gains, *refs, count, rows, steps, tile, parts):
@@ -847,10 +849,11 @@
     slot_row = jnp.broadcast_to(slot[None, :], (8, n))
     slot_col = jnp.broadcast_to(slot[:, None], (n, 128))
 
-    dy_own, dy_other = pack(slot_row, cotangent)
-    dys = (dy_own, swap(dy_other, "core"))
     lines = [gather_experts(0, line, pieces[1])]
     h1, qkv, w_qkv, gains = first(ids, tokens, pieces, lines[:1])
+
+    dy_own, dy_other = pack(slot_row, cotangent, [h1])
+    dys = (dy_own, swap(dy_other, "core"))
 
     def spread_chunk(block, hold):
         pieces = [block]

time: 536 us -> 531 us (level)
    pallas_call x12 -> x13, Pallas kernels: 268 us -> 274 us  [run_kernel(): pl.pallas_call(body, grid_spec=spec, out_shape=out_shape + [jax.ShapeDtyp...]
  transfers between devices with their start and end apart: 37 -> 37, of which waited for: 11 -> 10; matrix products, arithmetic and copies ran while one was open for 14% -> 14% of each run, Pallas kernels for 52% -> 52%
where the time goes in v4:
time: 531 us; the launch traced here: 525 us
  Pallas kernels  274 us (52%)
  waiting for transfers between devices  94.3 us (18%)
  other arithmetic  55.9 us (11%)
  starting transfers between devices  52.6 us (10%)
  local copies, waits for them, and re-layouts  39.7 us (7%)
  between operations  8.44 us (2%)
    pallas_call x13, Pallas kernels, run_kernel(): pl.pallas_call(body, grid_spec=spec, out_shape=out_shape + [jax.ShapeDtyp...  274 us
    ppermute x17, waiting for transfers between devices, swap(): return lax.ppermute(value, self.axes, pairs)  46.4 us
    all_to_all x3, waiting for transfers between devices, gather_line(): return lax.all_to_all(spread, 'fsdp', 0, 0)  23.8 us
    ppermute x17, starting transfers between devices, swap(): return lax.ppermute(value, self.axes, pairs)  18.5 us
    add x11, other arithmetic, after(): value = value + mark.astype(value.dtype)  16 us
    all_to_all x3, starting transfers between devices, gather_line(): return lax.all_to_all(spread, 'fsdp', 0, 0)  14.8 us
    ppermute x3, waiting for transfers between devices, reduce_line_direct(): part = lax.ppermute(pick(value, (zed + t) % self.fs, 0), 'fsdp', pairs)  13.2 us
  transfers between devices with their start and end apart: 37, of which 10 were waited for; matrix products, arithmetic and copies ran while one was open for 14% of the time, Pallas kernels for 52%

profile of v4, /device:TPU:0, one launch (start us, length us, event | category | flops | bytes accessed | tf_op | source)
XLA Modules:
  0.0 525.2 jit_solution(7719238838425810979)
XLA Ops:
  6.9 6.3 %all-to-all-start = ((bf16[4,32,4224]{2,1,0:T(8,128)(2,1)}), bf16[4,32,4224]{2,1,0:T(8,128)(2,1)S(1)}, u32[]{:S(2)}, u32[]{:S(2)}) async-start(bf16[4,32,4224]{2,1,0:T(8,128)(2,1)} %broadcast_in_dim.38), calls=%async_computation | async-start | bytes 2162688 | tf_op jit(solution)/shard_map/all_to_all | solution.py:115
  14.8 1.5 copy.91
  16.5 1.9 collective-permute-done.7
  19.4 20.3 %all-to-all-done = bf16[4,32,4224]{2,1,0:T(8,128)(2,1)S(1)} async-done(((bf16[4,32,4224]{2,1,0:T(8,128)(2,1)}), bf16[4,32,4224]{2,1,0:T(8,128)(2,1)S(1)}, u32[]{:S(2)}, u32[]{:S(2)}) %all-to-all-start) | async-done | bytes 1081376 | tf_op jit(solution)/shard_map/all_to_all | solution.py:115
  41.0 1.6 broadcast_in_dim.39
  42.6 3.8 all-to-all-start.1
  46.4 1.6 collective-permute-start
  48.0 1.5 collective-permute-start.1
  49.5 23.7 %collective-permute-done.refs_3_.refs_7_ = bf16[128,4224]{1,0:T(8,128)(2,1)} collective-permute-done((bf16[128,4224]{1,0:T(8,128)(2,1)S(1)}, bf16[128,4224]{1,0:T(8,128)(2,1)}, u32[]{:S(2)}, u32[]{:S(2)}) %collective-permute-start) | collective-permute-done | bytes 1081376 | tf_op jit(solution)/shard_map/ppermute | solution.py:111
  75.2 13.5 %collective-permute-done.2.refs_5_.refs_9_ = bf16[128,4224]{1,0:T(8,128)(2,1)} collective-permute-done((bf16[128,4224]{1,0:T(8,128)(2,1)}, bf16[128,4224]{1,0:T(8,128)(2,1)}, u32[]{:S(2)}, u32[]{:S(2)}) %collective-permute-start.2) | collective-permute-done | bytes 1081376 | tf_op jit(solution)/shard_map/ppermute | solution.py:111
  90.5 3.5 all-to-all-done.1
  94.4 1.5 pad_maximum_fusion.refs_10_.refs_5_
  96.0 1.5 collective-permute-start.8
  99.4 1.6 broadcast_in_dim.83
  101.0 4.8 all-to-all-start.2
  105.8 17.0 %qkv.1 = (bf16[1024,1024]{1,0:T(8,128)(2,1)}, bf16[3,1024,1024]{2,1,0:T(8,128)(2,1)}, bf16[1024,3072]{1,0:T(8,128)(2,1)}, f32[8,1024]{1,0:T(8,128)}) custom-call(s32[12]{0:T(128)} %pad_add_fusion.refs_0_, f32[1024,1024]{1,0:T(8,128)} %refs_1_.5, bf16[128,4224]{1,0:T(8,128)(2,1)} %bitcast.126, bf16[128,4224]{1,0:T(8,128)(2,1)} %collective-permute-done.refs_3_.refs_7_, ...), custom_call_target="tpu_custom_call" | custom-call | flops 18400000000 | bytes 1048576 | tf_op jit(solution)/shard_map/qkv/pallas_call | solution.py:77
  122.8 1.2 slice.199
  124.7 1.8 broadcast_add_fusion.2
  126.5 1.5 collective-permute-start.9
  128.0 5.1 pack.1
  134.9 21.3 %attend.2 = (bf16[1024,512]{1,0:T(8,128)(2,1)S(1)}, f32[4,8,1024]{2,1,0:T(8,128)S(1)}) custom-call(s32[1024,128]{1,0:T(8,128)S(1)} %broadcast_in_dim.45.refs_0_, s32[8,1024]{1,0:T(8,128)S(1)} %broadcast_in_dim.82.refs_1_, bf16[3,1024,1024]{2,1,0:T(8,128)(2,1)} %get-tuple-element.47.refs_2_, bf16[1024,1024]{1,0:T(8,128)(2,1)} %collective-permute-done.8.refs_3_.refs_6_), custom_call_target="tpu_custom_call" | custom-call | flops 24149999616 | bytes 1048576 | tf_op jit(solution)/shard_map/attend/pallas_call | solution.py:77
  157.2 1.8 broadcast_add_fusion.1
  160.6 21.7 %attend.3 = (bf16[1024,512]{1,0:T(8,128)(2,1)S(1)}, f32[4,8,1024]{2,1,0:T(8,128)S(1)}) custom-call(s32[1024,128]{1,0:T(8,128)S(1)} %broadcast_in_dim.45.refs_0_, s32[8,1024]{1,0:T(8,128)S(1)} %broadcast_in_dim.82.refs_1_, bf16[3,1024,1024]{2,1,0:T(8,128)(2,1)} %get-tuple-element.47.refs_2_, f32[4,8,1024]{2,1,0:T(8,128)S(1)} %get-tuple-element.49.refs_3_.refs_4_, ...), custom_call_target="tpu_custom_call" | custom-call | flops 24149999616 | bytes 1048576 | tf_op jit(solution)/shard_map/attend/pallas_call | solution.py:77
  184.0 13.4 %mix_out.1 = (f32[1024,1024]{1,0:T(8,128)}, bf16[1024,1024]{1,0:T(8,128)(2,1)}, bf16[640,1024]{1,0:T(8,128)(2,1)}, bf16[640,1024]{1,0:T(8,128)(2,1)}) custom-call(s32[12]{0:T(128)} %pad_add_fusion.refs_0_, s32[8,1024]{1,0:T(8,128)} %copy-done.11, f32[1024,1024]{1,0:T(8,128)} %refs_1_.5, f32[8,1024]{1,0:T(8,128)} %get-tuple-element.46.refs_3_.refs_1_.refs_0_, ...), custom_call_target="tpu_custom_call" | custom-call | flops 1150000000 | bytes 1048576 | tf_op jit(solution)/shard_map/mix_out/pallas_call | solution.py:77
  199.8 1.6 collective-permute-start.14
  201.9 48.3 %experts.2 = (bf16[2,640,1024]{2,1,0:T(8,128)(2,1)}, bf16[2,640,1024]{2,1,0:T(8,128)(2,1)}, bf16[2,1024,1024]{2,1,0:T(8,128)(2,1)}, bf16[2,1024,1024]{2,1,0:T(8,128)(2,1)}) custom-call(s32[12]{0:T(128)} %pad_add_fusion.refs_0_, bf16[640,1024]{1,0:T(8,128)(2,1)} %get-tuple-element.54.refs_1_, bf16[640,1024]{1,0:T(8,128)(2,1)} %collective-permute-done.10.refs_2_, ...), custom_call_target="tpu_custom_call" | custom-call | flops 60949999616 | bytes 1048576 | tf_op jit(solution)/shard_map/experts/pallas_call | solution.py:77
  250.2 1.7 collective-permute-start.17
  251.9 50.8 %experts.3 = (bf16[2,640,1024]{2,1,0:T(8,128)(2,1)}, bf16[2,640,1024]{2,1,0:T(8,128)(2,1)}, bf16[2,1024,1024]{2,1,0:T(8,128)(2,1)}, bf16[2,1024,1024]{2,1,0:T(8,128)(2,1)}) custom-call(s32[12]{0:T(128)} %pad_add_fusion.refs_0_, bf16[640,1024]{1,0:T(8,128)(2,1)} %get-tuple-element.54.refs_1_, bf16[640,1024]{1,0:T(8,128)(2,1)} %collective-permute-done.10.refs_2_, ...), custom_call_target="tpu_custom_call" | custom-call | flops 60949999616 | bytes 1048576 | tf_op jit(solution)/shard_map/experts/pallas_call | solution.py:77
  302.8 3.2 add_convert_fusion.4.refs_7_
  306.0 1.6 collective-permute-start.18
  309.6 18.0 %combine.1 = (f32[1024,1024]{1,0:T(8,128)}, f32[1024,1024]{1,0:T(8,128)}, bf16[1024,1024]{1,0:T(8,128)(2,1)}, bf16[1024,1024]{1,0:T(8,128)(2,1)}, f32[8,1024]{1,0:T(8,128)}, /*index=5*/bf16[2,1024,1024]{2,1,0:T(8,128)(2,1)}) custom-call(s32[1024,128]{1,0:T(8,128)} %broadcast_in_dim.37.refs_0_, ...), custom_call_target="tpu_custom_call", output_to_operand_aliasing={{5}: (8, {})} | custom-call | flops 19549999104 | bytes 1048576 | tf_op jit(solution)/shard_map/combine/pallas_call | solution.py:77
  330.2 3.5 collective-permute-done.18
  333.7 3.7 fusion.2
  337.7 1.5 pad_maximum_fusion.2.refs_5_
  339.3 5.0 all-to-all-start.4
  344.3 22.3 %attend_back.2.refs_5_.refs_4_ = bf16[3,1024,512]{2,1,0:T(8,128)(2,1)} custom-call(s32[1024,128]{1,0:T(8,128)} %copy-done.10, s32[8,1024]{1,0:T(8,128)} %copy-done.13, bf16[3,1024,1024]{2,1,0:T(8,128)(2,1)} %get-tuple-element.47.refs_2_, bf16[1024,1024]{1,0:T(8,128)(2,1)} %get-tuple-element.68.refs_3_, f32[4,8,1024]{2,1,0:T(8,128)} %copy-done.17, ...), custom_call_target="tpu_custom_call" | custom-call | flops 25300000768 | bytes 1048576 | tf_op jit(solution)/shard_map/attend_back/pallas_call | solution.py:77
  366.7 11.8 %weight_grads.2 = (bf16[4,128,2560]{2,1,0:T(8,128)(2,1)}, bf16[4,128,2560]{2,1,0:T(8,128)(2,1)}) custom-call(s32[12]{0:T(128)S(1)} %copy-done.14, bf16[1024,512]{1,0:T(8,128)(2,1)S(1)} %copy-done.4, bf16[1024,512]{1,0:T(8,128)(2,1)S(1)} %copy-done.6, bf16[1024,1024]{1,0:T(8,128)(2,1)S(1)} %copy-done.1, bf16[1,1024,1024]{2,1,0:T(8,128)(2,1)} %bitcast.138, ...), custom_call_target="tpu_custom_call" | custom-call | flops 115000000 | bytes 1048576 | tf_op jit(solution)/shard_map/weight_grads/pallas_call | solution.py:77
  378.6 2.6 add_convert_fusion.2.refs_6_
  381.1 1.6 collective-permute-start.21
  382.8 22.6 %attend_back.3.refs_2_.refs_5_ = bf16[3,1024,512]{2,1,0:T(8,128)(2,1)} custom-call(s32[1024,128]{1,0:T(8,128)} %copy-done.10, s32[8,1024]{1,0:T(8,128)} %copy-done.13, bf16[3,1024,1024]{2,1,0:T(8,128)(2,1)} %get-tuple-element.47.refs_2_, bf16[1024,1024]{1,0:T(8,128)(2,1)} %get-tuple-element.68.refs_3_, f32[4,8,1024]{2,1,0:T(8,128)} %copy-done.16, ...), custom_call_target="tpu_custom_call" | custom-call | flops 25300000768 | bytes 1048576 | tf_op jit(solution)/shard_map/attend_back/pallas_call | solution.py:77
  407.2 2.7 fusion.1.refs_3_
  409.9 1.3 slice.275
  412.2 3.7 fusion.3
  416.2 1.5 pad_maximum_fusion.3.refs_4_
  417.6 5.3 %all-to-all-start.3 = ((bf16[4,256,1024]{2,1,0:T(8,128)(2,1)}), bf16[4,256,1024]{2,1,0:T(8,128)(2,1)}, u32[]{:S(2)}, u32[]{:S(2)}) async-start(bf16[4,256,1024]{2,1,0:T(8,128)(2,1)} %pad_maximum_fusion.3.refs_4_), calls=%async_computation.3 | async-start | bytes 4194304 | tf_op jit(solution)/shard_map/all_to_all | solution.py:143
  423.0 7.5 %weight_grads.3 = (bf16[4,128,1536]{2,1,0:T(8,128)(2,1)S(1)}, bf16[4,128,1536]{2,1,0:T(8,128)(2,1)}) custom-call(s32[12]{0:T(128)S(1)} %copy-done.14, bf16[1024,1024]{1,0:T(8,128)(2,1)S(1)} %copy-done.1, bf16[3,1024,512]{2,1,0:T(8,128)(2,1)} %attend_back.3.refs_2_.refs_5_, bf16[4,128,2560]{2,1,0:T(8,128)(2,1)} %copy-done.18, ...), custom_call_target="tpu_custom_call" | custom-call | flops 115000000 | bytes 1048576 | tf_op jit(solution)/shard_map/weight_grads/pallas_call | solution.py:77
  432.7 2.1 convert_reduce_fusion
  434.8 1.6 add_convert_fusion.6
  439.3 1.8 add_convert_fusion.5.refs_6_
  442.1 1.4 collective-permute-start.25
  443.5 5.6 %collective-permute-done.24 = bf16[1,128,2560]{2,1,0:T(8,128)(2,1)S(1)} collective-permute-done((bf16[1,128,2560]{2,1,0:T(8,128)(2,1)S(1)}, bf16[1,128,2560]{2,1,0:T(8,128)(2,1)S(1)}, u32[]{:S(2)}, u32[]{:S(2)}) %collective-permute-start.24) | collective-permute-done | bytes 655392 | tf_op jit(solution)/shard_map/ppermute | solution.py:111
  449.3 14.0 %token_grads.1 = (f32[1024,1024]{1,0:T(8,128)}, f32[8,1024]{1,0:T(8,128)S(1)}) custom-call(f32[8,1024]{1,0:T(8,128)S(1)} %copy-done.12, f32[1024,1024]{1,0:T(8,128)} %refs_1_.5, f32[1024,1024]{1,0:T(8,128)} %get-tuple-element.66.refs_2_, bf16[1024,3072]{1,0:T(8,128)(2,1)} %get-tuple-element.67.refs_3_, bf16[3,1024,512]{2,1,0:T(8,128)(2,1)S(1)} %copy-done.2, ...), custom_call_target="tpu_custom_call" | custom-call | flops 1150000000 | bytes 1048576 | tf_op jit(solution)/shard_map/token_grads/pallas_call | solution.py:77
  463.3 8.6 %all-to-all-done.3 = bf16[4,256,1024]{2,1,0:T(8,128)(2,1)} async-done(((bf16[4,256,1024]{2,1,0:T(8,128)(2,1)}), bf16[4,256,1024]{2,1,0:T(8,128)(2,1)}, u32[]{:S(2)}, u32[]{:S(2)}) %all-to-all-start.3) | async-done | bytes 2097184 | tf_op jit(solution)/shard_map/all_to_all | solution.py:143
  471.8 2.1 convert_reduce_fusion.1
  476.0 1.4 fusion.7
  479.8 2.8 all-to-all-start.5
  482.7 4.2 fusion.9
  486.9 1.3 fusion.15
  493.9 3.8 collective-permute-start.30
  498.7 1.3 fusion.38
  500.4 1.5 fusion.6
  504.6 1.3 reshape.279
  507.7 13.2 %collective-permute-done.29 = bf16[32,4096]{1,0:T(8,128)(2,1)} collective-permute-done((bf16[32,4096]{1,0:T(8,128)(2,1)}, bf16[32,4096]{1,0:T(8,128)(2,1)}, u32[]{:S(2)}, u32[]{:S(2)}) %collective-permute-start.29) | collective-permute-done | bytes 262176 | tf_op jit(solution)/shard_map/ppermute | solution.py:138
  521.0 1.3 fusion.17
  (215 shorter events, 52.5 us)
Async XLA Ops:
  1.6 11.7 %copy-start.30 = (f32[32,2,4096]{2,1,0:T(2,128)S(1)}, f32[32,2,4096]{2,1,0:T(2,128)}, u32[]{:S(2)}) copy-start(f32[32,2,4096]{2,1,0:T(2,128)} %param.25) | copy-start | bytes 3145732
  6.9 32.7 %all-to-all-start = ((bf16[4,32,4224]{2,1,0:T(8,128)(2,1)}), bf16[4,32,4224]{2,1,0:T(8,128)(2,1)S(1)}, u32[]{:S(2)}, u32[]{:S(2)}) async-start(bf16[4,32,4224]{2,1,0:T(8,128)(2,1)} %broadcast_in_dim.38), calls=%async_computation | async-start | bytes 2162688 | tf_op jit(solution)/shard_map/all_to_all | solution.py:115
  16.4 2.0 collective-permute-start.7
  39.7 34.9 %copy-start.22 = (bf16[4,32,4224]{2,1,0:T(8,128)(2,1)}, bf16[4,32,4224]{2,1,0:T(8,128)(2,1)S(1)}, u32[]{:S(2)}) copy-start(bf16[4,32,4224]{2,1,0:T(8,128)(2,1)S(1)} %all-to-all-done) | copy-start | bytes 3244036
  42.6 5.4 %copy-start.38 = (s32[1,8]{1,0:T(1,128)S(1)}, s32[1,8]{1,0:T(1,128)}, u32[]{:S(2)}) copy-start(s32[1,8]{1,0:T(1,128)} %param.27) | copy-start | bytes 100
  42.6 30.6 %copy-start.36 = (s32[2,4]{1,0:T(2,128)S(1)}, s32[2,4]{1,0:T(2,128)}, u32[]{:S(2)}) copy-start(s32[2,4]{1,0:T(2,128)} %constant.108.clone) | copy-start | bytes 100
  42.6 30.7 %copy-start.34 = (s32[1024,1]{0,1:T(1,128)S(1)}, s32[1024,1]{0,1:T(1,128)}, u32[]{:S(2)}) copy-start(s32[1024,1]{0,1:T(1,128)} %param.28) | copy-start | bytes 12292
  42.6 31.3 %copy-start.35 = (s32[1024]{0:T(1024)S(1)}, s32[1024]{0:T(1024)}, u32[]{:S(2)}) copy-start(s32[1024]{0:T(1024)} %param.29) | copy-start | bytes 12292
  42.6 51.4 %all-to-all-start.1 = ((bf16[4,256,1024]{2,1,0:T(8,128)(2,1)}), bf16[4,256,1024]{2,1,0:T(8,128)(2,1)S(1)}, u32[]{:S(2)}, u32[]{:S(2)}) async-start(bf16[4,256,1024]{2,1,0:T(8,128)(2,1)} %broadcast_in_dim.39), calls=%async_computation.1 | async-start | bytes 4194304 | tf_op jit(solution)/shard_map/all_to_all | solution.py:115
  46.4 26.9 %collective-permute-start = (bf16[128,4224]{1,0:T(8,128)(2,1)S(1)}, bf16[128,4224]{1,0:T(8,128)(2,1)}, u32[]{:S(2)}, u32[]{:S(2)}) collective-permute-start(bf16[128,4224]{1,0:T(8,128)(2,1)S(1)} %bitcast.123), channel_id=1, source_target_pairs={{0,16},{4,12},{8,24},{12,4},{16,0},{20,28},{24,8},{28,20},{1,17},{... | collective-permute-start | bytes 3244040 | tf_op jit(solution)/shard_map/ppermute | solution.py:111
  48.0 27.1 %collective-permute-start.1 = (bf16[128,4224]{1,0:T(8,128)(2,1)S(1)}, bf16[128,4224]{1,0:T(8,128)(2,1)}, u32[]{:S(2)}, u32[]{:S(2)}) collective-permute-start(bf16[128,4224]{1,0:T(8,128)(2,1)S(1)} %bitcast.124), channel_id=1, source_target_pairs={{0,8},{4,20},{8,0},{12,28},{16,24},{20,4},{24,16},{28,12},{1,9},{5... | collective-permute-start | bytes 3244040 | tf_op jit(solution)/shard_map/ppermute | solution.py:111
  73.2 15.5 %collective-permute-start.2 = (bf16[128,4224]{1,0:T(8,128)(2,1)}, bf16[128,4224]{1,0:T(8,128)(2,1)}, u32[]{:S(2)}, u32[]{:S(2)}) collective-permute-start(bf16[128,4224]{1,0:T(8,128)(2,1)} %collective-permute-done.refs_3_.refs_7_), channel_id=1, source_target_pairs={{0,8},{4,20},{8,0},{12,28},{16,24},{20,4},{24,16},{28,12},{1,9},{5... | collective-permute-start | bytes 3244040 | tf_op jit(solution)/shard_map/ppermute | solution.py:111
  74.6 31.2 %collective-permute-start.3 = (bf16[128,4224]{1,0:T(8,128)(2,1)S(1)}, bf16[128,4224]{1,0:T(8,128)(2,1)}, u32[]{:S(2)}, u32[]{:S(2)}) collective-permute-start(bf16[128,4224]{1,0:T(8,128)(2,1)S(1)} %bitcast.125), channel_id=1, source_target_pairs={{0,4},{4,0},{1,5},{5,1},{2,6},{6,2},{3,7},{7,3},{8,12},{12,8},{9,1... | collective-permute-start | bytes 3244040 | tf_op jit(solution)/shard_map/ppermute | solution.py:88
  74.6 31.2 %collective-permute-start.4 = (bf16[128,4224]{1,0:T(8,128)(2,1)}, bf16[128,4224]{1,0:T(8,128)(2,1)}, u32[]{:S(2)}, u32[]{:S(2)}) collective-permute-start(bf16[128,4224]{1,0:T(8,128)(2,1)} %collective-permute-done.refs_3_.refs_7_), channel_id=1, source_target_pairs={{0,4},{4,0},{1,5},{5,1},{2,6},{6,2},{3,7},{7,3},{8,12},{12,8},{9,1... | collective-permute-start | bytes 3244040 | tf_op jit(solution)/shard_map/ppermute | solution.py:88
  75.1 30.7 %collective-permute-start.5 = (bf16[128,4224]{1,0:T(8,128)(2,1)}, bf16[128,4224]{1,0:T(8,128)(2,1)}, u32[]{:S(2)}, u32[]{:S(2)}) collective-permute-start(bf16[128,4224]{1,0:T(8,128)(2,1)} %collective-permute-done.1.refs_4_.refs_8_), channel_id=1, source_target_pairs={{0,4},{4,0},{1,5},{5,1},{2,6},{6,2},{3,7},{7,3},{8,12},{12,8},{9,1... | collective-permute-start | bytes 3244040 | tf_op jit(solution)/shard_map/ppermute | solution.py:88
  88.7 17.1 %collective-permute-start.6 = (bf16[128,4224]{1,0:T(8,128)(2,1)}, bf16[128,4224]{1,0:T(8,128)(2,1)}, u32[]{:S(2)}, u32[]{:S(2)}) collective-permute-start(bf16[128,4224]{1,0:T(8,128)(2,1)} %collective-permute-done.2.refs_5_.refs_9_), channel_id=1, source_target_pairs={{0,4},{4,0},{1,5},{5,1},{2,6},{6,2},{3,7},{7,3},{8,12},{12,8},{9,1... | collective-permute-start | bytes 3244040 | tf_op jit(solution)/shard_map/ppermute | solution.py:88
  94.4 4.8 copy-start.32
  96.0 38.2 %collective-permute-start.8 = (bf16[1024,1024]{1,0:T(8,128)(2,1)}, bf16[1024,1024]{1,0:T(8,128)(2,1)}, u32[]{:S(2)}, u32[]{:S(2)}) collective-permute-start(bf16[1024,1024]{1,0:T(8,128)(2,1)} %pad_maximum_fusion.refs_10_.refs_5_), channel_id=1, source_target_pairs={{0,16},{4,12},{8,24},{12,4},{16,0},{20,28},{24,8},{28,20},{1,17},{... | collective-permute-start | bytes 6291464 | tf_op jit(solution)/shard_map/ppermute | solution.py:111
  101.0 56.2 %all-to-all-start.2 = ((bf16[4,256,1024]{2,1,0:T(8,128)(2,1)}), bf16[4,256,1024]{2,1,0:T(8,128)(2,1)}, u32[]{:S(2)}, u32[]{:S(2)}) async-start(bf16[4,256,1024]{2,1,0:T(8,128)(2,1)} %broadcast_in_dim.83), calls=%async_computation.2 | async-start | bytes 4194304 | tf_op jit(solution)/shard_map/all_to_all | solution.py:115
  126.5 34.1 %collective-permute-start.9 = (bf16[1024,1024]{1,0:T(8,128)(2,1)}, bf16[1024,1024]{1,0:T(8,128)(2,1)}, u32[]{:S(2)}, u32[]{:S(2)}) collective-permute-start(bf16[1024,1024]{1,0:T(8,128)(2,1)} %broadcast_add_fusion.2), channel_id=1, source_target_pairs={{0,8},{4,20},{8,0},{12,28},{16,24},{20,4},{24,16},{28,12},{1,9},{5... | collective-permute-start | bytes 6291464 | tf_op jit(solution)/shard_map/ppermute | solution.py:111
  128.0 5.1 copy-start.11
  134.2 67.8 %collective-permute-start.11 = (bf16[640,1024]{1,0:T(8,128)(2,1)S(1)}, bf16[640,1024]{1,0:T(8,128)(2,1)}, u32[]{:S(2)}, u32[]{:S(2)}) collective-permute-start(bf16[640,1024]{1,0:T(8,128)(2,1)S(1)} %get-tuple-element.57), channel_id=1, source_target_pairs={{0,4},{4,0},{1,5},{5,1},{2,6},{6,2},{3,7},{7,3},{8,12},{12,8},{9,1... | collective-permute-start | bytes 3932168 | tf_op jit(solution)/shard_map/ppermute | solution.py:88
  134.2 67.7 %collective-permute-start.12 = (bf16[1024,1024]{1,0:T(8,128)(2,1)}, bf16[1024,1024]{1,0:T(8,128)(2,1)}, u32[]{:S(2)}, u32[]{:S(2)}) collective-permute-start(bf16[1024,1024]{1,0:T(8,128)(2,1)} %collective-permute-done.8.refs_3_.refs_6_), channel_id=1, source_target_pairs={{0,8},{4,20},{8,0},{12,28},{16,24},{20,4},{24,16},{28,12},{1,9},{5... | collective-permute-start | bytes 6291464 | tf_op jit(solution)/shard_map/ppermute | solution.py:111
  134.9 25.8 %copy-start.10 = (s32[1024,128]{1,0:T(8,128)}, s32[1024,128]{1,0:T(8,128)S(1)}, u32[]{:S(2)}) copy-start(s32[1024,128]{1,0:T(8,128)S(1)} %broadcast_in_dim.45.refs_0_) | copy-start | bytes 1572868
  134.9 25.7 %copy-start.13 = (s32[8,1024]{1,0:T(8,128)}, s32[8,1024]{1,0:T(8,128)S(1)}, u32[]{:S(2)}) copy-start(s32[8,1024]{1,0:T(8,128)S(1)} %broadcast_in_dim.82.refs_1_) | copy-start | bytes 98308
  157.2 3.4 copy-start.17
  160.1 22.2 %copy-start.7 = (bf16[1024,1024]{1,0:T(8,128)(2,1)}, bf16[1024,1024]{1,0:T(8,128)(2,1)S(1)}, u32[]{:S(2)}) copy-start(bf16[1024,1024]{1,0:T(8,128)(2,1)S(1)} %pad_maximum_fusion.1.refs_5_.refs_7_) | copy-start | bytes 6291460
  160.1 37.3 %collective-permute-start.13 = (bf16[1024,1024]{1,0:T(8,128)(2,1)S(1)}, bf16[1024,1024]{1,0:T(8,128)(2,1)}, u32[]{:S(2)}, u32[]{:S(2)}) collective-permute-start(bf16[1024,1024]{1,0:T(8,128)(2,1)S(1)} %pad_maximum_fusion.1.refs_5_.refs_7_), channel_id=1, source_target_pairs={{0,16},{4,12},{8,24},{12,4},{16,0},{20,28},{24,8},{28,20},{1,17},{... | collective-permute-start | bytes 6291464 | tf_op jit(solution)/shard_map/ppermute | solution.py:111
  184.0 15.3 %copy-start.21 = (bf16[4,128,1024]{2,1,0:T(8,128)(2,1)S(1)}, bf16[4,128,1024]{2,1,0:T(8,128)(2,1)}, u32[]{:S(2)}) copy-start(bf16[4,128,1024]{2,1,0:T(8,128)(2,1)} %copy-done.20) | copy-start | bytes 3145732
  197.4 4.5 collective-permute-start.10
  199.8 52.1 %collective-permute-start.14 = (bf16[1024,1024]{1,0:T(8,128)(2,1)S(1)}, bf16[1024,1024]{1,0:T(8,128)(2,1)}, u32[]{:S(2)}, u32[]{:S(2)}) collective-permute-start(bf16[1024,1024]{1,0:T(8,128)(2,1)S(1)} %broadcast_add_fusion), channel_id=1, source_target_pairs={{0,8},{4,20},{8,0},{12,28},{16,24},{20,4},{24,16},{28,12},{1,9},{5... | collective-permute-start | bytes 6291464 | tf_op jit(solution)/shard_map/ppermute | solution.py:111
  201.4 50.5 %collective-permute-start.15 = (bf16[1024,1024]{1,0:T(8,128)(2,1)}, bf16[1024,1024]{1,0:T(8,128)(2,1)}, u32[]{:S(2)}, u32[]{:S(2)}) collective-permute-start(bf16[1024,1024]{1,0:T(8,128)(2,1)} %collective-permute-done.13.refs_9_.refs_8_), channel_id=1, source_target_pairs={{0,8},{4,20},{8,0},{12,28},{16,24},{20,4},{24,16},{28,12},{1,9},{5... | collective-permute-start | bytes 6291464 | tf_op jit(solution)/shard_map/ppermute | solution.py:111
  250.2 52.6 %collective-permute-start.17 = (bf16[2,1024,1024]{2,1,0:T(8,128)(2,1)}, bf16[2,1024,1024]{2,1,0:T(8,128)(2,1)}, u32[]{:S(2)}, u32[]{:S(2)}) collective-permute-start(bf16[2,1024,1024]{2,1,0:T(8,128)(2,1)} %get-tuple-element.63), channel_id=1, source_target_pairs={{0,8},{4,20},{8,0},{12,28},{16,24},{20,4},{24,16},{28,12},{1,9},{5... | collective-permute-start | bytes 12582920 | tf_op jit(solution)/shard_map/ppermute | solution.py:111
  302.7 5.2 collective-permute-start.16
  302.8 5.1 copy-start.33
  306.0 3.5 copy-start.27
  306.0 27.7 %collective-permute-start.18 = (bf16[1,1024,1024]{2,1,0:T(8,128)(2,1)S(1)}, bf16[1,1024,1024]{2,1,0:T(8,128)(2,1)}, u32[]{:S(2)}, u32[]{:S(2)}) collective-permute-start(bf16[1,1024,1024]{2,1,0:T(8,128)(2,1)S(1)} %add_convert_fusion.4.refs_7_), channel_id=1, source_target_pairs={{0,16},{4,12},{8,24},{12,4},{16,0},{20,28},{24,8},{28,20},{1,17},{... | collective-permute-start | bytes 6291464 | tf_op jit(solution)/shard_map/ppermute | solution.py:111
  309.6 24.2 %copy-start.25 = (bf16[2,1024,1024]{2,1,0:T(8,128)(2,1)S(1)}, bf16[2,1024,1024]{2,1,0:T(8,128)(2,1)}, u32[]{:S(2)}) copy-start(bf16[2,1024,1024]{2,1,0:T(8,128)(2,1)} %get-tuple-element.62) | copy-start | bytes 12582916
  327.5 51.0 %collective-permute-start.19 = (bf16[2,1024,1024]{2,1,0:T(8,128)(2,1)}, bf16[2,1024,1024]{2,1,0:T(8,128)(2,1)}, u32[]{:S(2)}, u32[]{:S(2)}) collective-permute-start(bf16[2,1024,1024]{2,1,0:T(8,128)(2,1)} %get-tuple-element.73), channel_id=1, source_target_pairs={{0,8},{4,20},{8,0},{12,28},{16,24},{20,4},{24,16},{28,12},{1,9},{5... | collective-permute-start | bytes 12582920 | tf_op jit(solution)/shard_map/ppermute | solution.py:111
  339.3 78.4 %all-to-all-start.4 = ((bf16[4,256,1024]{2,1,0:T(8,128)(2,1)}), bf16[4,256,1024]{2,1,0:T(8,128)(2,1)}, u32[]{:S(2)}, u32[]{:S(2)}) async-start(bf16[4,256,1024]{2,1,0:T(8,128)(2,1)} %pad_maximum_fusion.2.refs_5_), calls=%async_computation.4 | async-start | bytes 4194304 | tf_op jit(solution)/shard_map/all_to_all | solution.py:143
  344.3 22.4 %copy-start.1 = (bf16[1024,1024]{1,0:T(8,128)(2,1)S(1)}, bf16[1024,1024]{1,0:T(8,128)(2,1)}, u32[]{:S(2)}) copy-start(bf16[1024,1024]{1,0:T(8,128)(2,1)} %get-tuple-element.50.refs_2_.refs_3_.refs_1_) | copy-start | bytes 6291460
  344.3 22.4 %copy-start.4 = (bf16[1024,512]{1,0:T(8,128)(2,1)S(1)}, bf16[1024,512]{1,0:T(8,128)(2,1)}, u32[]{:S(2)}) copy-start(bf16[1024,512]{1,0:T(8,128)(2,1)} %copy-done.3) | copy-start | bytes 3145732
  344.3 22.4 %copy-start.6 = (bf16[1024,512]{1,0:T(8,128)(2,1)S(1)}, bf16[1024,512]{1,0:T(8,128)(2,1)}, u32[]{:S(2)}) copy-start(bf16[1024,512]{1,0:T(8,128)(2,1)} %copy-done.5) | copy-start | bytes 3145732
  344.3 22.4 %copy-start.14 = (s32[12]{0:T(128)S(1)}, s32[12]{0:T(128)}, u32[]{:S(2)}) copy-start(s32[12]{0:T(128)} %pad_add_fusion.refs_0_) | copy-start | bytes 148
  366.7 11.8 %copy-start.23 = (bf16[2,1024,1024]{2,1,0:T(8,128)(2,1)S(1)}, bf16[2,1024,1024]{2,1,0:T(8,128)(2,1)}, u32[]{:S(2)}) copy-start(bf16[2,1024,1024]{2,1,0:T(8,128)(2,1)} %get-tuple-element.72) | copy-start | bytes 12582916
  378.5 28.7 %collective-permute-start.20 = (bf16[4,128,2560]{2,1,0:T(8,128)(2,1)}, bf16[4,128,2560]{2,1,0:T(8,128)(2,1)}, u32[]{:S(2)}, u32[]{:S(2)}) collective-permute-start(bf16[4,128,2560]{2,1,0:T(8,128)(2,1)} %get-tuple-element.71.refs_5_), channel_id=1, source_target_pairs={{0,4},{4,0},{1,5},{5,1},{2,6},{6,2},{3,7},{7,3},{8,12},{12,8},{9,1... | collective-permute-start | bytes 7864328 | tf_op jit(solution)/shard_map/ppermute | solution.py:88
  381.1 31.0 %collective-permute-start.21 = (bf16[1,1024,1024]{2,1,0:T(8,128)(2,1)S(1)}, bf16[1,1024,1024]{2,1,0:T(8,128)(2,1)}, u32[]{:S(2)}, u32[]{:S(2)}) collective-permute-start(bf16[1,1024,1024]{2,1,0:T(8,128)(2,1)S(1)} %add_convert_fusion.2.refs_6_), channel_id=1, source_target_pairs={{0,16},{4,12},{8,24},{12,4},{16,0},{20,28},{24,8},{28,20},{1,17},{... | collective-permute-start | bytes 6291464 | tf_op jit(solution)/shard_map/ppermute | solution.py:111
  382.8 24.5 %copy-start.26 = (bf16[4,128,2560]{2,1,0:T(8,128)(2,1)S(1)}, bf16[4,128,2560]{2,1,0:T(8,128)(2,1)}, u32[]{:S(2)}) copy-start(bf16[4,128,2560]{2,1,0:T(8,128)(2,1)} %get-tuple-element.74) | copy-start | bytes 7864324
  407.2 4.9 copy-start.24
  409.9 6.0 %copy-start.18 = (bf16[4,128,2560]{2,1,0:T(8,128)(2,1)}, bf16[4,128,2560]{2,1,0:T(8,128)(2,1)S(1)}, u32[]{:S(2)}) copy-start(bf16[4,128,2560]{2,1,0:T(8,128)(2,1)S(1)} %fusion.1.refs_3_) | copy-start | bytes 7864324
  411.2 23.6 %collective-permute-start.23 = (bf16[2,128,2560]{2,1,0:T(8,128)(2,1)}, bf16[2,128,2560]{2,1,0:T(8,128)(2,1)}, u32[]{:S(2)}, u32[]{:S(2)}) collective-permute-start(bf16[2,128,2560]{2,1,0:T(8,128)(2,1)} %slice.275), channel_id=1, source_target_pairs={{0,8},{4,20},{8,0},{12,28},{16,24},{20,4},{24,16},{28,12},{1,9},{5... | collective-permute-start | bytes 3932168 | tf_op jit(solution)/shard_map/ppermute | solution.py:111
  417.6 54.2 %all-to-all-start.3 = ((bf16[4,256,1024]{2,1,0:T(8,128)(2,1)}), bf16[4,256,1024]{2,1,0:T(8,128)(2,1)}, u32[]{:S(2)}, u32[]{:S(2)}) async-start(bf16[4,256,1024]{2,1,0:T(8,128)(2,1)} %pad_maximum_fusion.3.refs_4_), calls=%async_computation.3 | async-start | bytes 4194304 | tf_op jit(solution)/shard_map/all_to_all | solution.py:143
  431.6 7.7 %collective-permute-start.22 = (bf16[4,128,1536]{2,1,0:T(8,128)(2,1)}, bf16[4,128,1536]{2,1,0:T(8,128)(2,1)}, u32[]{:S(2)}, u32[]{:S(2)}) collective-permute-start(bf16[4,128,1536]{2,1,0:T(8,128)(2,1)} %get-tuple-element.76), channel_id=1, source_target_pairs={{0,4},{4,0},{1,5},{5,1},{2,6},{6,2},{3,7},{7,3},{8,12},{12,8},{9,1... | collective-permute-start | bytes 4718600 | tf_op jit(solution)/shard_map/ppermute | solution.py:88
  436.5 12.6 %collective-permute-start.24 = (bf16[1,128,2560]{2,1,0:T(8,128)(2,1)S(1)}, bf16[1,128,2560]{2,1,0:T(8,128)(2,1)S(1)}, u32[]{:S(2)}, u32[]{:S(2)}) collective-permute-start(bf16[1,128,2560]{2,1,0:T(8,128)(2,1)S(1)} %slice.277), channel_id=1, source_target_pairs={{0,16},{4,12},{8,24},{12,4},{16,0},{20,28},{24,8},{28,20},{1,17},{... | collective-permute-start | bytes 1966088 | tf_op jit(solution)/shard_map/ppermute | solution.py:111
  441.1 8.2 %copy-start.2 = (bf16[3,1024,512]{2,1,0:T(8,128)(2,1)S(1)}, bf16[3,1024,512]{2,1,0:T(8,128)(2,1)}, u32[]{:S(2)}) copy-start(bf16[3,1024,512]{2,1,0:T(8,128)(2,1)} %attend_back.2.refs_5_.refs_4_) | copy-start | bytes 9437188
  441.1 8.2 %copy-start.12 = (f32[8,1024]{1,0:T(8,128)S(1)}, f32[8,1024]{1,0:T(8,128)}, u32[]{:S(2)}) copy-start(f32[8,1024]{1,0:T(8,128)} %get-tuple-element.46.refs_3_.refs_1_.refs_0_) | copy-start | bytes 98308
  442.1 33.9 %collective-permute-start.25 = (bf16[2,128,1536]{2,1,0:T(8,128)(2,1)}, bf16[2,128,1536]{2,1,0:T(8,128)(2,1)}, u32[]{:S(2)}, u32[]{:S(2)}) collective-permute-start(bf16[2,128,1536]{2,1,0:T(8,128)(2,1)} %slice.279), channel_id=1, source_target_pairs={{0,8},{4,20},{8,0},{12,28},{16,24},{20,4},{24,16},{28,12},{1,9},{5... | collective-permute-start | bytes 2359304 | tf_op jit(solution)/shard_map/ppermute | solution.py:111
  478.1 13.7 %collective-permute-start.26 = (bf16[1,128,1536]{2,1,0:T(8,128)(2,1)}, bf16[1,128,1536]{2,1,0:T(8,128)(2,1)}, u32[]{:S(2)}, u32[]{:S(2)}) collective-permute-start(bf16[1,128,1536]{2,1,0:T(8,128)(2,1)} %slice.282), channel_id=1, source_target_pairs={{0,16},{4,12},{8,24},{12,4},{16,0},{20,28},{24,8},{28,20},{1,17},{... | collective-permute-start | bytes 1179656 | tf_op jit(solution)/shard_map/ppermute | solution.py:111
  479.8 10.1 %all-to-all-start.5 = ((f32[32,1,128]{2,1,0:T(1,128)}), f32[32,1,128]{2,1,0:T(1,128)S(1)}, u32[]{:S(2)}, u32[]{:S(2)}) async-start(f32[32,1,128]{2,1,0:T(1,128)} %reshape.280), calls=%async_computation.5 | async-start | bytes 32768 | tf_op jit(solution)/shard_map/all_to_all | solution.py:965
  489.3 9.5 %collective-permute-start.27 = (f32[256,1024]{1,0:T(8,128)}, f32[256,1024]{1,0:T(8,128)}, u32[]{:S(2)}, u32[]{:S(2)}) collective-permute-start(f32[256,1024]{1,0:T(8,128)} %pad_maximum_fusion.4), channel_id=1, source_target_pairs={{0,4},{4,0},{1,5},{5,1},{2,6},{6,2},{3,7},{7,3},{8,12},{12,8},{9,1... | collective-permute-start | bytes 3145736 | tf_op jit(solution)/shard_map/ppermute | solution.py:88
  493.9 13.8 %collective-permute-start.30 = (bf16[32,4096]{1,0:T(8,128)(2,1)}, bf16[32,4096]{1,0:T(8,128)(2,1)}, u32[]{:S(2)}, u32[]{:S(2)}) collective-permute-start(bf16[32,4096]{1,0:T(8,128)(2,1)} %get-tuple-element.102), channel_id=1, source_target_pairs={{0,3},{1,0},{2,1},{3,2},{4,7},{5,4},{6,5},{7,6},{8,11},{9,8},{10,9... | collective-permute-start | bytes 786440 | tf_op jit(solution)/shard_map/ppermute | solution.py:138
  497.6 23.3 %collective-permute-start.29 = (bf16[32,4096]{1,0:T(8,128)(2,1)}, bf16[32,4096]{1,0:T(8,128)(2,1)}, u32[]{:S(2)}, u32[]{:S(2)}) collective-permute-start(bf16[32,4096]{1,0:T(8,128)(2,1)} %get-tuple-element.101), channel_id=1, source_target_pairs={{0,2},{1,3},{2,0},{3,1},{4,6},{5,7},{6,4},{7,5},{8,10},{9,11},{10,... | collective-permute-start | bytes 786440 | tf_op jit(solution)/shard_map/ppermute | solution.py:138
  497.6 23.3 %collective-permute-start.28 = (bf16[32,4096]{1,0:T(8,128)(2,1)}, bf16[32,4096]{1,0:T(8,128)(2,1)}, u32[]{:S(2)}, u32[]{:S(2)}) collective-permute-start(bf16[32,4096]{1,0:T(8,128)(2,1)} %get-tuple-element.100), channel_id=1, source_target_pairs={{0,1},{1,2},{2,3},{3,0},{4,5},{5,6},{6,7},{7,4},{8,9},{9,10},{10,1... | collective-permute-start | bytes 786440 | tf_op jit(solution)/shard_map/ppermute | solution.py:138
  505.8 19.1 %copy-start.31 = (f32[32,2,4096]{2,1,0:T(2,128)}, f32[32,2,4096]{2,1,0:T(2,128)S(1)}, u32[]{:S(2)}) copy-start(f32[32,2,4096]{2,1,0:T(2,128)S(1)} %reshape.279) | copy-start | bytes 3145732
  (12 other events, 19.5 us)
